TPU v7x, 32 devices: a whole 2x2x4 slice. The times are simulated.
32 devices in a mesh: dp: 16 (over z, x, core), mp: 2 (over y).
Axes of the slice: x: 2, y: 2, z: 4, core: 2. Of those that a mesh axis runs over, the one named last changes fastest.
Arguments:
- tokens: bfloat16 [8192, 2048], P(('dp', 'mp')), may hold values from -6 to 6
- norm_gain: bfloat16 [2048], P('dp'), may hold values from 0.5 to 1.5
- norm_shift: bfloat16 [2048], P('dp'), may hold values from -1.25 to 1.25
- in_weight: bfloat16 [3, 2048, 2048], P(None, 'dp', 'mp'), may hold values from -0.125 to 0.125
- in_bias: bfloat16 [3, 2048], P(None, ('mp', 'dp')), may hold values from -1.25 to 1.25
- out_weight: bfloat16 [2048, 2048], P('dp', 'mp'), may hold values from -0.375 to 0.375
- out_bias: bfloat16 [2048], P('dp'), may hold values from -1.25 to 1.25
- up_weight: bfloat16 [2048, 8192], P('dp', 'mp'), may hold values from -0.125 to 0.125
- up_bias: bfloat16 [8192], P(('mp', 'dp')), may hold values from -1.25 to 1.25
- down_weight: bfloat16 [2048, 8192], P('dp', 'mp'), may hold values from -0.0625 to 0.0625
- down_bias: bfloat16 [2048], P('dp'), may hold values from -1.25 to 1.25
- cotangent: bfloat16 [8192, 2048], P(('dp', 'mp')), may hold values from -6 to 6
Outputs:
- result: bfloat16 [8192, 2048], P(('dp', 'mp'))
- grad_tokens: float32 [8192, 2048], P(('dp', 'mp'))
- grad_gain: float32 [2048], P('dp')
- grad_shift: float32 [2048], P('dp')
- grad_in_weight: float32 [3, 2048, 2048], P(None, 'dp', 'mp')
- grad_in_bias: float32 [3, 2048], P(None, ('mp', 'dp'))
- grad_out_weight: float32 [2048, 2048], P('dp', 'mp')
- grad_out_bias: float32 [2048], P('dp')
- grad_up_weight: float32 [2048, 8192], P('dp', 'mp')
- grad_up_bias: float32 [8192], P(('mp', 'dp'))
- grad_down_weight: float32 [2048, 8192], P('dp', 'mp')
- grad_down_bias: float32 [2048], P('dp')
All inputs are finite; a program needn't handle non-finite values.
Results may differ from a plain program's by a relative error of at most 0.0095.
Values may be sent and summed in bfloat16 or wider, within the bound.
A program may use at most 384 MiB of HBM per device.

v0:
```python
import math

import jax
import jax.numpy as jnp
from jax import lax
from jax.sharding import PartitionSpec as P

HEAD = 64
ROT = 32


norm_eps = 1e-05


def normalize(rows):
    middle = jnp.mean(rows, axis=-1, keepdims=True)
    centered = rows - middle
    spread = jnp.mean(centered * centered, axis=-1, keepdims=True)
    inv_spread = lax.rsqrt(spread + norm_eps)
    return (centered * inv_spread, inv_spread)


def rotary_tables(length):
    half_rot = ROT // 2
    position = jnp.arange(length, dtype=jnp.float32)
    freqs = jnp.exp(jnp.arange(half_rot, dtype=jnp.float32) * (-math.log(10000.0) / half_rot))
    angles = position[:, None] * freqs[None, :]
    angles = jnp.concatenate([angles, angles], axis=1)
    return (jnp.cos(angles), jnp.sin(angles))


def rotate(vectors, cosine, sine):
    half_rot = ROT // 2
    turned = vectors[..., :ROT]
    swapped = jnp.concatenate([-turned[..., half_rot:], turned[..., :half_rot]], axis=-1)
    turned = turned * cosine[:, None, :] + swapped * sine[:, None, :]
    return jnp.concatenate([turned, vectors[..., ROT:]], axis=-1)


def attend(queries, keys):
    length = queries.shape[0]
    scores = jnp.einsum("qhe,khe->hqk", queries, keys, preferred_element_type=jnp.float32) * (
        1.0 / math.sqrt(HEAD)
    )
    row_ids = lax.broadcasted_iota(jnp.int32, (length, length), 0)
    col_ids = lax.broadcasted_iota(jnp.int32, (length, length), 1)
    scores = jnp.where((col_ids <= row_ids)[None], scores, -1e30)
    top_score = jnp.max(scores, axis=-1, keepdims=True)
    powers = jnp.exp(scores - top_score)
    return powers / jnp.sum(powers, axis=-1, keepdims=True)


def smooth_gate(inputs):
    return jax.nn.gelu(inputs, approximate=True)


def per_device(
    tokens,
    norm_gain,
    norm_shift,
    in_weight,
    in_bias,
    out_weight,
    out_bias,
    up_weight,
    up_bias,
    down_weight,
    down_bias,
    cotangent,
):
    gathered = (
        lax.all_gather(norm_gain, "dp", axis=0, tiled=True),
        lax.all_gather(norm_shift, "dp", axis=0, tiled=True),
        lax.all_gather(in_weight, "dp", axis=1, tiled=True),
        lax.all_gather(in_bias, "dp", axis=1, tiled=True),
        lax.all_gather(out_weight, "dp", axis=0, tiled=True),
        lax.all_gather(out_bias, "dp", axis=0, tiled=True),
        lax.all_gather(up_weight, "dp", axis=0, tiled=True),
        lax.all_gather(up_bias, "dp", axis=0, tiled=True),
        lax.all_gather(down_weight, "dp", axis=0, tiled=True),
        lax.all_gather(down_bias, "dp", axis=0, tiled=True),
    )
    (
        full_gain,
        full_shift,
        full_in,
        full_in_bias,
        full_out,
        full_out_bias,
        full_up,
        full_up_bias,
        full_down,
        full_down_bias,
    ) = gathered
    sequence = lax.all_gather(tokens, "mp", axis=0, tiled=True)
    length = sequence.shape[0]
    heads_here = full_in.shape[2] // HEAD
    unit_rows = normalize(sequence.astype(jnp.float32))[0]
    normed = (unit_rows * full_gain.astype(jnp.float32) + full_shift.astype(jnp.float32)).astype(
        jnp.bfloat16
    )
    projected = (
        jnp.einsum("sd,kde->kse", normed, full_in, preferred_element_type=jnp.float32)
        + full_in_bias.astype(jnp.float32)[:, None, :]
    )
    cosine, sine = rotary_tables(length)
    query_pre = projected[0].reshape(length, heads_here, HEAD)
    key_pre = projected[1].reshape(length, heads_here, HEAD)
    queries = rotate(query_pre, cosine, sine).astype(jnp.bfloat16)
    keys = rotate(key_pre, cosine, sine).astype(jnp.bfloat16)
    values = projected[2].reshape(length, heads_here, HEAD).astype(jnp.bfloat16)
    weights = attend(queries, keys).astype(jnp.bfloat16)
    mixed = jnp.einsum("hqk,khe->qhe", weights, values, preferred_element_type=jnp.float32)
    mixed = mixed.reshape(length, heads_here * HEAD).astype(jnp.bfloat16)
    attended = jnp.einsum("se,de->sd", mixed, full_out, preferred_element_type=jnp.float32)
    preact = jnp.dot(normed, full_up, preferred_element_type=jnp.float32) + full_up_bias.astype(
        jnp.float32
    )
    activated = smooth_gate(preact).astype(jnp.bfloat16)
    branches = attended + jnp.einsum(
        "sf,df->sd", activated, full_down, preferred_element_type=jnp.float32
    )
    summed = lax.psum_scatter(
        branches.astype(jnp.bfloat16), "mp", scatter_dimension=0, tiled=True
    ).astype(jnp.float32)
    outcome = (
        tokens.astype(jnp.float32)
        + summed
        + full_out_bias.astype(jnp.float32)
        + full_down_bias.astype(jnp.float32)
    ).astype(jnp.bfloat16)
    back_gain, back_in, back_out, back_up, back_down = (
        lax.all_gather(norm_gain, "dp", axis=0, tiled=True),
        lax.all_gather(in_weight, "dp", axis=1, tiled=True),
        lax.all_gather(out_weight, "dp", axis=0, tiled=True),
        lax.all_gather(up_weight, "dp", axis=0, tiled=True),
        lax.all_gather(down_weight, "dp", axis=0, tiled=True),
    )
    grad_rows = lax.all_gather(cotangent, "mp", axis=0, tiled=True)
    grad_bias = jnp.sum(grad_rows.astype(jnp.float32), axis=0)
    grad_down = jnp.einsum("sd,sf->df", grad_rows, activated, preferred_element_type=jnp.float32)
    grad_act = jnp.dot(grad_rows, back_down, preferred_element_type=jnp.float32)
    gate_pull = jax.vjp(smooth_gate, preact)[1]
    grad_pre = gate_pull(grad_act)[0].astype(jnp.bfloat16)
    grad_up = jnp.einsum("sd,sf->df", normed, grad_pre, preferred_element_type=jnp.float32)
    grad_up_bias = jnp.sum(grad_pre.astype(jnp.float32), axis=0)
    grad_normed = jnp.einsum("sf,df->sd", grad_pre, back_up, preferred_element_type=jnp.float32)
    grad_out = jnp.einsum("sd,se->de", grad_rows, mixed, preferred_element_type=jnp.float32)
    grad_mixed = jnp.dot(grad_rows, back_out, preferred_element_type=jnp.float32).astype(
        jnp.bfloat16
    )
    grad_mixed = grad_mixed.reshape(length, heads_here, HEAD)
    again_probs = attend(queries, keys)
    again_low = again_probs.astype(jnp.bfloat16)
    grad_probs = jnp.einsum("qhe,khe->hqk", grad_mixed, values, preferred_element_type=jnp.float32)
    row_total = jnp.sum(again_probs * grad_probs, axis=-1, keepdims=True)
    grad_scores = (again_probs * (grad_probs - row_total)).astype(jnp.bfloat16)
    grad_values = jnp.einsum(
        "hqk,qhe->khe", again_low, grad_mixed, preferred_element_type=jnp.float32
    ).astype(jnp.bfloat16)
    score_scale = 1.0 / math.sqrt(HEAD)
    grad_queries = (
        jnp.einsum("hqk,khe->qhe", grad_scores, keys, preferred_element_type=jnp.float32)
        * score_scale
    ).astype(jnp.bfloat16)
    grad_keys = (
        jnp.einsum("hqk,qhe->khe", grad_scores, queries, preferred_element_type=jnp.float32)
        * score_scale
    ).astype(jnp.bfloat16)

    def turn(vectors):
        return rotate(vectors, cosine, sine)

    turn_pull = jax.vjp(turn, query_pre)[1]
    query_back = turn_pull(grad_queries.astype(jnp.float32))[0].astype(jnp.bfloat16)
    key_back = turn_pull(grad_keys.astype(jnp.float32))[0].astype(jnp.bfloat16)
    grad_proj = jnp.stack(
        [
            query_back.reshape(length, -1),
            key_back.reshape(length, -1),
            grad_values.reshape(length, -1),
        ]
    )
    grad_in = jnp.einsum("sd,kse->kde", normed, grad_proj, preferred_element_type=jnp.float32)
    grad_in_bias = jnp.sum(grad_proj.astype(jnp.float32), axis=1)
    grad_normed = grad_normed + jnp.einsum(
        "kse,kde->sd", grad_proj, back_in, preferred_element_type=jnp.float32
    )
    grad_own = lax.psum_scatter(
        grad_normed.astype(jnp.bfloat16), "mp", scatter_dimension=0, tiled=True
    ).astype(jnp.float32)
    own_unit, own_inv = normalize(tokens.astype(jnp.float32))
    gain_part = jnp.sum(grad_own * own_unit, axis=0)
    shift_part = jnp.sum(grad_own, axis=0)
    gain_total, shift_total = lax.psum((gain_part, shift_part), "mp")
    scaled = grad_own * back_gain.astype(jnp.float32)
    centered_grad = (
        scaled
        - jnp.mean(scaled, axis=-1, keepdims=True)
        - own_unit * jnp.mean(scaled * own_unit, axis=-1, keepdims=True)
    )
    grad_input = cotangent.astype(jnp.float32) + own_inv * centered_grad
    owned = (
        lax.psum_scatter(gain_total, "dp", scatter_dimension=0, tiled=True),
        lax.psum_scatter(shift_total, "dp", scatter_dimension=0, tiled=True),
        lax.psum_scatter(grad_in, "dp", scatter_dimension=1, tiled=True),
        lax.psum_scatter(grad_in_bias, "dp", scatter_dimension=1, tiled=True),
        lax.psum_scatter(grad_out, "dp", scatter_dimension=0, tiled=True),
        lax.psum_scatter(grad_bias, "dp", scatter_dimension=0, tiled=True),
        lax.psum_scatter(grad_up, "dp", scatter_dimension=0, tiled=True),
        lax.psum_scatter(grad_up_bias, "dp", scatter_dimension=0, tiled=True),
        lax.psum_scatter(grad_down, "dp", scatter_dimension=0, tiled=True),
    )
    return (
        outcome,
        grad_input,
        owned[0],
        owned[1],
        owned[2],
        owned[3],
        owned[4],
        owned[5],
        owned[6],
        owned[7],
        owned[8],
        owned[5],
    )


def solution(mesh):
    return jax.shard_map(
        per_device,
        mesh=mesh,
        in_specs=(
            P(("dp", "mp"), None),
            P("dp"),
            P("dp"),
            P(None, "dp", "mp"),
            P(None, ("mp", "dp")),
            P("dp", "mp"),
            P("dp"),
            P("dp", "mp"),
            P(("mp", "dp")),
            P("dp", "mp"),
            P("dp"),
            P(("dp", "mp"), None),
        ),
        out_specs=(
            P(("dp", "mp"), None),
            P(("dp", "mp"), None),
            P("dp"),
            P("dp"),
            P(None, "dp", "mp"),
            P(None, ("mp", "dp")),
            P("dp", "mp"),
            P("dp"),
            P("dp", "mp"),
            P(("mp", "dp")),
            P("dp", "mp"),
            P("dp"),
        ),
        check_vma=False,
    )
```

profile of v0, /device:TPU:0, one launch (start us, length us, event | category | flops | bytes accessed | tf_op | source)
XLA Modules:
  0.0 1654.5 jit_solution(9396203273978793173)
XLA Ops:
  7.3 0.7 all-gather.13.cloned.1.call-update
  8.0 0.7 all-gather.23.cloned.1.call-update
  8.7 0.7 all-gather.17.cloned.1.call-update
  11.2 23.0 %all-gather = bf16[16,1,128]{2,1,0:T(2,128)(2,1)S(1)} all-gather(bf16[1,1,128]{2,1,0:T(2,128)(2,1)S(1)} %bitcast.107), channel_id=1, replica_groups=mesh['dp'=16,'mp'=2] {'dp'}, dimensions={0}, use_global_device_ids=true | all-gather | bytes 4352 | tf_op jit(solution)/shard_map/all_gather | solution.py:72
  34.2 17.3 %all-gather.1 = bf16[16,1,128]{2,1,0:T(2,128)(2,1)S(1)} all-gather(bf16[1,1,128]{2,1,0:T(2,128)(2,1)S(1)} %bitcast.108), channel_id=1, replica_groups=mesh['dp'=16,'mp'=2] {'dp'}, dimensions={0}, use_global_device_ids=true | all-gather | bytes 4352 | tf_op jit(solution)/shard_map/all_gather | solution.py:73
  51.5 18.8 %all-gather.2 = bf16[16,64,3]{1,2,0:T(4,128)(2,1)S(1)} all-gather(bf16[1,64,3]{1,2,0:T(4,128)(2,1)S(1)} %bitcast.106), channel_id=1, replica_groups=mesh['dp'=16,'mp'=2] {'dp'}, dimensions={0}, use_global_device_ids=true | all-gather | bytes 6528 | tf_op jit(solution)/shard_map/all_gather | solution.py:75
  70.5 17.4 %all-gather.3 = bf16[16,1,256]{2,1,0:T(2,128)(2,1)S(1)} all-gather(bf16[1,1,256]{2,1,0:T(2,128)(2,1)S(1)} %reshape.127), channel_id=1, replica_groups=mesh['dp'=16,'mp'=2] {'dp'}, dimensions={0}, use_global_device_ids=true | all-gather | bytes 8704 | tf_op jit(solution)/shard_map/all_gather | solution.py:79
  88.6 0.8 fusion.54
  89.4 0.8 iota_compare_fusion
  90.1 2.0 convert_reduce_fusion.2
  92.2 2.3 fusion.14
  94.5 38.5 %all-gather.17.cloned.1.call-done = bf16[2048,1024]{1,0:T(8,128)(2,1)} async-done(((bf16[128,1024]{1,0:T(8,128)(2,1)}), bf16[2048,1024]{1,0:T(8,128)(2,1)}) %all-gather.17.cloned.1.call-update) | async-done | bytes 4194320 | tf_op jit(solution)/shard_map/all_gather | solution.py:76
  133.1 5.2 convolution_convert_fusion
  138.2 1.5 copy.84
  139.8 94.7 %all-gather.15.cloned.1.call-done = bf16[3,2048,1024]{2,1,0:T(8,128)(2,1)} async-done(((bf16[3,128,1024]{2,1,0:T(8,128)(2,1)}), bf16[3,2048,1024]{2,1,0:T(8,128)(2,1)}) %all-gather.15.cloned.1.call-update) | async-done | bytes 12582928 | tf_op jit(solution)/shard_map/all_gather | solution.py:74
  234.4 9.4 add_bitcast_fusion
  244.0 2.3 fusion.71
  246.3 1.9 copy.81
  248.2 2.9 copy.82
  251.1 2.1 slice.78
  253.2 0.9 slice.79
  254.1 1.3 copy.80
  255.6 1.5 slice_negate_fusion.2
  257.3 2.4 fusion.51
  259.7 11.2 fusion.76
  270.9 16.7 %multiply_reduce_fusion = (f32[16,512]{1,0:T(8,128)}, f32[16,512,512]{1,2,0:T(8,128)}) fusion(f32[16,512,512]{1,2,0:T(8,128)} %get-tuple-element.95, f32[16,512]{1,0:T(8,128)} %get-tuple-element.94, bf16[512,16,64]{0,2,1:T(8,128)(2,1)} %bitcast.84, bf16[512,16,64]{0,2,1:T(8,128)(2,1)} %bitcast.86), kind=kOutput, calls=%fused_computation.3 | convolution fusion | flops 549445632 | bytes 35717120 | tf_op jit(solution)/shard_map/qhe,khe->hqk/dot_general | solution.py:155
  288.2 8.5 multiply_convert_fusion
  296.7 3.9 convert_bitcast_fusion
  300.6 1.4 convert_bitcast_fusion.1
  302.1 1.8 fusion.72
  305.3 1.4 add_convert_fusion.1
  307.3 10.3 fusion.45
  317.6 1.5 copy.90
  319.1 0.7 convert_reduce_fusion.1
  319.8 1.0 copy.100
  320.9 8.8 fusion.42
  329.8 12.2 fusion.63
  342.0 19.5 %all-gather.19.cloned.1.call-done = bf16[2048,4096]{1,0:T(8,128)(2,1)} async-done(((bf16[128,4096]{1,0:T(8,128)(2,1)}), bf16[2048,4096]{1,0:T(8,128)(2,1)}) %all-gather.19.cloned.1.call-update) | async-done | bytes 16777232 | tf_op jit(solution)/shard_map/all_gather | solution.py:78
  361.5 14.4 fusion.67
  376.0 112.7 %all-gather.21.cloned.1.call-done = bf16[2048,4096]{1,0:T(8,128)(2,1)} async-done(((bf16[128,4096]{1,0:T(8,128)(2,1)}), bf16[2048,4096]{1,0:T(8,128)(2,1)}) %all-gather.21.cloned.1.call-update) | async-done | bytes 16777232 | tf_op jit(solution)/shard_map/all_gather | solution.py:80
  488.6 19.0 %convert_reduce_fusion = (f32[4096]{0:T(1024)S(1)}, bf16[512,4096]{1,0:T(8,128)(2,1)S(1)}) fusion(f32[512,4096]{1,0:T(8,128)} %fusion.67, f32[4096]{0:T(1024)S(1)} %bitcast.98, bf16[512,2048]{1,0:T(8,128)(2,1)} %all-gather.23.cloned.1.call-done, bf16[2048,4096]{1,0:T(8,128)(2,1)} %all-gather.21.cloned.1.call-done), kind=kOutput, calls=%fused_computation.17 | convolution fusion | flops 8638164992 | bytes 31490048 | tf_op jit(solution)/shard_map/dot_general | solution.py:142
  507.7 2.0 copy-done.26
  509.7 14.2 fusion.18
  523.9 6.8 fusion.77
  530.8 18.3 %add_convert_fusion = bf16[512,2048]{1,0:T(8,128)(2,1)} fusion(f32[512,2048]{1,0:T(8,128)} %fusion.77, bf16[2048,4096]{1,0:T(8,128)(2,1)} %all-gather.21.cloned.1.call-done, f32[512,4096]{1,0:T(8,128)} %fusion.67, f32[4096]{0:T(1024)S(1)} %bitcast.99), kind=kOutput, calls=%fused_computation.37 | convolution fusion | flops 8613003264 | bytes 31473664 | tf_op jit(solution)/shard_map/sf,df->sd/dot_general | solution.py:120
  549.3 7.7 convolution_bitcast_fusion.2
  557.1 13.6 convolution_bitcast_fusion.1
  570.8 19.7 %convolution_bitcast_fusion = f32[2048,4096]{0,1:T(8,128)} fusion(bf16[512,2048]{1,0:T(8,128)(2,1)} %all-gather.23.cloned.1.call-done, f32[512,4096]{1,0:T(8,128)} %fusion.67, f32[4096]{0:T(1024)S(1)} %bitcast.100), kind=kOutput, calls=%fused_computation.1 | convolution fusion | flops 8610906112 | bytes 44056576 | tf_op jit(solution)/shard_map/sd,sf->df/dot_general | solution.py:141
  590.8 17.8 %fusion.65 = f32[2048,4096]{1,0:T(8,128)} fusion(bf16[512,4096]{1,0:T(8,128)(2,1)} %copy-done.26, bf16[512,2048]{1,0:T(8,128)(2,1)S(1)} %copy-done.3, f32[2048]{0:T(1024)S(1)} %bitcast.105, f32[2048]{0:T(1024)S(1)} %bitcast.92, f32[512]{0:T(512)S(1)} %copy-done.17, f32[512]{0:T(512)S(1)} %copy-done.15), kind=kOutput, calls=%fused_computation.118 | convolution fusion | flops 8596226048 | bytes 39866368 | tf_op jit(solution)/shard_map/sd,sf->df/dot_general | solution.py:145
  611.1 19.0 %all-gather.4 = bf16[16,1,128]{2,1,0:T(2,128)(2,1)S(1)} all-gather(bf16[1,1,128]{2,1,0:T(2,128)(2,1)S(1)} %bitcast.109), channel_id=1, replica_groups=mesh['dp'=16,'mp'=2] {'dp'}, dimensions={0}, use_global_device_ids=true | all-gather | bytes 4352 | tf_op jit(solution)/shard_map/all_gather | solution.py:77
  630.2 17.3 %all-gather.5 = bf16[16,1,128]{2,1,0:T(2,128)(2,1)S(1)} all-gather(bf16[1,1,128]{2,1,0:T(2,128)(2,1)S(1)} %bitcast.110), channel_id=1, replica_groups=mesh['dp'=16,'mp'=2] {'dp'}, dimensions={0}, use_global_device_ids=true | all-gather | bytes 4352 | tf_op jit(solution)/shard_map/all_gather | solution.py:81
  648.1 2.0 convert_reduce_fusion.3
  650.1 1.4 copy.101
  651.5 2.3 fusion.37
  653.9 62.4 %all-reduce.12 = (f32[2048]{0:T(1024)S(1)}, f32[2048]{0:T(1024)S(1)}, f32[2048]{0:T(1024)S(1)}, f32[4096]{0:T(1024)S(1)}) all-reduce(f32[2048]{0:T(1024)S(1)} %get-tuple-element.60, f32[2048]{0:T(1024)S(1)} %get-tuple-element.63, f32[2048]{0:T(1024)S(1)} %convert_reduce_fusion.3, ...), channel_id=4, replica_groups=mesh['dp'=16,'mp'=2] {'dp'}, use_global_device_ids=true, to_apply=%region_13.14.clone | all-reduce | flops 10240 | bytes 81920
  716.5 0.6 dynamic-slice.7
  717.2 5.4 all-reduce.13
  722.6 4.4 fusion.31
  727.0 2.0 copy.93
  729.1 244.4 %reduce-scatter.14.cloned.1.call-done = f32[3,128,1024]{1,2,0:T(8,128)} async-done(((f32[3,2048,1024]{1,2,0:T(8,128)}), f32[3,128,1024]{1,2,0:T(8,128)}) %reduce-scatter.14.cloned.1.call-update) | async-done | bytes 1572880 | tf_op jit(solution)/shard_map/reduce_scatter | solution.py:206
  973.5 3.0 copy.92
  976.5 333.3 %reduce-scatter.20.cloned.1.call-done = f32[128,4096]{0,1:T(8,128)} async-done(((f32[2048,4096]{0,1:T(8,128)}), f32[128,4096]{0,1:T(8,128)}) %reduce-scatter.20.cloned.1.call-update) | async-done | bytes 2097168 | tf_op jit(solution)/shard_map/reduce_scatter | solution.py:212
  1309.8 2.9 copy.94
  1312.7 334.3 %reduce-scatter.18.cloned.1.call-done = f32[128,4096]{1,0:T(8,128)} async-done(((f32[2048,4096]{1,0:T(8,128)}), f32[128,4096]{1,0:T(8,128)}) %reduce-scatter.18.cloned.1.call-update) | async-done | bytes 2097168 | tf_op jit(solution)/shard_map/reduce_scatter | solution.py:210
  (122 shorter events, 9.4 us)
Async XLA Ops:
  7.2 4.0 copy-start.19
  7.2 27.0 %copy-start.20 = (bf16[128]{0:T(256)(128)(2,1)S(1)}, bf16[128]{0:T(256)(128)(2,1)}, u32[]{:S(2)}) copy-start(bf16[128]{0:T(256)(128)(2,1)} %param.14) | copy-start | bytes 772
  7.2 44.3 %copy-start.18 = (bf16[3,64]{1,0:T(4,128)(2,1)S(1)}, bf16[3,64]{1,0:T(4,128)(2,1)}, u32[]{:S(2)}) copy-start(bf16[3,64]{1,0:T(4,128)(2,1)} %param.16) | copy-start | bytes 1156
  7.2 63.2 %copy-start.23 = (bf16[256]{0:T(256)(128)(2,1)S(1)}, bf16[256]{0:T(256)(128)(2,1)}, u32[]{:S(2)}) copy-start(bf16[256]{0:T(256)(128)(2,1)} %param.20) | copy-start | bytes 1540
  7.2 82.9 %all-gather.13.cloned.1.call-start = ((), (), s32[]{:S(2)}) async-start(), calls=%async_computation.7 | async-start | bytes 3145728 | tf_op jit(solution)/shard_map/all_gather | solution.py:95
  8.0 86.6 %all-gather.23.cloned.1.call-start = ((), (), s32[]{:S(2)}) async-start(), calls=%async_computation.13 | async-start | bytes 3145728 | tf_op jit(solution)/shard_map/all_gather | solution.py:139
  8.7 124.4 %all-gather.17.cloned.1.call-start = ((), (), s32[]{:S(2)}) async-start(), calls=%async_computation.9 | async-start | bytes 4456448 | tf_op jit(solution)/shard_map/all_gather | solution.py:76
  9.4 225.0 %all-gather.15.cloned.1.call-start = ((), (), s32[]{:S(2)}) async-start(), calls=%async_computation.8 | async-start | bytes 13369344 | tf_op jit(solution)/shard_map/all_gather | solution.py:74
  10.0 351.5 %all-gather.19.cloned.1.call-start = ((), (), s32[]{:S(2)}) async-start(), calls=%async_computation.10 | async-start | bytes 17825792 | tf_op jit(solution)/shard_map/all_gather | solution.py:78
  10.6 478.0 %all-gather.21.cloned.1.call-start = ((), (), s32[]{:S(2)}) async-start(), calls=%async_computation.11 | async-start | bytes 17825792 | tf_op jit(solution)/shard_map/all_gather | solution.py:80
  11.2 638.9 %reduce-scatter.22.cloned.1.call-start = ((), (), s32[]{:S(2)}) async-start(), calls=%async_computation.19 | async-start | bytes 557056
  92.2 142.2 %copy-start.14 = (f32[512]{0:T(512)}, f32[512]{0:T(512)S(1)}, u32[]{:S(2)}) copy-start(f32[512]{0:T(512)S(1)} %broadcast_multiply_fusion) | copy-start | bytes 6148
  94.5 139.9 %copy-start.16 = (f32[512]{0:T(512)}, f32[512]{0:T(512)S(1)}, u32[]{:S(2)}) copy-start(f32[512]{0:T(512)S(1)} %add_rsqrt_fusion) | copy-start | bytes 6148
  94.5 139.9 %copy-start.2 = (bf16[512,2048]{1,0:T(8,128)(2,1)S(1)}, bf16[512,2048]{1,0:T(8,128)(2,1)}, u32[]{:S(2)}) copy-start(bf16[512,2048]{1,0:T(8,128)(2,1)} %all-gather.13.cloned.1.call-done) | copy-start | bytes 6291460
  255.4 1.9 copy-start.1
  255.5 4.2 copy-start.7
  255.5 4.2 copy-start.8
  255.6 4.2 copy-start.11
  270.9 16.7 %slice-start = ((s8[16777216]{0:T(1024)(128)(4,1)}), s8[4194304]{0:T(1024)(128)(4,1)S(1)}, s32[]{:S(2)}) async-start(s8[16777216]{0:T(1024)(128)(4,1)} %bitcast.73), calls=%async_computation.20 | async-start | bytes 8388608
  270.9 16.7 %slice-start.1 = ((s8[16777216]{0:T(1024)(128)(4,1)}), s8[4194304]{0:T(1024)(128)(4,1)S(1)}, s32[]{:S(2)}) async-start(s8[16777216]{0:T(1024)(128)(4,1)} %bitcast.73), calls=%async_computation.21 | async-start | bytes 8388608
  270.9 16.7 %slice-start.2 = ((s8[16777216]{0:T(1024)(128)(4,1)}), s8[4194304]{0:T(1024)(128)(4,1)S(1)}, s32[]{:S(2)}) async-start(s8[16777216]{0:T(1024)(128)(4,1)} %bitcast.73), calls=%async_computation.22 | async-start | bytes 8388608
  270.9 17.3 %slice-start.3 = ((s8[16777216]{0:T(1024)(128)(4,1)}), s8[4194304]{0:T(1024)(128)(4,1)S(1)}, s32[]{:S(2)}) async-start(s8[16777216]{0:T(1024)(128)(4,1)} %bitcast.73), calls=%async_computation.23 | async-start | bytes 8388608
  296.7 3.9 copy-start.9
  300.6 1.4 copy-start.10
  304.8 2.5 copy-start.12
  307.3 11.8 copy-start.4
  319.1 10.6 copy-start.5
  329.7 31.8 %copy-start.3 = (bf16[512,2048]{1,0:T(8,128)(2,1)S(1)}, bf16[512,2048]{1,0:T(8,128)(2,1)}, u32[]{:S(2)}) copy-start(bf16[512,2048]{1,0:T(8,128)(2,1)} %all-gather.13.cloned.1.call-done) | copy-start | bytes 6291460
  329.7 31.8 %copy-start.15 = (f32[512]{0:T(512)S(1)}, f32[512]{0:T(512)}, u32[]{:S(2)}) copy-start(f32[512]{0:T(512)} %copy-done.14) | copy-start | bytes 6148
  329.7 31.8 %copy-start.17 = (f32[512]{0:T(512)S(1)}, f32[512]{0:T(512)}, u32[]{:S(2)}) copy-start(f32[512]{0:T(512)} %copy-done.16) | copy-start | bytes 6148
  329.7 321.8 %reduce-scatter.12.cloned.1.call-start = ((), (), s32[]{:S(2)}) async-start(), calls=%async_computation.14 | async-start | bytes 3145728 | tf_op jit(solution)/shard_map/reduce_scatter | solution.py:189
  342.0 146.7 %copy-start.13 = (f32[16,1,256]{2,1,0:T(1,128)S(1)}, f32[16,1,256]{2,1,0:T(1,128)}, u32[]{:S(2)}) copy-start(f32[16,1,256]{2,1,0:T(1,128)} %convert_element_type.161) | copy-start | bytes 49156
  507.7 2.0 copy-start.26
  523.9 198.7 %reduce-scatter.10.cloned.1.call-start = ((), (), s32[]{:S(2)}) async-start(), calls=%async_computation.12 | async-start | bytes 3145728 | tf_op jit(solution)/shard_map/reduce_scatter | solution.py:123
  549.0 178.0 %reduce-scatter.16.cloned.1.call-start = ((), (), s32[]{:S(2)}) async-start(), calls=%async_computation.16 | async-start | bytes 8912896 | tf_op jit(solution)/shard_map/reduce_scatter | solution.py:208
  557.1 416.4 %reduce-scatter.14.cloned.1.call-start = ((), (), s32[]{:S(2)}) async-start(), calls=%async_computation.15 | async-start | bytes 26738688 | tf_op jit(solution)/shard_map/reduce_scatter | solution.py:206
  570.7 739.1 %reduce-scatter.20.cloned.1.call-start = ((), (), s32[]{:S(2)}) async-start(), calls=%async_computation.18 | async-start | bytes 35651584 | tf_op jit(solution)/shard_map/reduce_scatter | solution.py:212
  590.5 1056.5 %reduce-scatter.18.cloned.1.call-start = ((), (), s32[]{:S(2)}) async-start(), calls=%async_computation.17 | async-start | bytes 35651584 | tf_op jit(solution)/shard_map/reduce_scatter | solution.py:210
  608.6 0.7 copy-start.24
  608.6 2.5 copy-start.21
  608.6 21.6 %copy-start.22 = (bf16[128]{0:T(256)(128)(2,1)S(1)}, bf16[128]{0:T(256)(128)(2,1)}, u32[]{:S(2)}) copy-start(bf16[128]{0:T(256)(128)(2,1)} %param.22) | copy-start | bytes 772
  608.6 38.9 %copy-start = (bf16[256,2048]{1,0:T(8,128)(2,1)S(1)}, bf16[256,2048]{1,0:T(8,128)(2,1)}, u32[]{:S(2)}) copy-start(bf16[256,2048]{1,0:T(8,128)(2,1)} %param.12) | copy-start | bytes 3145732
  608.6 114.0 %copy-start.6 = (bf16[256,2048]{1,0:T(8,128)(2,1)S(1)}, bf16[256,2048]{1,0:T(8,128)(2,1)}, u32[]{:S(2)}) copy-start(bf16[256,2048]{1,0:T(8,128)(2,1)} %param.23) | copy-start | bytes 3145732
  716.5 930.5 %copy-start.25 = (f32[128]{0:T(128)}, f32[128]{0:T(128)S(1)}, u32[]{:S(2)}) copy-start(f32[128]{0:T(128)S(1)} %dynamic-slice.5) | copy-start | bytes 1540
Sparse Core Ops, SparseCore 0:
  9.6 35.8 all-gather.12
  47.0 33.1 all-gather.22
  82.3 50.7 all-gather.16
  135.1 99.2 all-gather.14
  236.4 125.0 all-gather.18
  363.5 125.0 all-gather.20
  492.8 53.9 reduce-scatter.21
  549.6 30.8 reduce-scatter.11
  583.3 31.8 reduce-scatter.9
  619.7 105.3 reduce-scatter.15
  729.7 243.7 reduce-scatter.13
  978.2 331.5 reduce-scatter.19
  1315.2 331.7 reduce-scatter.17
where the time goes:
time: 1660 us; the launch traced here: 1650 us
  waiting for transfers between devices  1180 us (71%)
  matrix products  211 us (13%)
  blocking collectives  181 us (11%)
  other arithmetic  33.2 us (2%)
  local copies, waits for them, and re-layouts  31.6 us (2%)
    reduce_scatter x1, waiting for transfers between devices, per_device(): lax.psum_scatter(grad_up, 'dp', scatter_dimension=0, tiled=True)  334 us
    reduce_scatter x1, waiting for transfers between devices, per_device(): lax.psum_scatter(grad_down, 'dp', scatter_dimension=0, tiled=True)  333 us
    reduce_scatter x1, waiting for transfers between devices, per_device(): lax.psum_scatter(grad_in, 'dp', scatter_dimension=1, tiled=True)  244 us
    all_gather x1, waiting for transfers between devices, per_device(): lax.all_gather(down_weight, 'dp', axis=0, tiled=True)  113 us
    all_gather x1, waiting for transfers between devices, per_device(): lax.all_gather(in_weight, 'dp', axis=1, tiled=True)  94.7 us
    unnamed x1, blocking collectives  62.4 us
    all_gather x1, waiting for transfers between devices, per_device(): lax.all_gather(out_weight, 'dp', axis=0, tiled=True)  38.5 us
  transfers between devices with their start and end apart: 13, of which 7 were waited for; matrix products, arithmetic and copies ran while one was open for 16% of the time, Pallas kernels for 0%

commit v1 on v0

v1 whole, which is shorter than its diff:
```python
import math

import jax
import jax.numpy as jnp
from jax import lax
from jax.sharding import PartitionSpec as P

HEAD = 64
ROT = 32
QUARTERS = 4
norm_eps = 1e-05
F32 = jnp.float32
BF16 = jnp.bfloat16


def normalize(rows):
    middle = jnp.mean(rows, axis=-1, keepdims=True)
    centered = rows - middle
    spread = jnp.mean(centered * centered, axis=-1, keepdims=True)
    inv_spread = lax.rsqrt(spread + norm_eps)
    return (centered * inv_spread, inv_spread)


def rotary_tables(length):
    half_rot = ROT // 2
    position = jnp.arange(length, dtype=F32)
    freqs = jnp.exp(jnp.arange(half_rot, dtype=F32) * (-math.log(10000.0) / half_rot))
    angles = position[:, None] * freqs[None, :]
    angles = jnp.concatenate([angles, angles], axis=1)
    return (jnp.cos(angles), jnp.sin(angles))


def rotate(vectors, cosine, sine):
    half_rot = ROT // 2
    turned = vectors[..., :ROT]
    swapped = jnp.concatenate([-turned[..., half_rot:], turned[..., :half_rot]], axis=-1)
    turned = turned * cosine[:, None, :] + swapped * sine[:, None, :]
    return jnp.concatenate([turned, vectors[..., ROT:]], axis=-1)


def attend(queries, keys):
    length = queries.shape[1]
    scores = jnp.einsum("gqhe,gkhe->ghqk", queries, keys, preferred_element_type=F32) * (
        1.0 / math.sqrt(HEAD)
    )
    row_ids = lax.broadcasted_iota(jnp.int32, (length, length), 0)
    col_ids = lax.broadcasted_iota(jnp.int32, (length, length), 1)
    scores = jnp.where((col_ids <= row_ids)[None, None], scores, -1e30)
    top_score = jnp.max(scores, axis=-1, keepdims=True)
    powers = jnp.exp(scores - top_score)
    return powers / jnp.sum(powers, axis=-1, keepdims=True)


def smooth_gate(inputs):
    return jax.nn.gelu(inputs, approximate=True)


def per_device(
    tokens,
    norm_gain,
    norm_shift,
    in_weight,
    in_bias,
    out_weight,
    out_bias,
    up_weight,
    up_bias,
    down_weight,
    down_bias,
    cotangent,
):
    n_dp = lax.axis_size("dp")
    n_mp = lax.axis_size("mp")
    lines = n_dp // QUARTERS
    dp = lax.axis_index("dp")
    mp = lax.axis_index("mp")
    quarter = dp % QUARTERS
    line = dp // QUARTERS
    line_groups = [[k * QUARTERS + q for k in range(lines)] for q in range(QUARTERS)]
    team = QUARTERS * n_mp
    team_groups = [[k * team + i for i in range(team)] for k in range(lines)]
    own_rows, width = tokens.shape

    def pick(array, index, axis):
        return lax.dynamic_index_in_dim(array, index, axis, keepdims=False)

    def place(buffer, piece, index, axis):
        return lax.dynamic_update_index_in_dim(buffer, piece, index, axis)

    def swap_quarters(array, axis):
        got = []
        for j in range(QUARTERS):
            piece = pick(array, quarter ^ j, axis)
            if j:
                piece = lax.ppermute(piece, "dp", [(d, d ^ j) for d in range(n_dp)])
            got.append(piece)
        return got

    def gather_lines(piece):
        ups, downs = [piece], [piece]
        for k in range(1, lines):
            up_pairs = [
                (d, d + QUARTERS)
                for d in range(n_dp)
                if k - 1 <= d // QUARTERS < lines - 1
            ]
            down_pairs = [(n_dp - 1 - a, n_dp - 1 - b) for a, b in up_pairs]
            ups.append(lax.ppermute(ups[-1], "dp", up_pairs))
            downs.append(lax.ppermute(downs[-1], "dp", down_pairs))
        whole = jnp.zeros((lines,) + piece.shape, piece.dtype)
        whole = place(whole, piece, line, 0)
        for k in range(1, lines):
            whole = place(
                whole,
                jnp.where(line >= k, ups[k], downs[lines - k]),
                (line - k) % lines,
                0,
            )
        return whole.reshape((-1,) + piece.shape[1:])

    def gather_weight(block):
        got = swap_quarters(block, 1)
        rows = jnp.zeros((QUARTERS,) + got[0].shape, block.dtype)
        for j in range(QUARTERS):
            rows = place(rows, got[j], quarter ^ j, 0)
        return gather_lines(rows.reshape((-1,) + got[0].shape[1:]))

    def scatter_grad(grad):
        mine = lax.psum_scatter(
            grad.astype(BF16),
            "dp",
            scatter_dimension=0,
            tiled=True,
            axis_index_groups=line_groups,
        )
        got = swap_quarters(mine.reshape((QUARTERS, -1) + mine.shape[1:]), 0)
        cols = jnp.zeros((got[0].shape[0], QUARTERS) + got[0].shape[1:], F32)
        for j in range(QUARTERS):
            cols = place(cols, got[j].astype(F32), quarter ^ j, 1)
        return cols

    def gather_team(rows):
        return lax.all_gather(
            rows, ("dp", "mp"), axis=0, tiled=True, axis_index_groups=team_groups
        )

    def scatter_team(partial):
        parts = partial.astype(BF16).reshape(QUARTERS // 2, 2, n_mp, own_rows, width)
        core = dp % 2
        half = (dp // 2) % (QUARTERS // 2)
        mine = pick(parts, core, 1)
        got = lax.ppermute(pick(parts, 1 - core, 1), "dp", [(d, d ^ 1) for d in range(n_dp)])
        pair = (mine.astype(F32) + got.astype(F32)).astype(BF16)
        total = pick(pick(pair, half, 0), mp, 0).astype(F32)
        for a in range(QUARTERS // 2):
            for b in range(n_mp):
                if a or b:
                    piece = pick(pick(pair, half ^ a, 0), (mp + b) % n_mp, 0)
                    pairs = [
                        (d * n_mp + m, (d ^ (2 * a)) * n_mp + (m + b) % n_mp)
                        for d in range(n_dp)
                        for m in range(n_mp)
                    ]
                    total = total + lax.ppermute(piece, ("dp", "mp"), pairs).astype(F32)
        return total

    small = jnp.concatenate(
        [norm_gain, norm_shift, out_bias, down_bias, in_bias.reshape(-1), up_bias]
    )
    small = lax.all_gather(small, "dp", axis=0, tiled=False).astype(F32)
    each = norm_gain.shape[0]
    full_gain = small[:, :each].reshape(-1)
    full_shift = small[:, each : 2 * each].reshape(-1)
    full_out_bias = small[:, 2 * each : 3 * each].reshape(-1)
    full_down_bias = small[:, 3 * each : 4 * each].reshape(-1)
    in_each = in_bias.shape[1]
    up_each = up_bias.shape[0]
    in_part = small[:, 4 * each : 4 * each + 3 * in_each].reshape(QUARTERS, lines, 3, in_each)
    my_in_bias = pick(in_part, quarter, 0).transpose(1, 0, 2).reshape(-1)
    my_up_bias = pick(small[:, 4 * each + 3 * in_each :].reshape(QUARTERS, -1), quarter, 0)

    sequence = gather_team(tokens)
    rows_here = in_weight.shape[1]
    block_in = in_weight.transpose(1, 0, 2).reshape(rows_here, 3, QUARTERS, -1)
    block_in = block_in.transpose(0, 2, 1, 3).reshape(rows_here, QUARTERS, -1)
    full_in = gather_weight(block_in)
    full_out = gather_weight(out_weight.reshape(rows_here, QUARTERS, -1))
    full_up = gather_weight(up_weight.reshape(rows_here, QUARTERS, -1))
    full_down = gather_weight(down_weight.reshape(rows_here, QUARTERS, -1))
    grad_rows = gather_team(cotangent)

    group_rows = sequence.shape[0]
    length = n_mp * own_rows
    groups = group_rows // length
    unit_rows = normalize(sequence.astype(F32))[0]
    normed = (unit_rows * full_gain + full_shift).astype(BF16)
    projected = jnp.dot(normed, full_in, preferred_element_type=F32) + my_in_bias
    heads_here = projected.shape[1] // (3 * HEAD)
    projected = projected.reshape(groups, length, 3, heads_here, HEAD)
    cosine, sine = rotary_tables(length)
    query_pre = projected[:, :, 0]
    key_pre = projected[:, :, 1]
    queries = rotate(query_pre, cosine, sine).astype(BF16)
    keys = rotate(key_pre, cosine, sine).astype(BF16)
    values = projected[:, :, 2].astype(BF16)
    probs = attend(queries, keys)
    probs_low = probs.astype(BF16)
    mixed = jnp.einsum("ghqk,gkhe->gqhe", probs_low, values, preferred_element_type=F32)
    mixed = mixed.reshape(group_rows, heads_here * HEAD).astype(BF16)

    grad_out = jnp.einsum("sd,se->de", grad_rows, mixed, preferred_element_type=F32)
    own_grad_out = scatter_grad(grad_out)
    grad_mixed = jnp.dot(grad_rows, full_out, preferred_element_type=F32).astype(BF16)
    grad_mixed = grad_mixed.reshape(groups, length, heads_here, HEAD)
    grad_probs = jnp.einsum("gqhe,gkhe->ghqk", grad_mixed, values, preferred_element_type=F32)
    row_total = jnp.sum(probs * grad_probs, axis=-1, keepdims=True)
    grad_scores = (probs * (grad_probs - row_total)).astype(BF16)
    grad_values = jnp.einsum(
        "ghqk,gqhe->gkhe", probs_low, grad_mixed, preferred_element_type=F32
    ).astype(BF16)
    score_scale = 1.0 / math.sqrt(HEAD)
    grad_queries = (
        jnp.einsum("ghqk,gkhe->gqhe", grad_scores, keys, preferred_element_type=F32) * score_scale
    ).astype(BF16)
    grad_keys = (
        jnp.einsum("ghqk,gqhe->gkhe", grad_scores, queries, preferred_element_type=F32)
        * score_scale
    ).astype(BF16)

    def turn(vectors):
        return rotate(vectors, cosine, sine)

    turn_pull = jax.vjp(turn, query_pre)[1]
    query_back = turn_pull(grad_queries.astype(F32))[0].astype(BF16)
    key_back = turn_pull(grad_keys.astype(F32))[0].astype(BF16)
    grad_proj = jnp.stack([query_back, key_back, grad_values], axis=2).reshape(group_rows, -1)
    grad_in = jnp.einsum("sd,se->de", normed, grad_proj, preferred_element_type=F32)
    own_grad_in = scatter_grad(grad_in)
    grad_in_bias = jnp.sum(grad_proj.astype(F32), axis=0)

    preact = jnp.dot(normed, full_up, preferred_element_type=F32) + my_up_bias
    activated = smooth_gate(preact).astype(BF16)
    grad_down = jnp.einsum("sd,sf->df", grad_rows, activated, preferred_element_type=F32)
    own_grad_down = scatter_grad(grad_down)
    grad_act = jnp.dot(grad_rows, full_down, preferred_element_type=F32)
    gate_pull = jax.vjp(smooth_gate, preact)[1]
    grad_pre = gate_pull(grad_act)[0].astype(BF16)
    grad_up = jnp.einsum("sd,sf->df", normed, grad_pre, preferred_element_type=F32)
    own_grad_up = scatter_grad(grad_up)
    grad_up_bias = jnp.sum(grad_pre.astype(F32), axis=0)

    branches = jnp.einsum("se,de->sd", mixed, full_out, preferred_element_type=F32)
    branches = branches + jnp.einsum("sf,df->sd", activated, full_down, preferred_element_type=F32)
    summed = scatter_team(branches)
    outcome = (tokens.astype(F32) + summed + full_out_bias + full_down_bias).astype(BF16)

    grad_normed = jnp.einsum("sf,df->sd", grad_pre, full_up, preferred_element_type=F32)
    grad_normed = grad_normed + jnp.einsum(
        "se,de->sd", grad_proj, full_in, preferred_element_type=F32
    )
    grad_own = scatter_team(grad_normed)
    own_unit, own_inv = normalize(tokens.astype(F32))
    gain_part = jnp.sum(grad_own * own_unit, axis=0)
    shift_part = jnp.sum(grad_own, axis=0)
    bias_part = jnp.sum(cotangent.astype(F32), axis=0)
    scaled = grad_own * full_gain
    centered_grad = (
        scaled
        - jnp.mean(scaled, axis=-1, keepdims=True)
        - own_unit * jnp.mean(scaled * own_unit, axis=-1, keepdims=True)
    )
    grad_input = cotangent.astype(F32) + own_inv * centered_grad

    wide = jnp.stack([gain_part, shift_part, bias_part])
    wide = lax.psum(wide, "mp").reshape(3, n_dp, each).transpose(1, 0, 2).reshape(n_dp, 3 * each)
    in_blocks = grad_in_bias.reshape(3, lines, in_each).transpose(1, 0, 2).reshape(lines, -1)
    up_blocks = grad_up_bias.reshape(lines, up_each)
    mine = jnp.concatenate([in_blocks, up_blocks], axis=1)
    spread = place(jnp.zeros((QUARTERS,) + mine.shape, F32), mine, quarter, 0)
    vector = jnp.concatenate([wide, spread.reshape(n_dp, -1)], axis=1)
    owned = lax.psum_scatter(vector, "dp", scatter_dimension=0, tiled=True).reshape(-1)
    own_gain = owned[:each]
    own_shift = owned[each : 2 * each]
    own_bias = owned[2 * each : 3 * each]
    own_in_bias = owned[3 * each : 3 * each + 3 * in_each].reshape(3, in_each)
    own_up_bias = owned[3 * each + 3 * in_each :]

    final_in = own_grad_in.reshape(rows_here, QUARTERS, 3, -1).transpose(2, 0, 1, 3)
    return (
        outcome,
        grad_input,
        own_gain,
        own_shift,
        final_in.reshape(in_weight.shape),
        own_in_bias,
        own_grad_out.reshape(out_weight.shape),
        own_bias,
        own_grad_up.reshape(up_weight.shape),
        own_up_bias,
        own_grad_down.reshape(down_weight.shape),
        own_bias,
    )


def solution(mesh):
    return jax.shard_map(
        per_device,
        mesh=mesh,
        in_specs=(
            P(("dp", "mp"), None),
            P("dp"),
            P("dp"),
            P(None, "dp", "mp"),
            P(None, ("mp", "dp")),
            P("dp", "mp"),
            P("dp"),
            P("dp", "mp"),
            P(("mp", "dp")),
            P("dp", "mp"),
            P("dp"),
            P(("dp", "mp"), None),
        ),
        out_specs=(
            P(("dp", "mp"), None),
            P(("dp", "mp"), None),
            P("dp"),
            P("dp"),
            P(None, "dp", "mp"),
            P(None, ("mp", "dp")),
            P("dp", "mp"),
            P("dp"),
            P("dp", "mp"),
            P(("mp", "dp")),
            P("dp", "mp"),
            P("dp"),
        ),
        check_vma=False,
    )
```

time: 1660 us -> 922 us (0.56)
  waiting for transfers between devices: 1180 us -> 235 us
  local copies, waits for them, and re-layouts: 31.6 us -> 167 us
  starting transfers between devices: 0.98 us -> 63.3 us
  other arithmetic: 33.2 us -> 78.9 us
  blocking collectives: 181 us -> 156 us
  matrix products: 211 us -> 192 us
    reduce_scatter x6 -> x4, waiting for transfers between devices: 912 us -> 0.03 us  [scatter_grad(): lax.psum_scatter(grad.astype(BF16), 'dp', scatter_dimension=0, tiled=True...]
    all_gather x6 -> x2, waiting for transfers between devices: 265 us -> 0.01 us  [gather_team(): lax.all_gather(rows, ('dp', 'mp'), axis=0, tiled=True, axis_index_groups=...]
    ppermute x0 -> x56, waiting for transfers between devices: none -> 234 us  [the longest x12 125 us: gather_lines(): downs.append(lax.ppermute(downs[-1], 'dp', down_pairs))]
    all_gather x6 -> x0, blocking collectives: 113 us -> none  [the longest x1 23 us: per_device(): lax.all_gather(norm_gain, 'dp', axis=0, tiled=True)]
    unnamed x1 -> x2, blocking collectives: 62.4 us -> 148 us
    ppermute x0 -> x56, starting transfers between devices: none -> 63.1 us  [the longest x12 24.7 us: gather_lines(): ups.append(lax.ppermute(ups[-1], 'dp', up_pairs))]
    dynamic_update_slice x0 -> x30, local copies, waits for them, and re-layouts: none -> 34.3 us  [place(): return lax.dynamic_update_index_in_dim(buffer, piece, index, axis)]
    unnamed x74 -> x146, local copies, waits for them, and re-layouts: 15.9 us -> 44.6 us
  transfers between devices with their start and end apart: 13 -> 62, of which waited for: 7 -> 16; matrix products, arithmetic and copies ran while one was open for 16% -> 36% of each run, Pallas kernels for 0% -> 0%
where the time goes in v1:
time: 922 us; the launch traced here: 910 us
  waiting for transfers between devices  235 us (25%)
  matrix products  192 us (21%)
  local copies, waits for them, and re-layouts  167 us (18%)
  blocking collectives  156 us (17%)
  other arithmetic  78.9 us (9%)
  starting transfers between devices  63.3 us (7%)
  between operations  16.7 us (2%)
    unnamed x2, blocking collectives  148 us
    ppermute x12, waiting for transfers between devices, gather_lines(): downs.append(lax.ppermute(downs[-1], 'dp', down_pairs))  125 us
    ppermute x6, waiting for transfers between devices, scatter_team(): total = total + lax.ppermute(piece, ('dp', 'mp'), pairs).astype(F32)  70.4 us
    unnamed x146, local copies, waits for them, and re-layouts  44.6 us
    ppermute x24, waiting for transfers between devices, swap_quarters(): piece = lax.ppermute(piece, 'dp', [(d, d ^ j) for d in range(n_dp)])  38.9 us
    dynamic_update_slice x30, local copies, waits for them, and re-layouts, place(): return lax.dynamic_update_index_in_dim(buffer, piece, index, axis)  34.3 us
    ppermute x12, starting transfers between devices, gather_lines(): ups.append(lax.ppermute(ups[-1], 'dp', up_pairs))  24.7 us
    dynamic_slice x27, local copies, waits for them, and re-layouts, pick(): return lax.dynamic_index_in_dim(array, index, axis, keepdims=False)  23.2 us
  transfers between devices with their start and end apart: 62, of which 16 were waited for; matrix products, arithmetic and copies ran while one was open for 36% of the time, Pallas kernels for 0%

profile of v1, /device:TPU:0, one launch (start us, length us, event | category | flops | bytes accessed | tf_op | source)
XLA Modules:
  0.0 910.2 jit_solution(8385044301196506799)
XLA Ops:
  48.6 4.6 collective-permute-start.12
  54.2 15.3 %collective-permute-done.28 = bf16[128,1024]{1,0:T(8,128)(2,1)S(1)} collective-permute-done((bf16[128,1024]{1,0:T(8,128)(2,1)}, bf16[128,1024]{1,0:T(8,128)(2,1)S(1)}, u32[]{:S(2)}, u32[]{:S(2)}) %collective-permute-start.28) | collective-permute-done | bytes 262176 | tf_op jit(solution)/shard_map/ppermute | solution.py:95
  71.6 8.7 collective-permute-done.29
  81.6 5.4 collective-permute-start.3
  87.0 4.4 collective-permute-done.20
  94.8 35.6 %collective-permute-done.15 = bf16[512,256]{1,0:T(8,128)(2,1)S(1)} collective-permute-done((bf16[512,256]{1,0:T(8,128)(2,1)S(1)}, bf16[512,256]{1,0:T(8,128)(2,1)S(1)}, u32[]{:S(2)}, u32[]{:S(2)}) %collective-permute-start.15) | collective-permute-done | bytes 262176 | tf_op jit(solution)/shard_map/ppermute | solution.py:109
  135.0 5.5 collective-permute-start.21
  142.3 90.0 %all-reduce.8 = bf16[15360]{0:T(1024)(128)(2,1)S(1)} all-reduce(bf16[15360]{0:T(1024)(128)(2,1)S(1)} %dynamic-update-slice), channel_id=2, replica_groups=mesh['dp'=16,'mp'=2] {'dp'}, use_global_device_ids=true, to_apply=%add.8 | all-reduce | flops 15360 | bytes 61440
  246.7 9.2 %collective-permute-done.5 = bf16[512,768]{1,0:T(8,128)(2,1)} collective-permute-done((bf16[512,768]{1,0:T(8,128)(2,1)}, bf16[512,768]{1,0:T(8,128)(2,1)}, u32[]{:S(2)}, u32[]{:S(2)}) %collective-permute-start.5) | collective-permute-done | bytes 786464 | tf_op jit(solution)/shard_map/ppermute | solution.py:109
  265.7 12.7 %collective-permute-done.32 = bf16[512,1024]{1,0:T(8,128)(2,1)} collective-permute-done((bf16[512,1024]{1,0:T(8,128)(2,1)}, bf16[512,1024]{1,0:T(8,128)(2,1)}, u32[]{:S(2)}, u32[]{:S(2)}) %collective-permute-start.32) | collective-permute-done | bytes 1048608 | tf_op jit(solution)/shard_map/ppermute | solution.py:109
  279.0 21.8 %collective-permute-done.23 = bf16[512,1024]{1,0:T(8,128)(2,1)} collective-permute-done((bf16[512,1024]{1,0:T(8,128)(2,1)}, bf16[512,1024]{1,0:T(8,128)(2,1)}, u32[]{:S(2)}, u32[]{:S(2)}) %collective-permute-start.23) | collective-permute-done | bytes 1048608 | tf_op jit(solution)/shard_map/ppermute | solution.py:109
  304.3 13.3 %collective-permute-done.6 = bf16[512,768]{1,0:T(8,128)(2,1)S(1)} collective-permute-done((bf16[512,768]{1,0:T(8,128)(2,1)}, bf16[512,768]{1,0:T(8,128)(2,1)S(1)}, u32[]{:S(2)}, u32[]{:S(2)}) %collective-permute-start.6) | collective-permute-done | bytes 786464 | tf_op jit(solution)/shard_map/ppermute | solution.py:109
  320.4 19.7 %collective-permute-done.24 = bf16[512,1024]{1,0:T(8,128)(2,1)S(1)} collective-permute-done((bf16[512,1024]{1,0:T(8,128)(2,1)}, bf16[512,1024]{1,0:T(8,128)(2,1)S(1)}, u32[]{:S(2)}, u32[]{:S(2)}) %collective-permute-start.24) | collective-permute-done | bytes 1048608 | tf_op jit(solution)/shard_map/ppermute | solution.py:109
  341.4 2.6 bitcast_dynamic-update-slice_fusion.5
  344.0 12.8 %collective-permute-done.33 = bf16[512,1024]{1,0:T(8,128)(2,1)S(1)} collective-permute-done((bf16[512,1024]{1,0:T(8,128)(2,1)}, bf16[512,1024]{1,0:T(8,128)(2,1)S(1)}, u32[]{:S(2)}, u32[]{:S(2)}) %collective-permute-start.33) | collective-permute-done | bytes 1048608 | tf_op jit(solution)/shard_map/ppermute | solution.py:109
  358.2 2.6 bitcast_dynamic-update-slice_fusion.1
  363.5 2.6 bitcast_dynamic-update-slice_fusion
  366.1 4.7 convert_reduce_fusion
  374.2 4.1 fusion.6
  378.3 3.3 copy-done.7
  381.6 8.5 broadcast_add_fusion
  390.1 11.7 %reshape.381 = f32[4,512,3,4,64]{4,3,2,1,0:T(4,128)} reshape(f32[2048,768]{1,0:T(8,128)} %broadcast_add_fusion) | data formatting | bytes 12582912 | tf_op jit(solution)/shard_map/reshape | solution.py:199
  401.8 4.3 slice.115
  406.0 7.3 fusion.86
  413.3 3.5 copy.269
  417.7 4.7 copy.270
  428.0 6.7 fusion.32
  434.7 2.7 reshape.335
  437.4 4.1 copy.268
  441.5 3.5 fusion.65
  445.0 11.5 %fusion.92 = (f32[4,4,512]{2,1,0:T(4,128)}, f32[4,4,512,512]{2,3,1,0:T(8,128)}) fusion(pred[512,512]{0,1:T(8,128)(4,1)S(1)} %copy-done.27, bf16[4,512,4,32]{1,3,2,0:T(8,128)(2,1)S(1)} %copy-done.16, bf16[4,512,4,32]{1,3,2,0:T(8,128)(2,1)} %get-tuple-element.110, bf16[4,512,4,32]{1,3,2,0:T(8,128)(2,1)S(1)} %copy-done.15, ...), kind=kOutput, calls=%fused_computation.248 | convolution fusion | flops 557842944 | bytes 19169280 | tf_op jit(solution)/shard_map/sub | solution.py:50
  456.5 9.8 %fusion.54 = bf16[4,512,1,4,64]{1,4,3,0,2:T(8,128)(2,1)} fusion(bf16[4,512,4,64]{1,0,3,2:T(4,128)(2,1)} %reshape.335, f32[4,4,512,512]{2,3,1,0:T(8,128)} %get-tuple-element.125, f32[4,4,512]{2,1,0:T(4,128)} %get-tuple-element.124), kind=kOutput, calls=%fused_computation.90 | convolution fusion | flops 545783808 | bytes 18907136 | tf_op jit(solution)/shard_map/ghqk,gqhe->gkhe/dot_general | solution.py:218
  466.3 8.7 fusion.57
  475.1 9.3 %multiply_reduce_fusion = (f32[4,4,512]{2,1,0:T(4,128)}, f32[4,4,512,512]{2,3,1,0:T(8,128)}) fusion(f32[4,4,512,512]{2,3,1,0:T(8,128)S(1)} %bitcast.326, f32[4,4,512]{2,1,0:T(4,128)S(1)} %copy-done.40, bf16[4,512,1,4,64]{1,4,3,0,2:T(8,128)(2,1)} %copy.268, bf16[4,512,4,64]{1,0,3,2:T(4,128)(2,1)} %reshape.335), kind=kOutput, calls=%fused_computation.11 | convolution fusion | flops 549445632 | bytes 35717120 | tf_op jit(solution)/shard_map/gqhe,gkhe->ghqk/dot_general | solution.py:215
  484.4 8.3 multiply_convert_fusion
  492.6 3.8 convert_bitcast_fusion.1
  496.4 2.7 convert_bitcast_fusion.2
  499.2 14.7 %fusion.93 = f32[2048,1024]{1,0:T(8,128)} fusion(bf16[2048,2048]{1,0:T(8,128)(2,1)} %copy-done.7, bf16[2048,1024]{1,0:T(8,128)(2,1)} %bitcast.53), kind=kOutput, calls=%fused_computation.249 | convolution fusion | flops 8589934592 | bytes 20971520 | tf_op jit(solution)/shard_map/dot_general | solution.py:241
  515.0 3.4 fusion.33
  530.1 8.3 convolution_convert_fusion.1
  538.4 13.3 %fusion.94 = f32[2048,2048]{1,0:T(8,128)} fusion(bf16[2048,768]{0,1:T(8,128)(2,1)} %bitcast.355, bf16[2048,768]{1,0:T(8,128)(2,1)} %bitcast.361), kind=kOutput, calls=%fused_computation.250 | convolution fusion | flops 6442450944 | bytes 23068672 | tf_op jit(solution)/shard_map/se,de->sd/dot_general | solution.py:258
  551.7 16.5 %convert_bitcast_fusion = bf16[2048,1024]{0,1:T(8,128)(2,1)} fusion(bf16[2048,2048]{1,0:T(8,128)(2,1)} %all-gather.6.cloned.1.call-done, f32[2048,1024]{1,0:T(8,128)} %fusion.93, f32[1024]{0:T(1024)S(1)} %bitcast.391), kind=kOutput, calls=%fused_computation.41 | convolution fusion | flops 8613003264 | bytes 20975616 | tf_op jit(solution)/shard_map/sd,sf->df/dot_general | solution.py:243
  568.2 18.7 %fusion.84 = f32[2048,2048]{1,0:T(8,128)} fusion(bf16[2048,1024]{1,0:T(8,128)(2,1)} %bitcast.68, f32[2048,1024]{1,0:T(8,128)} %fusion.93, f32[1024]{0:T(1024)S(1)} %bitcast.392), kind=kOutput, calls=%fused_computation.241 | convolution fusion | flops 8610906112 | bytes 29364224 | tf_op jit(solution)/shard_map/sf,df->sd/dot_general | solution.py:253
  587.0 8.6 add_convert_fusion.1
  595.6 2.8 dynamic-slice_bitcast_fusion.1
  600.2 20.1 %convert_reduce_fusion.1 = (f32[1024]{0:T(1024)S(1)}, bf16[2048,1024]{1,0:T(8,128)(2,1)}) fusion(f32[2048,1024]{1,0:T(8,128)} %fusion.93, f32[1024]{0:T(1024)S(1)} %bitcast.393, bf16[2048,2048]{1,0:T(8,128)(2,1)} %all-gather.6.cloned.1.call-done, bf16[2048,1024]{1,0:T(8,128)(2,1)} %bitcast.68), kind=kOutput, calls=%fused_computation.34 | convolution fusion | flops 8638168064 | bytes 25174016 | tf_op jit(solution)/shard_map/dot_general | solution.py:245
  620.3 14.5 %add_convert_fusion = bf16[2048,2048]{1,0:T(8,128)(2,1)S(1)} fusion(f32[2048,2048]{1,0:T(8,128)} %fusion.94, bf16[2048,1024]{1,0:T(8,128)(2,1)} %get-tuple-element.129, bf16[2048,1024]{1,0:T(8,128)(2,1)} %bitcast.53), kind=kOutput, calls=%fused_computation.9 | convolution fusion | flops 8598323200 | bytes 33554432 | tf_op jit(solution)/shard_map/sf,df->sd/dot_general | solution.py:257
  637.4 3.0 copy-done.6
  640.9 13.4 %convolution_convert_fusion = bf16[2048,1024]{1,0:T(8,128)(2,1)} fusion(bf16[2048,2048]{1,0:T(8,128)(2,1)} %copy-done.7, bf16[2048,1024]{1,0:T(8,128)(2,1)S(1)} %copy-done.52), kind=kOutput, calls=%fused_computation.48 | convolution fusion | flops 8592031744 | bytes 16777216 | tf_op jit(solution)/shard_map/sd,sf->df/dot_general | solution.py:248
  660.8 5.4 fusion.15
  671.9 5.5 fusion.16
  682.1 34.4 %collective-permute-done.41 = bf16[256,2048]{1,0:T(8,128)(2,1)S(1)} collective-permute-done((bf16[256,2048]{1,0:T(8,128)(2,1)S(1)}, bf16[256,2048]{1,0:T(8,128)(2,1)S(1)}, u32[]{:S(2)}, u32[]{:S(2)}) %collective-permute-start.41) | collective-permute-done | bytes 1048608 | tf_op jit(solution)/shard_map/ppermute | solution.py:164
  723.4 3.3 fusion.37
  726.7 34.2 %collective-permute-done.37 = bf16[256,2048]{1,0:T(8,128)(2,1)} collective-permute-done((bf16[256,2048]{1,0:T(8,128)(2,1)}, bf16[256,2048]{1,0:T(8,128)(2,1)}, u32[]{:S(2)}, u32[]{:S(2)}) %collective-permute-start.37) | collective-permute-done | bytes 1048608 | tf_op jit(solution)/shard_map/ppermute | solution.py:164
  762.8 5.7 convert_reduce_fusion.4
  768.6 8.3 psum.7
  776.9 57.9 %all-reduce.9 = f32[16,832]{1,0:T(8,128)S(1)} all-reduce(f32[16,832]{1,0:T(8,128)S(1)} %pad_maximum_fusion.16), channel_id=3, replica_groups=mesh['dp'=16,'mp'=2] {'dp'}, use_global_device_ids=true, to_apply=%region_15.16.clone | all-reduce | flops 13312 | bytes 106496
  842.8 5.7 collective-permute-done.45
  848.6 3.3 collective-permute-done.46
  876.3 4.1 dynamic_update_slice.203
  880.5 8.3 dynamic_update_slice.204
  888.8 4.1 dynamic_update_slice.205
  893.0 3.0 copy.276
  899.5 3.2 copy.271
  (410 shorter events, 180.1 us)
Async XLA Ops:
  7.2 358.9 %all-gather.4.cloned.1.call-start = ((), (), s32[]{:S(2)}) async-start(), calls=%async_computation.4 | async-start | bytes 9437184 | tf_op jit(solution)/shard_map/all_gather | solution.py:143
  7.9 420.1 %all-gather.6.cloned.1.call-start = ((), (), s32[]{:S(2)}) async-start(), calls=%async_computation.5 | async-start | bytes 9437184 | tf_op jit(solution)/shard_map/all_gather | solution.py:143
  10.0 29.2 %collective-permute-start.9 = (bf16[128,256]{1,0:T(8,128)(2,1)}, bf16[128,256]{1,0:T(8,128)(2,1)}, u32[]{:S(2)}, u32[]{:S(2)}) collective-permute-start(bf16[128,256]{1,0:T(8,128)(2,1)} %bitcast.28), channel_id=1, source_target_pairs={{0,2},{2,0},{4,6},{6,4},{8,10},{10,8},{12,14},{14,12},{16,18},{18,... | collective-permute-start | bytes 196616 | tf_op jit(solution)/shard_map/ppermute | solution.py:95
  11.2 29.5 %collective-permute-start.10 = (bf16[128,256]{1,0:T(8,128)(2,1)}, bf16[128,256]{1,0:T(8,128)(2,1)}, u32[]{:S(2)}, u32[]{:S(2)}) collective-permute-start(bf16[128,256]{1,0:T(8,128)(2,1)} %bitcast.30), channel_id=1, source_target_pairs={{0,4},{2,6},{4,0},{6,2},{8,12},{10,14},{12,8},{14,10},{16,20},{18,... | collective-permute-start | bytes 196616 | tf_op jit(solution)/shard_map/ppermute | solution.py:95
  14.4 28.1 %collective-permute-start.11 = (bf16[128,256]{1,0:T(8,128)(2,1)}, bf16[128,256]{1,0:T(8,128)(2,1)S(1)}, u32[]{:S(2)}, u32[]{:S(2)}) collective-permute-start(bf16[128,256]{1,0:T(8,128)(2,1)} %bitcast.32), channel_id=1, source_target_pairs={{0,6},{2,4},{4,2},{6,0},{8,14},{10,12},{12,10},{14,8},{16,22},{18,... | collective-permute-start | bytes 196616 | tf_op jit(solution)/shard_map/ppermute | solution.py:95
  17.7 27.3 %collective-permute-start = (bf16[128,768]{1,0:T(8,128)(2,1)}, bf16[128,768]{1,0:T(8,128)(2,1)}, u32[]{:S(2)}, u32[]{:S(2)}) collective-permute-start(bf16[128,768]{1,0:T(8,128)(2,1)} %bitcast.8), channel_id=1, source_target_pairs={{0,2},{2,0},{4,6},{6,4},{8,10},{10,8},{12,14},{14,12},{16,18},{18,... | collective-permute-start | bytes 589832 | tf_op jit(solution)/shard_map/ppermute | solution.py:95
  18.6 27.3 %collective-permute-start.1 = (bf16[128,768]{1,0:T(8,128)(2,1)}, bf16[128,768]{1,0:T(8,128)(2,1)}, u32[]{:S(2)}, u32[]{:S(2)}) collective-permute-start(bf16[128,768]{1,0:T(8,128)(2,1)} %bitcast.10), channel_id=1, source_target_pairs={{0,4},{2,6},{4,0},{6,2},{8,12},{10,14},{12,8},{14,10},{16,20},{18,... | collective-permute-start | bytes 589832 | tf_op jit(solution)/shard_map/ppermute | solution.py:95
  20.5 635.9 %reduce-scatter.7.cloned.1.call-start = ((), (), s32[]{:S(2)}) async-start(), calls=%async_computation.7 | async-start | bytes 1310720 | tf_op jit(solution)/shard_map/reduce_scatter | solution.py:129
  39.2 8.0 collective-permute-start.2
  40.7 7.9 collective-permute-start.18
  42.5 39.1 %collective-permute-start.19 = (bf16[128,1024]{1,0:T(8,128)(2,1)}, bf16[128,1024]{1,0:T(8,128)(2,1)S(1)}, u32[]{:S(2)}, u32[]{:S(2)}) collective-permute-start(bf16[128,1024]{1,0:T(8,128)(2,1)} %bitcast.375), channel_id=1, source_target_pairs={{0,4},{2,6},{4,0},{6,2},{8,12},{10,14},{12,8},{14,10},{16,20},{18,... | collective-permute-start | bytes 786440 | tf_op jit(solution)/shard_map/ppermute | solution.py:95
  44.9 8.3 collective-permute-start.27
  45.9 23.7 %collective-permute-start.28 = (bf16[128,1024]{1,0:T(8,128)(2,1)}, bf16[128,1024]{1,0:T(8,128)(2,1)S(1)}, u32[]{:S(2)}, u32[]{:S(2)}) collective-permute-start(bf16[128,1024]{1,0:T(8,128)(2,1)} %bitcast.59), channel_id=1, source_target_pairs={{0,4},{2,6},{4,0},{6,2},{8,12},{10,14},{12,8},{14,10},{16,20},{18,... | collective-permute-start | bytes 786440 | tf_op jit(solution)/shard_map/ppermute | solution.py:95
  47.2 22.3 %collective-permute-start.13 = (bf16[512,256]{1,0:T(8,128)(2,1)}, bf16[512,256]{1,0:T(8,128)(2,1)S(1)}, u32[]{:S(2)}, u32[]{:S(2)}) collective-permute-start(bf16[512,256]{1,0:T(8,128)(2,1)} %bitcast.35), channel_id=1, source_target_pairs={{30,22},{28,20},{26,18},{24,16},{22,14},{20,12},{18,10},{16,8},{14... | collective-permute-start | bytes 786440 | tf_op jit(solution)/shard_map/ppermute | solution.py:109
  48.5 196.3 %copy-start.11 = (bf16[4,128,768]{2,1,0:T(8,128)(2,1)}, bf16[4,128,768]{2,1,0:T(8,128)(2,1)S(1)}, u32[]{:S(2)}) copy-start(bf16[4,128,768]{2,1,0:T(8,128)(2,1)S(1)} %bitcast_dynamic-update-slice_fusion.24) | copy-start | bytes 2359300
  48.6 22.3 %collective-permute-start.12 = (bf16[512,256]{1,0:T(8,128)(2,1)}, bf16[512,256]{1,0:T(8,128)(2,1)S(1)}, u32[]{:S(2)}, u32[]{:S(2)}) collective-permute-start(bf16[512,256]{1,0:T(8,128)(2,1)} %bitcast.35), channel_id=1, source_target_pairs={{0,8},{2,10},{4,12},{6,14},{8,16},{10,18},{12,20},{14,22},{16,24},... | collective-permute-start | bytes 786440 | tf_op jit(solution)/shard_map/ppermute | solution.py:108
  53.2 27.1 %collective-permute-start.29 = (bf16[128,1024]{1,0:T(8,128)(2,1)}, bf16[128,1024]{1,0:T(8,128)(2,1)S(1)}, u32[]{:S(2)}, u32[]{:S(2)}) collective-permute-start(bf16[128,1024]{1,0:T(8,128)(2,1)} %bitcast.376), channel_id=1, source_target_pairs={{0,6},{2,4},{4,2},{6,0},{8,14},{10,12},{12,10},{14,8},{16,22},{18,... | collective-permute-start | bytes 786440 | tf_op jit(solution)/shard_map/ppermute | solution.py:95
  69.5 21.9 %collective-permute-start.20 = (bf16[128,1024]{1,0:T(8,128)(2,1)}, bf16[128,1024]{1,0:T(8,128)(2,1)S(1)}, u32[]{:S(2)}, u32[]{:S(2)}) collective-permute-start(bf16[128,1024]{1,0:T(8,128)(2,1)} %bitcast.374), channel_id=1, source_target_pairs={{0,6},{2,4},{4,2},{6,0},{8,14},{10,12},{12,10},{14,8},{16,22},{18,... | collective-permute-start | bytes 786440 | tf_op jit(solution)/shard_map/ppermute | solution.py:95
  69.6 23.1 %collective-permute-start.14 = (bf16[512,256]{1,0:T(8,128)(2,1)S(1)}, bf16[512,256]{1,0:T(8,128)(2,1)S(1)}, u32[]{:S(2)}, u32[]{:S(2)}) collective-permute-start(bf16[512,256]{1,0:T(8,128)(2,1)S(1)} %collective-permute-done.13), channel_id=1, source_target_pairs={{22,14},{20,12},{18,10},{16,8},{14,6},{12,4},{10,2},{8,0},{23,15},... | collective-permute-start | bytes 786440 | tf_op jit(solution)/shard_map/ppermute | solution.py:109
  70.9 174.0 %copy-start.28 = (bf16[512,256]{1,0:T(8,128)(2,1)}, bf16[512,256]{1,0:T(8,128)(2,1)S(1)}, u32[]{:S(2)}) copy-start(bf16[512,256]{1,0:T(8,128)(2,1)S(1)} %collective-permute-done.12) | copy-start | bytes 786436
  70.9 23.2 %collective-permute-start.16 = (bf16[512,256]{1,0:T(8,128)(2,1)S(1)}, bf16[512,256]{1,0:T(8,128)(2,1)S(1)}, u32[]{:S(2)}, u32[]{:S(2)}) collective-permute-start(bf16[512,256]{1,0:T(8,128)(2,1)S(1)} %collective-permute-done.12), channel_id=1, source_target_pairs={{8,16},{10,18},{12,20},{14,22},{16,24},{18,26},{20,28},{22,30},{9,... | collective-permute-start | bytes 786440 | tf_op jit(solution)/shard_map/ppermute | solution.py:108
  80.3 53.9 %collective-permute-start.4 = (bf16[512,768]{1,0:T(8,128)(2,1)S(1)}, bf16[512,768]{1,0:T(8,128)(2,1)S(1)}, u32[]{:S(2)}, u32[]{:S(2)}) collective-permute-start(bf16[512,768]{1,0:T(8,128)(2,1)S(1)} %bitcast.357), channel_id=1, source_target_pairs={{30,22},{28,20},{26,18},{24,16},{22,14},{20,12},{18,10},{16,8},{14... | collective-permute-start | bytes 2359304 | tf_op jit(solution)/shard_map/ppermute | solution.py:109
  81.6 151.6 %collective-permute-start.3 = (bf16[512,768]{1,0:T(8,128)(2,1)S(1)}, bf16[512,768]{1,0:T(8,128)(2,1)}, u32[]{:S(2)}, u32[]{:S(2)}) collective-permute-start(bf16[512,768]{1,0:T(8,128)(2,1)S(1)} %bitcast.358), channel_id=1, source_target_pairs={{0,8},{2,10},{4,12},{6,14},{8,16},{10,18},{12,20},{14,22},{16,24},... | collective-permute-start | bytes 2359304 | tf_op jit(solution)/shard_map/ppermute | solution.py:108
  91.4 144.6 %collective-permute-start.31 = (bf16[512,1024]{1,0:T(8,128)(2,1)S(1)}, bf16[512,1024]{1,0:T(8,128)(2,1)}, u32[]{:S(2)}, u32[]{:S(2)}) collective-permute-start(bf16[512,1024]{1,0:T(8,128)(2,1)S(1)} %bitcast.346), channel_id=1, source_target_pairs={{30,22},{28,20},{26,18},{24,16},{22,14},{20,12},{18,10},{16,8},{14... | collective-permute-start | bytes 3145736 | tf_op jit(solution)/shard_map/ppermute | solution.py:109
  92.7 37.7 %collective-permute-start.15 = (bf16[512,256]{1,0:T(8,128)(2,1)S(1)}, bf16[512,256]{1,0:T(8,128)(2,1)S(1)}, u32[]{:S(2)}, u32[]{:S(2)}) collective-permute-start(bf16[512,256]{1,0:T(8,128)(2,1)S(1)} %collective-permute-done.14), channel_id=1, source_target_pairs={{14,6},{12,4},{10,2},{8,0},{15,7},{13,5},{11,3},{9,1}} | collective-permute-start | bytes 786440 | tf_op jit(solution)/shard_map/ppermute | solution.py:109
  94.0 38.8 %collective-permute-start.17 = (bf16[512,256]{1,0:T(8,128)(2,1)S(1)}, bf16[512,256]{1,0:T(8,128)(2,1)S(1)}, u32[]{:S(2)}, u32[]{:S(2)}) collective-permute-start(bf16[512,256]{1,0:T(8,128)(2,1)S(1)} %collective-permute-done.16), channel_id=1, source_target_pairs={{16,24},{18,26},{20,28},{22,30},{17,25},{19,27},{21,29},{23,31}} | collective-permute-start | bytes 786440 | tf_op jit(solution)/shard_map/ppermute | solution.py:108
  130.4 109.7 %collective-permute-start.30 = (bf16[512,1024]{1,0:T(8,128)(2,1)S(1)}, bf16[512,1024]{1,0:T(8,128)(2,1)}, u32[]{:S(2)}, u32[]{:S(2)}) collective-permute-start(bf16[512,1024]{1,0:T(8,128)(2,1)S(1)} %bitcast.347), channel_id=1, source_target_pairs={{0,8},{2,10},{4,12},{6,14},{8,16},{10,18},{12,20},{14,22},{16,24},... | collective-permute-start | bytes 3145736 | tf_op jit(solution)/shard_map/ppermute | solution.py:108
  132.9 108.6 %collective-permute-start.22 = (bf16[512,1024]{1,0:T(8,128)(2,1)S(1)}, bf16[512,1024]{1,0:T(8,128)(2,1)}, u32[]{:S(2)}, u32[]{:S(2)}) collective-permute-start(bf16[512,1024]{1,0:T(8,128)(2,1)S(1)} %bitcast.343), channel_id=1, source_target_pairs={{30,22},{28,20},{26,18},{24,16},{22,14},{20,12},{18,10},{16,8},{14... | collective-permute-start | bytes 3145736 | tf_op jit(solution)/shard_map/ppermute | solution.py:109
  135.0 110.9 %collective-permute-start.21 = (bf16[512,1024]{1,0:T(8,128)(2,1)S(1)}, bf16[512,1024]{1,0:T(8,128)(2,1)}, u32[]{:S(2)}, u32[]{:S(2)}) collective-permute-start(bf16[512,1024]{1,0:T(8,128)(2,1)S(1)} %bitcast.344), channel_id=1, source_target_pairs={{0,8},{2,10},{4,12},{6,14},{8,16},{10,18},{12,20},{14,22},{16,24},... | collective-permute-start | bytes 3145736 | tf_op jit(solution)/shard_map/ppermute | solution.py:108
  233.2 22.7 %collective-permute-start.5 = (bf16[512,768]{1,0:T(8,128)(2,1)}, bf16[512,768]{1,0:T(8,128)(2,1)}, u32[]{:S(2)}, u32[]{:S(2)}) collective-permute-start(bf16[512,768]{1,0:T(8,128)(2,1)} %copy-done.23), channel_id=1, source_target_pairs={{22,14},{20,12},{18,10},{16,8},{14,6},{12,4},{10,2},{8,0},{23,15},... | collective-permute-start | bytes 2359304 | tf_op jit(solution)/shard_map/ppermute | solution.py:109
  236.0 24.5 %collective-permute-start.7 = (bf16[512,768]{1,0:T(8,128)(2,1)}, bf16[512,768]{1,0:T(8,128)(2,1)}, u32[]{:S(2)}, u32[]{:S(2)}) collective-permute-start(bf16[512,768]{1,0:T(8,128)(2,1)} %collective-permute-done.3), channel_id=1, source_target_pairs={{8,16},{10,18},{12,20},{14,22},{16,24},{18,26},{20,28},{22,30},{9,... | collective-permute-start | bytes 2359304 | tf_op jit(solution)/shard_map/ppermute | solution.py:108
  240.2 38.2 %collective-permute-start.32 = (bf16[512,1024]{1,0:T(8,128)(2,1)}, bf16[512,1024]{1,0:T(8,128)(2,1)}, u32[]{:S(2)}, u32[]{:S(2)}) collective-permute-start(bf16[512,1024]{1,0:T(8,128)(2,1)} %collective-permute-done.31), channel_id=1, source_target_pairs={{22,14},{20,12},{18,10},{16,8},{14,6},{12,4},{10,2},{8,0},{23,15},... | collective-permute-start | bytes 3145736 | tf_op jit(solution)/shard_map/ppermute | solution.py:109
  241.5 59.4 %collective-permute-start.23 = (bf16[512,1024]{1,0:T(8,128)(2,1)}, bf16[512,1024]{1,0:T(8,128)(2,1)}, u32[]{:S(2)}, u32[]{:S(2)}) collective-permute-start(bf16[512,1024]{1,0:T(8,128)(2,1)} %collective-permute-done.22), channel_id=1, source_target_pairs={{22,14},{20,12},{18,10},{16,8},{14,6},{12,4},{10,2},{8,0},{23,15},... | collective-permute-start | bytes 3145736 | tf_op jit(solution)/shard_map/ppermute | solution.py:109
  246.0 56.2 %collective-permute-start.34 = (bf16[512,1024]{1,0:T(8,128)(2,1)}, bf16[512,1024]{1,0:T(8,128)(2,1)S(1)}, u32[]{:S(2)}, u32[]{:S(2)}) collective-permute-start(bf16[512,1024]{1,0:T(8,128)(2,1)} %collective-permute-done.30), channel_id=1, source_target_pairs={{8,16},{10,18},{12,20},{14,22},{16,24},{18,26},{20,28},{22,30},{9,... | collective-permute-start | bytes 3145736 | tf_op jit(solution)/shard_map/ppermute | solution.py:108
  255.9 47.6 %collective-permute-start.25 = (bf16[512,1024]{1,0:T(8,128)(2,1)}, bf16[512,1024]{1,0:T(8,128)(2,1)S(1)}, u32[]{:S(2)}, u32[]{:S(2)}) collective-permute-start(bf16[512,1024]{1,0:T(8,128)(2,1)} %collective-permute-done.21), channel_id=1, source_target_pairs={{8,16},{10,18},{12,20},{14,22},{16,24},{18,26},{20,28},{22,30},{9,... | collective-permute-start | bytes 3145736 | tf_op jit(solution)/shard_map/ppermute | solution.py:108
  260.5 57.0 %collective-permute-start.6 = (bf16[512,768]{1,0:T(8,128)(2,1)}, bf16[512,768]{1,0:T(8,128)(2,1)S(1)}, u32[]{:S(2)}, u32[]{:S(2)}) collective-permute-start(bf16[512,768]{1,0:T(8,128)(2,1)} %collective-permute-done.5), channel_id=1, source_target_pairs={{14,6},{12,4},{10,2},{8,0},{15,7},{13,5},{11,3},{9,1}} | collective-permute-start | bytes 2359304 | tf_op jit(solution)/shard_map/ppermute | solution.py:109
  278.3 41.8 %collective-permute-start.8 = (bf16[512,768]{1,0:T(8,128)(2,1)}, bf16[512,768]{1,0:T(8,128)(2,1)S(1)}, u32[]{:S(2)}, u32[]{:S(2)}) collective-permute-start(bf16[512,768]{1,0:T(8,128)(2,1)} %collective-permute-done.7), channel_id=1, source_target_pairs={{16,24},{18,26},{20,28},{22,30},{17,25},{19,27},{21,29},{23,31}} | collective-permute-start | bytes 2359304 | tf_op jit(solution)/shard_map/ppermute | solution.py:108
  300.8 39.2 %collective-permute-start.24 = (bf16[512,1024]{1,0:T(8,128)(2,1)}, bf16[512,1024]{1,0:T(8,128)(2,1)S(1)}, u32[]{:S(2)}, u32[]{:S(2)}) collective-permute-start(bf16[512,1024]{1,0:T(8,128)(2,1)} %collective-permute-done.23), channel_id=1, source_target_pairs={{14,6},{12,4},{10,2},{8,0},{15,7},{13,5},{11,3},{9,1}} | collective-permute-start | bytes 3145736 | tf_op jit(solution)/shard_map/ppermute | solution.py:109
  302.2 54.6 %collective-permute-start.33 = (bf16[512,1024]{1,0:T(8,128)(2,1)}, bf16[512,1024]{1,0:T(8,128)(2,1)S(1)}, u32[]{:S(2)}, u32[]{:S(2)}) collective-permute-start(bf16[512,1024]{1,0:T(8,128)(2,1)} %collective-permute-done.32), channel_id=1, source_target_pairs={{14,6},{12,4},{10,2},{8,0},{15,7},{13,5},{11,3},{9,1}} | collective-permute-start | bytes 3145736 | tf_op jit(solution)/shard_map/ppermute | solution.py:109
  303.5 59.9 %collective-permute-start.35 = (bf16[512,1024]{1,0:T(8,128)(2,1)S(1)}, bf16[512,1024]{1,0:T(8,128)(2,1)S(1)}, u32[]{:S(2)}, u32[]{:S(2)}) collective-permute-start(bf16[512,1024]{1,0:T(8,128)(2,1)S(1)} %collective-permute-done.34), channel_id=1, source_target_pairs={{16,24},{18,26},{20,28},{22,30},{17,25},{19,27},{21,29},{23,31}} | collective-permute-start | bytes 3145736 | tf_op jit(solution)/shard_map/ppermute | solution.py:108
  317.6 43.3 %collective-permute-start.26 = (bf16[512,1024]{1,0:T(8,128)(2,1)S(1)}, bf16[512,1024]{1,0:T(8,128)(2,1)S(1)}, u32[]{:S(2)}, u32[]{:S(2)}) collective-permute-start(bf16[512,1024]{1,0:T(8,128)(2,1)S(1)} %collective-permute-done.25), channel_id=1, source_target_pairs={{16,24},{18,26},{20,28},{22,30},{17,25},{19,27},{21,29},{23,31}} | collective-permute-start | bytes 3145736 | tf_op jit(solution)/shard_map/ppermute | solution.py:108
  518.4 320.3 %reduce-scatter.5.cloned.1.call-start = ((), (), s32[]{:S(2)}) async-start(), calls=%async_computation.6 | async-start | bytes 3932160 | tf_op jit(solution)/shard_map/reduce_scatter | solution.py:129
  538.4 315.2 %reduce-scatter.11.cloned.1.call-start = ((), (), s32[]{:S(2)}) async-start(), calls=%async_computation.9 | async-start | bytes 5242880 | tf_op jit(solution)/shard_map/reduce_scatter | solution.py:129
  586.9 274.3 %reduce-scatter.9.cloned.1.call-start = ((), (), s32[]{:S(2)}) async-start(), calls=%async_computation.8 | async-start | bytes 5242880 | tf_op jit(solution)/shard_map/reduce_scatter | solution.py:129
  600.2 71.7 %collective-permute-start.36 = (bf16[2,2,256,2048]{3,2,1,0:T(8,128)(2,1)}, bf16[2,2,256,2048]{3,2,1,0:T(8,128)(2,1)}, u32[]{:S(2)}, u32[]{:S(2)}) collective-permute-start(bf16[2,2,256,2048]{3,2,1,0:T(8,128)(2,1)} %dynamic-slice_bitcast_fusion.1), channel_id=1, source_target_pairs={{0,2},{2,0},{4,6},{6,4},{8,10},{10,8},{12,14},{14,12},{16,18},{18,... | collective-permute-start | bytes 12582920 | tf_op jit(solution)/shard_map/ppermute | solution.py:152
  640.4 20.4 %collective-permute-start.40 = (bf16[2,2,256,2048]{3,2,1,0:T(8,128)(2,1)}, bf16[2,2,256,2048]{3,2,1,0:T(8,128)(2,1)}, u32[]{:S(2)}, u32[]{:S(2)}) collective-permute-start(bf16[2,2,256,2048]{3,2,1,0:T(8,128)(2,1)} %dynamic-slice_bitcast_fusion), channel_id=1, source_target_pairs={{0,2},{2,0},{4,6},{6,4},{8,10},{10,8},{12,14},{14,12},{16,18},{18,... | collective-permute-start | bytes 12582920 | tf_op jit(solution)/shard_map/ppermute | solution.py:152
  658.3 2.5 collective-permute-start.47
  658.4 11.2 %collective-permute-start.48 = (bf16[128,256]{1,0:T(8,128)(2,1)S(1)}, bf16[128,256]{1,0:T(8,128)(2,1)S(1)}, u32[]{:S(2)}, u32[]{:S(2)}) collective-permute-start(bf16[128,256]{1,0:T(8,128)(2,1)S(1)} %bitcast.384), channel_id=1, source_target_pairs={{0,4},{2,6},{4,0},{6,2},{8,12},{10,14},{12,8},{14,10},{16,20},{18,... | collective-permute-start | bytes 196616 | tf_op jit(solution)/shard_map/ppermute | solution.py:95
  658.4 23.4 %collective-permute-start.49 = (bf16[128,256]{1,0:T(8,128)(2,1)S(1)}, bf16[128,256]{1,0:T(8,128)(2,1)S(1)}, u32[]{:S(2)}, u32[]{:S(2)}) collective-permute-start(bf16[128,256]{1,0:T(8,128)(2,1)S(1)} %bitcast.383), channel_id=1, source_target_pairs={{0,6},{2,4},{4,2},{6,0},{8,14},{10,12},{12,10},{14,8},{16,22},{18,... | collective-permute-start | bytes 196616 | tf_op jit(solution)/shard_map/ppermute | solution.py:95
  668.0 48.4 %collective-permute-start.41 = (bf16[256,2048]{1,0:T(8,128)(2,1)S(1)}, bf16[256,2048]{1,0:T(8,128)(2,1)S(1)}, u32[]{:S(2)}, u32[]{:S(2)}) collective-permute-start(bf16[256,2048]{1,0:T(8,128)(2,1)S(1)} %get-tuple-element.57), channel_id=1, source_target_pairs={{0,1},{1,0},{2,3},{3,2},{4,5},{5,4},{6,7},{7,6},{8,9},{9,8},{10,11... | collective-permute-start | bytes 3145736 | tf_op jit(solution)/shard_map/ppermute | solution.py:164
  669.9 53.5 %collective-permute-start.43 = (bf16[256,2048]{1,0:T(8,128)(2,1)}, bf16[256,2048]{1,0:T(8,128)(2,1)}, u32[]{:S(2)}, u32[]{:S(2)}) collective-permute-start(bf16[256,2048]{1,0:T(8,128)(2,1)} %get-tuple-element.58), channel_id=1, source_target_pairs={{0,5},{1,4},{2,7},{3,6},{4,1},{5,0},{6,3},{7,2},{8,13},{9,12},{10,... | collective-permute-start | bytes 3145736 | tf_op jit(solution)/shard_map/ppermute | solution.py:164
  670.2 53.3 %collective-permute-start.42 = (bf16[256,2048]{1,0:T(8,128)(2,1)}, bf16[256,2048]{1,0:T(8,128)(2,1)}, u32[]{:S(2)}, u32[]{:S(2)}) collective-permute-start(bf16[256,2048]{1,0:T(8,128)(2,1)} %get-tuple-element.59), channel_id=1, source_target_pairs={{0,4},{1,5},{2,6},{3,7},{4,0},{5,1},{6,2},{7,3},{8,12},{9,13},{10,... | collective-permute-start | bytes 3145736 | tf_op jit(solution)/shard_map/ppermute | solution.py:164
  680.3 80.6 %collective-permute-start.37 = (bf16[256,2048]{1,0:T(8,128)(2,1)}, bf16[256,2048]{1,0:T(8,128)(2,1)}, u32[]{:S(2)}, u32[]{:S(2)}) collective-permute-start(bf16[256,2048]{1,0:T(8,128)(2,1)} %get-tuple-element.60), channel_id=1, source_target_pairs={{0,1},{1,0},{2,3},{3,2},{4,5},{5,4},{6,7},{7,6},{8,9},{9,8},{10,11... | collective-permute-start | bytes 3145736 | tf_op jit(solution)/shard_map/ppermute | solution.py:164
  681.8 79.1 %collective-permute-start.39 = (bf16[256,2048]{1,0:T(8,128)(2,1)}, bf16[256,2048]{1,0:T(8,128)(2,1)}, u32[]{:S(2)}, u32[]{:S(2)}) collective-permute-start(bf16[256,2048]{1,0:T(8,128)(2,1)} %get-tuple-element.61), channel_id=1, source_target_pairs={{0,5},{1,4},{2,7},{3,6},{4,1},{5,0},{6,3},{7,2},{8,13},{9,12},{10,... | collective-permute-start | bytes 3145736 | tf_op jit(solution)/shard_map/ppermute | solution.py:164
  716.5 46.3 %collective-permute-start.38 = (bf16[256,2048]{1,0:T(8,128)(2,1)}, bf16[256,2048]{1,0:T(8,128)(2,1)}, u32[]{:S(2)}, u32[]{:S(2)}) collective-permute-start(bf16[256,2048]{1,0:T(8,128)(2,1)} %get-tuple-element.62), channel_id=1, source_target_pairs={{0,4},{1,5},{2,6},{3,7},{4,0},{5,1},{6,2},{7,3},{8,12},{9,13},{10,... | collective-permute-start | bytes 3145736 | tf_op jit(solution)/shard_map/ppermute | solution.py:164
  840.7 2.1 collective-permute-start.44
  840.8 7.8 collective-permute-start.45
  840.9 11.0 %collective-permute-start.46 = (bf16[128,768]{0,1:T(8,128)(2,1)S(1)}, bf16[128,768]{0,1:T(8,128)(2,1)S(1)}, u32[]{:S(2)}, u32[]{:S(2)}) collective-permute-start(bf16[128,768]{0,1:T(8,128)(2,1)S(1)} %bitcast.378), channel_id=1, source_target_pairs={{0,6},{2,4},{4,2},{6,0},{8,14},{10,12},{12,10},{14,8},{16,22},{18,... | collective-permute-start | bytes 589832 | tf_op jit(solution)/shard_map/ppermute | solution.py:95
  859.3 10.1 %collective-permute-start.53 = (bf16[128,1024]{1,0:T(8,128)(2,1)}, bf16[128,1024]{1,0:T(8,128)(2,1)}, u32[]{:S(2)}, u32[]{:S(2)}) collective-permute-start(bf16[128,1024]{1,0:T(8,128)(2,1)} %bitcast.133), channel_id=1, source_target_pairs={{0,2},{2,0},{4,6},{6,4},{8,10},{10,8},{12,14},{14,12},{16,18},{18,... | collective-permute-start | bytes 786440 | tf_op jit(solution)/shard_map/ppermute | solution.py:95
  859.6 10.9 %collective-permute-start.54 = (bf16[128,1024]{1,0:T(8,128)(2,1)S(1)}, bf16[128,1024]{1,0:T(8,128)(2,1)}, u32[]{:S(2)}, u32[]{:S(2)}) collective-permute-start(bf16[128,1024]{1,0:T(8,128)(2,1)S(1)} %bitcast.373), channel_id=1, source_target_pairs={{0,4},{2,6},{4,0},{6,2},{8,12},{10,14},{12,8},{14,10},{16,20},{18,... | collective-permute-start | bytes 786440 | tf_op jit(solution)/shard_map/ppermute | solution.py:95
  860.0 13.0 %collective-permute-start.55 = (bf16[128,1024]{1,0:T(8,128)(2,1)}, bf16[128,1024]{1,0:T(8,128)(2,1)S(1)}, u32[]{:S(2)}, u32[]{:S(2)}) collective-permute-start(bf16[128,1024]{1,0:T(8,128)(2,1)} %bitcast.137), channel_id=1, source_target_pairs={{0,6},{2,4},{4,2},{6,0},{8,14},{10,12},{12,10},{14,8},{16,22},{18,... | collective-permute-start | bytes 786440 | tf_op jit(solution)/shard_map/ppermute | solution.py:95
  867.2 30.5 %collective-permute-start.52 = (bf16[128,1024]{1,0:T(8,128)(2,1)S(1)}, bf16[128,1024]{1,0:T(8,128)(2,1)}, u32[]{:S(2)}, u32[]{:S(2)}) collective-permute-start(bf16[128,1024]{1,0:T(8,128)(2,1)S(1)} %get-tuple-element.75), channel_id=1, source_target_pairs={{0,6},{2,4},{4,2},{6,0},{8,14},{10,12},{12,10},{14,8},{16,22},{18,... | collective-permute-start | bytes 786440 | tf_op jit(solution)/shard_map/ppermute | solution.py:95
  867.8 28.1 %collective-permute-start.51 = (bf16[128,1024]{1,0:T(8,128)(2,1)}, bf16[128,1024]{1,0:T(8,128)(2,1)}, u32[]{:S(2)}, u32[]{:S(2)}) collective-permute-start(bf16[128,1024]{1,0:T(8,128)(2,1)} %get-tuple-element.76), channel_id=1, source_target_pairs={{0,4},{2,6},{4,0},{6,2},{8,12},{10,14},{12,8},{14,10},{16,20},{18,... | collective-permute-start | bytes 786440 | tf_op jit(solution)/shard_map/ppermute | solution.py:95
  869.5 3.5 collective-permute-start.50
  (59 other events, 1816.2 us)
Sparse Core Ops, SparseCore 0:
  9.9 83.0 all-gather.3
  94.8 54.4 all-gather.5
  518.6 24.7 reduce-scatter.6
  545.6 58.8 reduce-scatter.4
  606.8 76.7 reduce-scatter.10
  685.7 77.2 reduce-scatter.8

commit v2 on v1

v2 whole, which is shorter than its diff:
```python
import functools
import math

import jax
import jax.numpy as jnp
from jax import lax
from jax.experimental import pallas as pl
from jax.experimental.pallas import tpu as pltpu
from jax.sharding import PartitionSpec as P

HEAD = 64
ROT = 32
QUARTERS = 4
SMALL = 16
norm_eps = 1e-05
F32 = jnp.float32
BF16 = jnp.bfloat16


def normalize(rows):
    middle = jnp.mean(rows, axis=-1, keepdims=True)
    centered = rows - middle
    spread = jnp.mean(centered * centered, axis=-1, keepdims=True)
    inv_spread = lax.rsqrt(spread + norm_eps)
    return (centered * inv_spread, inv_spread)


def attention_kernel(heads, pre_ref, table_ref, dout_ref, mixed_ref, back_ref):
    length, wide = dout_ref.shape
    block = length // 2
    half_rot = ROT // 2
    scale = 1.0 / math.sqrt(HEAD)
    cosine, first, second = table_ref[0], table_ref[1], table_ref[2]

    def turn(v):
        return (
            v * cosine
            + pltpu.roll(v, wide - half_rot, 1) * first
            + pltpu.roll(v, half_rot, 1) * second
        )

    def turn_back(g):
        return (
            g * cosine
            + pltpu.roll(g * first, half_rot, 1)
            + pltpu.roll(g * second, wide - half_rot, 1)
        )

    queries = turn(pre_ref[0]).astype(BF16)
    keys = turn(pre_ref[1]).astype(BF16)
    values = pre_ref[2].astype(BF16)
    douts = dout_ref[...]
    head_of = lax.broadcasted_iota(jnp.int32, (block, wide), 1) // HEAD
    nothing = jnp.zeros((block, wide), BF16)
    mixed = [None, None]
    dq, dk, dv = [None, None], [None, None], [None, None]

    def dot(a, b, contract):
        return lax.dot_general(a, b, (contract, ((), ())), preferred_element_type=F32)

    def add(total, part):
        return part if total is None else total + part

    for head in range(heads):
        here = head_of == head

        def only(v):
            return jnp.where(here, v, nothing)

        q_here = [only(queries[i * block : (i + 1) * block]) for i in range(2)]
        k_here = [only(keys[i * block : (i + 1) * block]) for i in range(2)]
        v_here = [only(values[i * block : (i + 1) * block]) for i in range(2)]
        d_here = [only(douts[i * block : (i + 1) * block]) for i in range(2)]
        for i in range(2):
            seen = (i + 1) * block
            scores = dot(q_here[i], keys[:seen], ((1,), (1,))) * scale
            row = lax.broadcasted_iota(jnp.int32, (block, seen), 0) + i * block
            col = lax.broadcasted_iota(jnp.int32, (block, seen), 1)
            scores = jnp.where(col <= row, scores, -1e30)
            powers = jnp.exp(scores - jnp.max(scores, axis=1, keepdims=True))
            probs = powers * (1.0 / jnp.sum(powers, axis=1, keepdims=True))
            low = probs.astype(BF16)
            dprobs = dot(d_here[i], values[:seen], ((1,), (1,)))
            total = jnp.sum(probs * dprobs, axis=1, keepdims=True)
            dscores = (probs * (dprobs - total)).astype(BF16)
            for j in range(i + 1):
                part = slice(j * block, (j + 1) * block)
                mixed[i] = add(mixed[i], dot(low[:, part], v_here[j], ((1,), (0,))))
                dq[i] = add(dq[i], dot(dscores[:, part], k_here[j], ((1,), (0,))))
                dv[j] = add(dv[j], dot(low[:, part], d_here[i], ((0,), (0,))))
                dk[j] = add(dk[j], dot(dscores[:, part], q_here[i], ((0,), (0,))))
    mixed_ref[...] = jnp.concatenate(mixed, axis=0).astype(BF16)
    dq_low = (jnp.concatenate(dq, axis=0) * scale).astype(BF16)
    dk_low = (jnp.concatenate(dk, axis=0) * scale).astype(BF16)
    back_ref[0] = turn_back(dq_low.astype(F32)).astype(BF16)
    back_ref[1] = turn_back(dk_low.astype(F32)).astype(BF16)
    back_ref[2] = jnp.concatenate(dv, axis=0).astype(BF16)


def rotary_tables(length, heads):
    half_rot = ROT // 2
    position = jnp.arange(length, dtype=F32)
    freqs = jnp.exp(jnp.arange(half_rot, dtype=F32) * (-math.log(10000.0) / half_rot))
    angles = position[:, None] * freqs[None, :]
    cosine, sine = jnp.cos(angles), jnp.sin(angles)
    rest = jnp.zeros((length, HEAD - ROT), F32)
    none = jnp.zeros_like(sine)
    tables = jnp.stack(
        [
            jnp.concatenate([cosine, cosine, rest + 1.0], axis=1),
            jnp.concatenate([-sine, none, rest], axis=1),
            jnp.concatenate([none, sine, rest], axis=1),
        ]
    )
    return jnp.tile(tables, (1, 1, heads))


def attention(projected, tables, grad_mixed):
    _, length, wide = tables.shape
    rows = grad_mixed.shape[0]
    heads = wide // HEAD
    pairs = rows // length * heads
    return pl.pallas_call(
        functools.partial(attention_kernel, heads),
        grid=(rows // length,),
        out_shape=(
            jax.ShapeDtypeStruct((rows, wide), BF16),
            jax.ShapeDtypeStruct((3, rows, wide), BF16),
        ),
        in_specs=[
            pl.BlockSpec((3, length, wide), lambda g: (0, g, 0)),
            pl.BlockSpec((3, length, wide), lambda g: (0, 0, 0)),
            pl.BlockSpec((length, wide), lambda g: (g, 0)),
        ],
        out_specs=(
            pl.BlockSpec((length, wide), lambda g: (g, 0)),
            pl.BlockSpec((3, length, wide), lambda g: (0, g, 0)),
        ),
        compiler_params=pltpu.CompilerParams(vmem_limit_bytes=40 * 2**20),
        cost_estimate=pl.CostEstimate(
            flops=14 * pairs * length * length * HEAD,
            bytes_accessed=24 * rows * wide,
            transcendentals=pairs * length * length,
        ),
    )(projected, tables, grad_mixed)


MESH = pl.DeviceIdType.MESH


def gather_kernel(
    lines,
    tok_ref,
    cot_ref,
    in_ref,
    out_ref,
    up_ref,
    small_ref,
    seq_ref,
    grad_ref,
    heads_ref,
    up_full_ref,
    smalls_ref,
    local_sem,
    swap_send,
    swap_recv,
    team_send,
    team_recv,
    line_send,
    line_recv,
):
    dp = lax.axis_index("dp")
    mp = lax.axis_index("mp")
    quarter = dp % QUARTERS
    line = dp // QUARTERS
    other = 1 - mp
    rows = tok_ref.shape[0]
    depth = out_ref.shape[0]
    wide = out_ref.shape[1] // QUARTERS
    tall = small_ref.shape[0]
    up_wide = up_ref.shape[1] // QUARTERS

    barrier = pltpu.get_barrier_semaphore()
    for peer in ((dp ^ 1, mp), (dp ^ 2, mp), (dp ^ 3, mp), (dp, other)):
        pl.semaphore_signal(barrier, inc=1, device_id=peer, device_id_type=MESH)
    has_above = line < lines - 1
    has_below = line > 0

    @pl.when(has_above)
    def _():
        pl.semaphore_signal(barrier, inc=1, device_id=(dp + QUARTERS, mp), device_id_type=MESH)

    @pl.when(has_below)
    def _():
        pl.semaphore_signal(barrier, inc=1, device_id=(dp - QUARTERS, mp), device_id_type=MESH)

    pl.semaphore_wait(barrier, 4 + has_above.astype(jnp.int32) + has_below.astype(jnp.int32))

    def columns(index, size):
        return pl.ds(pl.multiple_of(index * size, size), size)

    def weight_views(device, to):
        part = columns(device % QUARTERS, depth)
        return (
            (small_ref, smalls_ref.at[columns(device, tall), :]),
            (up_ref.at[:, columns(to, up_wide)], up_full_ref.at[columns(device, depth), :]),
            (in_ref.at[:, :, columns(to, wide)], heads_ref.at[0:3, part, :]),
            (out_ref.at[:, columns(to, wide)], heads_ref.at[3, part, :]),
        )

    def swap(kind, j, device):
        src, dst = weight_views(device, quarter ^ j)[kind]
        return pltpu.make_async_remote_copy(
            src_ref=src,
            dst_ref=dst,
            send_sem=swap_send.at[kind, j - 1],
            recv_sem=swap_recv.at[kind, j - 1],
            device_id=(dp ^ j, mp),
            device_id_type=MESH,
        )

    def seat(device, half_of):
        return columns((device % QUARTERS) * 2 + half_of, rows)

    rows_of = ((tok_ref, seq_ref), (cot_ref, grad_ref))

    def relay(which, number, place, peer):
        view = rows_of[which][1].at[place, :]
        return pltpu.make_async_remote_copy(
            src_ref=view,
            dst_ref=view,
            send_sem=team_send.at[which, number],
            recv_sem=team_recv.at[which, number],
            device_id=peer,
            device_id_type=MESH,
        )

    def offer(which, number, peer):
        src, dst = rows_of[which]
        return pltpu.make_async_remote_copy(
            src_ref=src,
            dst_ref=dst.at[seat(dp, mp), :],
            send_sem=team_send.at[which, number],
            recv_sem=team_recv.at[which, number],
            device_id=peer,
            device_id_type=MESH,
        )

    across, aside, twin = (dp ^ 2, mp), (dp, other), (dp ^ 1, mp)

    def part_seat(device, half_of, part):
        low = rows // 4 * 3
        start = ((device % QUARTERS) * 2 + half_of) * rows + part * low
        size = rows - low if part else low
        return pl.ds(pl.multiple_of(start, rows // 4), size)

    def line_views(kind, chunk):
        if kind == 0:
            return smalls_ref.at[columns(chunk, QUARTERS * tall), :]
        return up_full_ref.at[columns(chunk, QUARTERS * depth), :]

    def line_copy(kind, way, step, chunk):
        view = line_views(kind, chunk)
        return pltpu.make_async_remote_copy(
            src_ref=view,
            dst_ref=view,
            send_sem=line_send.at[kind, way, step - 1],
            recv_sem=line_recv.at[kind, way, step - 1],
            device_id=(dp + (QUARTERS if way == 0 else -QUARTERS), mp),
            device_id_type=MESH,
        )

    def sends(way, step):
        if way == 0:
            return (line >= step - 1) & has_above, line - (step - 1)
        return (line <= lines - step) & has_below, line + (step - 1)

    def takes(way, step):
        if way == 0:
            return line >= step, line - step
        return line <= lines - 1 - step, line + step

    def start_line(kinds, step):
        for kind in kinds:
            for way in (0, 1):
                go, chunk = sends(way, step)

                @pl.when(go)
                def _():
                    line_copy(kind, way, step, chunk).start()

    def wait_line(kinds, step):
        for kind in kinds:
            for way in (0, 1):
                go, chunk = takes(way, step)

                @pl.when(go)
                def _():
                    line_copy(kind, way, step, chunk).wait_recv()

    own = []
    for kind, (src, dst) in enumerate(weight_views(dp, quarter)):
        own.append(pltpu.make_async_copy(src, dst, local_sem.at[kind]))
    for which, (src, dst) in enumerate(rows_of):
        own.append(
            pltpu.make_async_copy(src, dst.at[seat(dp, mp), :], local_sem.at[4 + which])
        )
    pending = []

    def begin(*copies):
        for copy in copies:
            copy.start()
            pending.append(copy)

    near, beside = seat(dp ^ 2, mp), seat(dp, other)

    def pass_on(which):
        relay(which, 0, near, across).wait_recv()
        begin(
            relay(which, 3, part_seat(dp ^ 2, mp, 0), aside),
            relay(which, 4, near, twin),
        )
        relay(which, 1, beside, aside).wait_recv()
        begin(
            relay(which, 5, part_seat(dp, other, 1), across),
            relay(which, 6, beside, twin),
        )

    def hand_over(which):
        for part, peer in ((0, aside), (1, across)):
            far = part_seat(dp ^ 2, other, part)
            relay(which, 3 + 2 * part, far, peer).wait_recv()
            begin(relay(which, 7 + part, far, twin))

    for kind in (0, 1):
        begin(*[swap(kind, j, dp) for j in (2, 3, 1)])
        own[kind].start()
    begin(offer(0, 1, aside), offer(0, 2, twin))
    for kind in (2, 3, 4, 5):
        own[kind].start()
    for kind in (0, 1):
        own[kind].wait()
        for j in (1, 2, 3):
            swap(kind, j, dp ^ j).wait_recv()
    if lines > 1:
        start_line((0, 1), 1)
    begin(offer(0, 0, across), offer(1, 1, aside), offer(1, 2, twin))

    def tokens_round():
        pass_on(0)
        begin(offer(1, 0, across))
        hand_over(0)

    def grads_round():
        pass_on(1)
        for kind in (2, 3):
            begin(*[swap(kind, j, dp) for j in (2, 3, 1)])

    rounds = [tokens_round, grads_round]
    for step in range(1, lines):
        wait_line((0, 1), step)
        if step < lines - 1:
            start_line((0, 1), step + 1)
        if rounds:
            rounds.pop(0)()
    for left in rounds:
        left()
    hand_over(1)

    for number in (2, 3, 4, 5):
        own[number].wait()
    for kind in (2, 3):
        for j in (1, 2, 3):
            swap(kind, j, dp ^ j).wait_recv()
    for which in (0, 1):
        relay(which, 2, seat(dp ^ 1, mp), twin).wait_recv()
        relay(which, 4, seat(dp ^ 3, mp), twin).wait_recv()
        relay(which, 6, seat(dp ^ 1, other), twin).wait_recv()
        for part in (0, 1):
            relay(which, 7 + part, part_seat(dp ^ 3, other, part), twin).wait_recv()
    for copy in pending:
        copy.wait_send()
    for kind in (0, 1):
        for step in range(1, lines):
            for way in (0, 1):
                go, chunk = sends(way, step)

                @pl.when(go)
                def _():
                    line_copy(kind, way, step, chunk).wait_send()


def gather_first(lines, team, tokens, cotangent, in_weight, out_weight, up_weight, small):
    depth = out_weight.shape[0]
    wide = out_weight.shape[1] // QUARTERS
    up_wide = up_weight.shape[1] // QUARTERS
    whole = lines * QUARTERS * depth
    anywhere = pl.BlockSpec(memory_space=pl.ANY)
    steps = max(lines - 1, 1)
    together = jax.ShapeDtypeStruct((team * tokens.shape[0], tokens.shape[1]), BF16)
    return pl.pallas_call(
        functools.partial(gather_kernel, lines),
        out_shape=(
            together,
            together,
            jax.ShapeDtypeStruct((4, QUARTERS * depth, wide), BF16),
            jax.ShapeDtypeStruct((whole, up_wide), BF16),
            jax.ShapeDtypeStruct((lines * QUARTERS * small.shape[0], small.shape[1]), BF16),
        ),
        in_specs=[anywhere] * 6,
        out_specs=(anywhere,) * 5,
        scratch_shapes=[
            pltpu.SemaphoreType.DMA((6,)),
            pltpu.SemaphoreType.DMA((4, 3)),
            pltpu.SemaphoreType.DMA((4, 3)),
            pltpu.SemaphoreType.DMA((2, 9)),
            pltpu.SemaphoreType.DMA((2, 9)),
            pltpu.SemaphoreType.DMA((2, 2, steps)),
            pltpu.SemaphoreType.DMA((2, 2, steps)),
        ],
        compiler_params=pltpu.CompilerParams(collective_id=1, has_side_effects=True),
    )(tokens, cotangent, in_weight, out_weight, up_weight, small)


def small_kernel(lines, both, vec_ref, total_ref, land_a, part, land_b, land_c, send, recv):
    dp = lax.axis_index("dp")
    mp = lax.axis_index("mp")
    quarter = dp % QUARTERS
    line = dp // QUARTERS
    aside = (dp, 1 - mp)

    def in_line(k):
        return (lax.rem(line + k, lines) * QUARTERS + quarter, mp)

    barrier = pltpu.get_barrier_semaphore()
    peers = [(dp ^ j, mp) for j in (1, 2, 3)] + [in_line(k) for k in range(1, lines)] + [aside]
    for peer in peers:
        pl.semaphore_signal(barrier, inc=1, device_id=peer, device_id_type=MESH)
    pl.semaphore_wait(barrier, len(peers))

    def move(number, src, dst, peer):
        return pltpu.make_async_remote_copy(
            src_ref=src,
            dst_ref=dst,
            send_sem=send.at[number],
            recv_sem=recv.at[number],
            device_id=peer,
            device_id_type=MESH,
        )

    first = [
        move(j - 1, vec_ref.at[quarter ^ j], land_a.at[j - 1], (dp ^ j, mp)) for j in (1, 2, 3)
    ]
    for copy in first:
        copy.start()
    for copy in first:
        copy.wait()
    part[...] = (vec_ref[quarter] + land_a[0]) + (land_a[1] + land_a[2])
    second = [
        move(2 + k, part.at[lax.rem(line + k, lines)], land_b.at[k - 1], in_line(k))
        for k in range(1, lines)
    ]
    for copy in second:
        copy.start()
    total = part[line]
    for k, copy in enumerate(second):
        copy.wait()
        total = total + land_b[k]
    total_ref[...] = total
    third = move(2 + lines, total_ref, land_c, aside)
    third.start()
    third.wait()
    shape = total_ref.shape
    index = lax.broadcasted_iota(jnp.int32, shape, 0) * shape[1]
    index = index + lax.broadcasted_iota(jnp.int32, shape, 1)
    total_ref[...] = jnp.where(index < both, total + land_c[...], total)


def sum_small(lines, both, vector):
    tile = vector.shape[2:]
    count = lines + 3
    return pl.pallas_call(
        functools.partial(small_kernel, lines, both),
        out_shape=jax.ShapeDtypeStruct(tile, F32),
        in_specs=[pl.BlockSpec(memory_space=pltpu.VMEM)],
        out_specs=pl.BlockSpec(memory_space=pltpu.VMEM),
        scratch_shapes=[
            pltpu.VMEM((3, lines) + tile, F32),
            pltpu.VMEM((lines,) + tile, F32),
            pltpu.VMEM((max(lines - 1, 1),) + tile, F32),
            pltpu.VMEM(tile, F32),
            pltpu.SemaphoreType.DMA((count,)),
            pltpu.SemaphoreType.DMA((count,)),
        ],
        compiler_params=pltpu.CompilerParams(collective_id=2, has_side_effects=True),
    )(vector)


def smooth_gate(u):
    slope = math.sqrt(2.0 / math.pi)
    square = u * u
    curve = jnp.tanh(slope * (u + 0.044715 * (u * square)))
    rise = 0.5 * (1.0 + curve)
    bend = 0.5 * u * (1.0 - curve * curve) * (slope * (1.0 + 3.0 * 0.044715 * square))
    return u * rise, rise + bend


def norm_kernel(rows_ref, gain_ref, shift_ref, out_ref):
    rows = rows_ref[...].astype(F32)
    unit = normalize(rows)[0]
    out_ref[...] = (unit * gain_ref[...] + shift_ref[...]).astype(BF16)


def norm_rows(rows, gain, shift):
    count, width = rows.shape
    block = min(count, 256)
    return pl.pallas_call(
        norm_kernel,
        grid=(count // block,),
        out_shape=jax.ShapeDtypeStruct((count, width), BF16),
        in_specs=[
            pl.BlockSpec((block, width), lambda i: (i, 0)),
            pl.BlockSpec((1, width), lambda i: (0, 0)),
            pl.BlockSpec((1, width), lambda i: (0, 0)),
        ],
        out_specs=pl.BlockSpec((block, width), lambda i: (i, 0)),
        cost_estimate=pl.CostEstimate(
            flops=8 * count * width, bytes_accessed=4 * count * width, transcendentals=0
        ),
    )(rows, gain, shift)


def per_device(
    tokens,
    norm_gain,
    norm_shift,
    in_weight,
    in_bias,
    out_weight,
    out_bias,
    up_weight,
    up_bias,
    down_weight,
    down_bias,
    cotangent,
):
    n_dp = lax.axis_size("dp")
    n_mp = lax.axis_size("mp")
    lines = n_dp // QUARTERS
    dp = lax.axis_index("dp")
    mp = lax.axis_index("mp")
    quarter = dp % QUARTERS
    line = dp // QUARTERS
    team = QUARTERS * n_mp
    own_rows, width = tokens.shape

    last = [None]

    def then(*values):
        if last[0] is not None:
            *values, last[0] = lax.optimization_barrier(values + (last[0],))
        return values if len(values) > 1 else values[0]

    def ended(value):
        last[0] = value
        return value

    def pick(array, index, axis):
        return lax.dynamic_index_in_dim(array, index, axis, keepdims=False)

    def place(buffer, piece, index, axis):
        return lax.dynamic_update_index_in_dim(buffer, piece, index, axis)

    def swap_quarters(array, axis):
        got = []
        for j in range(QUARTERS):
            piece = pick(array, quarter ^ j, axis)
            if j:
                piece = lax.ppermute(piece, "dp", [(d, d ^ j) for d in range(n_dp)])
            got.append(piece)
        return got

    class Lines:
        def __init__(self, piece):
            self.ups, self.downs = [piece], [piece]

        def step(self):
            k = len(self.ups)
            if k < lines:
                up_pairs = [
                    (d, d + QUARTERS)
                    for d in range(n_dp)
                    if k - 1 <= d // QUARTERS < lines - 1
                ]
                down_pairs = [(n_dp - 1 - a, n_dp - 1 - b) for a, b in up_pairs]
                self.ups.append(lax.ppermute(self.ups[-1], "dp", up_pairs))
                self.downs.append(lax.ppermute(self.downs[-1], "dp", down_pairs))

        def meet(self):
            if len(self.ups) > 1:
                self.ups[-1], self.downs[-1] = then(self.ups[-1], self.downs[-1])
                ended(self.ups[-1])
                ended(self.downs[-1])

        def whole(self, axis):
            while len(self.ups) < lines:
                self.step()
            self.meet()
            slots = []
            for slot in range(lines):
                case = [
                    self.ups[k - slot] if k >= slot else self.downs[slot - k]
                    for k in range(lines)
                ]
                slots.append(lax.select_n(jnp.broadcast_to(line, case[0].shape), *case))
            return jnp.concatenate(slots, axis=axis)

    def in_order(got):
        which = jnp.broadcast_to(quarter, got[0].shape)
        return [
            lax.select_n(which, *[got[k ^ slot] for k in range(QUARTERS)])
            for slot in range(QUARTERS)
        ]

    def swap_rows(block):
        return jnp.concatenate(in_order(swap_quarters(block, 1)), axis=0)

    class Sums:
        def __init__(self, chunk):
            self.chunk = chunk
            self.ups, self.downs = [], []

        def add(self, index, got):
            part = self.chunk(jnp.clip(index, 0, lines - 1))
            if not got:
                return part.astype(BF16)
            return (part.astype(F32) + got[-1].astype(F32)).astype(BF16)

        def step(self):
            k = len(self.ups) + 1
            if k < lines:
                up_pairs = [
                    (d, d + QUARTERS)
                    for d in range(n_dp)
                    if d // QUARTERS <= min(k - 1, lines - 2)
                ]
                down_pairs = [(n_dp - 1 - a, n_dp - 1 - b) for a, b in up_pairs]
                up = self.add(line + (lines - k), self.ups)
                down = self.add(line - (lines - k), self.downs)
                self.ups.append(lax.ppermute(up, "dp", up_pairs))
                self.downs.append(lax.ppermute(down, "dp", down_pairs))

        def meet(self):
            if self.ups:
                self.ups[-1], self.downs[-1] = then(self.ups[-1], self.downs[-1])
                ended(self.downs[-1])

        def total(self):
            while len(self.ups) < lines - 1:
                self.meet()
                self.step()
            self.meet()
            part = self.chunk(line).astype(F32)
            return (part + self.ups[-1].astype(F32) + self.downs[-1].astype(F32)).astype(BF16)

    def hand_out(total, axis):
        shape = total.shape
        got = swap_quarters(total.reshape(shape[:axis] + (QUARTERS, -1) + shape[-1:]), axis)
        return jnp.concatenate([piece.astype(F32) for piece in in_order(got)], axis=axis + 1)

    def chunk_of(grad, axis):
        size = grad.shape[axis] // lines

        def chunk(index):
            return lax.dynamic_slice_in_dim(grad, index * size, size, axis)

        return chunk

    core = dp % 2
    half = (dp // 2) % (QUARTERS // 2)

    def of_core(array, which):
        parts = array.reshape((QUARTERS // 2, 2, n_mp * own_rows) + array.shape[1:])
        return pick(parts, which, 1).reshape((-1,) + array.shape[1:])

    def to_twin(rows):
        return lax.ppermute(rows, "dp", [(d, d ^ 1) for d in range(n_dp)])

    def to_owners(pair):
        pair = pair.reshape(QUARTERS // 2, n_mp, own_rows, width)
        parts = []
        for a in range(QUARTERS // 2):
            for b in range(n_mp):
                piece = pick(pick(pair, half ^ a, 0), (mp + b) % n_mp, 0)
                if a or b:
                    pairs = [
                        (d * n_mp + m, (d ^ (2 * a)) * n_mp + (m + b) % n_mp)
                        for d in range(n_dp)
                        for m in range(n_mp)
                    ]
                    piece = lax.ppermute(piece, ("dp", "mp"), pairs)
                parts.append(piece)
        return parts

    def add_up(parts):
        return sum(part.astype(F32) for part in parts)

    small = jnp.concatenate(
        [norm_gain, norm_shift, out_bias, down_bias, in_bias.reshape(-1), up_bias]
    )
    small = jnp.pad(small, (0, SMALL * 128 - small.shape[0])).reshape(SMALL, 128)
    sequence, grad_rows, heads_part, full_up, small = gather_first(
        lines, team, tokens, cotangent, in_weight, out_weight, up_weight, small
    )
    small = small.reshape(n_dp, -1).astype(F32)
    each = norm_gain.shape[0]
    full_gain = small[:, :each].reshape(-1)
    full_shift = small[:, each : 2 * each].reshape(-1)
    full_out_bias = small[:, 2 * each : 3 * each].reshape(-1)
    full_down_bias = small[:, 3 * each : 4 * each].reshape(-1)
    in_each = in_bias.shape[1]
    up_each = up_bias.shape[0]
    in_part = small[:, 4 * each : 4 * each + 3 * in_each].reshape(QUARTERS, lines, 3, in_each)
    my_in_bias = pick(in_part, quarter, 0).transpose(1, 0, 2).reshape(3, 1, -1)
    ends = 4 * each + 3 * in_each
    my_up_bias = pick(small[:, ends : ends + up_each].reshape(QUARTERS, -1), quarter, 0)

    rows_here = in_weight.shape[1]
    ended(sequence)
    heads_lines = Lines(heads_part)
    heads_lines.step()
    down_block = then(down_weight.reshape(rows_here, QUARTERS, -1))
    down_part = swap_rows(down_block)

    length = n_mp * own_rows
    normed = norm_rows(sequence, full_gain.reshape(1, -1), full_shift.reshape(1, -1))
    ended(normed)
    heads_lines.meet()
    heads_lines.step()
    preact = jnp.dot(normed, full_up, preferred_element_type=F32) + my_up_bias
    activated, slope = smooth_gate(preact)
    activated, slope = lax.optimization_barrier((activated.astype(BF16), slope.astype(BF16)))
    ended(activated)
    grad_down = jnp.einsum(
        "sd,sf->df", then(grad_rows), activated, preferred_element_type=F32
    ).astype(BF16)
    ended(grad_down)
    down_sums = Sums(chunk_of(grad_down, 0))
    down_sums.step()
    heads_lines.meet()
    heads_lines.step()
    down_part = ended(then(down_part))
    heads_lines.meet()
    down_lines = Lines(then(down_part))
    down_lines.step()
    down_sums.meet()
    down_sums.step()

    full_heads = heads_lines.whole(1)
    full_in, full_out = full_heads[:3], full_heads[3]
    projected = (
        jnp.einsum("sd,kde->kse", then(normed), full_in, preferred_element_type=F32) + my_in_bias
    )
    ended(projected)
    grad_mixed = jnp.dot(
        then(grad_rows), full_out, preferred_element_type=F32
    ).astype(BF16)
    ended(grad_mixed)
    down_lines.meet()
    down_lines.step()
    down_sums.meet()
    down_sums.step()
    tables = rotary_tables(length, projected.shape[2] // HEAD)
    mixed, grad_proj = attention(then(projected), tables, grad_mixed)
    ended(grad_proj)
    down_lines.meet()
    down_lines.step()
    grad_out = jnp.einsum(
        "sd,se->de", then(grad_rows), mixed, preferred_element_type=F32
    ).astype(BF16)
    ended(grad_out)
    grad_in = jnp.einsum(
        "sd,kse->kde", then(normed), grad_proj, preferred_element_type=F32
    ).astype(BF16)
    ended(grad_in)
    in_chunk, out_chunk = chunk_of(grad_in, 1), chunk_of(grad_out, 0)
    heads_sums = Sums(lambda k: jnp.concatenate([in_chunk(k), out_chunk(k)[None]], axis=0))
    heads_sums.step()
    grad_in_bias = jnp.sum(grad_proj.astype(F32), axis=1)
    down_sums.meet()
    own_grad_down = hand_out(down_sums.total(), 0)

    full_down = ended(down_lines.whole(0))
    grad_act = jnp.dot(then(grad_rows), full_down, preferred_element_type=F32)
    grad_pre = ended((grad_act * slope.astype(F32)).astype(BF16))
    heads_sums.meet()
    heads_sums.step()
    grad_up = jnp.einsum(
        "sd,sf->df", then(normed), grad_pre, preferred_element_type=F32
    ).astype(BF16)
    ended(grad_up)
    up_sums = Sums(chunk_of(grad_up, 0))
    up_sums.step()
    grad_up_bias = jnp.sum(grad_pre.astype(F32), axis=0)

    def forward_part(which):
        some_mixed, some_act = then(of_core(mixed, which), of_core(activated, which))
        sums = jnp.dot(some_act, full_down.T, preferred_element_type=F32)
        sums = sums + jnp.dot(some_mixed, full_out.T, preferred_element_type=F32)
        return ended(sums.astype(BF16))

    def backward_part(which):
        some_pre, some_proj = then(
            of_core(grad_pre, which), jnp.stack([of_core(grad_proj[k], which) for k in range(3)])
        )
        sums = jnp.dot(some_pre, full_up.T, preferred_element_type=F32)
        sums = sums + jnp.einsum("kse,kde->sd", some_proj, full_in, preferred_element_type=F32)
        return ended(sums.astype(BF16))

    def paired(mine, got):
        mine, got = then(mine, got)
        return ended((mine.astype(F32) + got.astype(F32)).astype(BF16))

    got = to_twin(forward_part(1 - core))
    mine = forward_part(core)
    heads_sums.meet()
    heads_sums.step()
    forward_parts = to_owners(paired(mine, got))
    got = to_twin(backward_part(1 - core))
    up_sums.meet()
    up_sums.step()
    mine = backward_part(core)
    heads_sums.meet()
    own_heads = hand_out(heads_sums.total(), 1)
    own_grad_in, own_grad_out = own_heads[:3], own_heads[3]
    backward_parts = to_owners(paired(mine, got))
    up_sums.meet()
    up_sums.step()
    forward_parts = then(*forward_parts)
    summed = ended(add_up(forward_parts))
    up_sums.meet()
    own_grad_up = hand_out(up_sums.total(), 0)
    outcome = (tokens.astype(F32) + summed + full_out_bias + full_down_bias).astype(BF16)

    grad_own = add_up(backward_parts)
    own_unit, own_inv = normalize(tokens.astype(F32))
    gain_part = jnp.sum(grad_own * own_unit, axis=0)
    shift_part = jnp.sum(grad_own, axis=0)
    bias_part = jnp.sum(cotangent.astype(F32), axis=0)
    scaled = grad_own * full_gain
    centered_grad = (
        scaled
        - jnp.mean(scaled, axis=-1, keepdims=True)
        - own_unit * jnp.mean(scaled * own_unit, axis=-1, keepdims=True)
    )
    grad_input = cotangent.astype(F32) + own_inv * centered_grad

    wide = jnp.stack([gain_part, shift_part, bias_part])
    wide = wide.reshape(3, lines, QUARTERS, each).transpose(2, 1, 0, 3)
    wide = wide.reshape(QUARTERS, lines, 3 * each)
    in_blocks = grad_in_bias.reshape(3, lines, in_each).transpose(1, 0, 2).reshape(lines, -1)
    mine = jnp.concatenate([in_blocks, grad_up_bias.reshape(lines, up_each)], axis=1)
    spread = place(jnp.zeros((QUARTERS,) + mine.shape, F32), mine, quarter, 0)
    spread = spread.reshape(lines, QUARTERS, -1).transpose(1, 0, 2)
    vector = jnp.concatenate([wide, spread], axis=2)
    vector = jnp.pad(vector, ((0, 0), (0, 0), (0, 1024 - vector.shape[2])))
    owned = sum_small(lines, 3 * each, vector.reshape(QUARTERS, lines, 8, 128)).reshape(-1)
    own_gain = owned[:each]
    own_shift = owned[each : 2 * each]
    own_bias = owned[2 * each : 3 * each]
    own_in_bias = owned[3 * each : 3 * each + 3 * in_each].reshape(3, in_each)
    own_up_bias = owned[3 * each + 3 * in_each : 3 * each + 3 * in_each + up_each]

    return (
        outcome,
        grad_input,
        own_gain,
        own_shift,
        own_grad_in.reshape(in_weight.shape),
        own_in_bias,
        own_grad_out.reshape(out_weight.shape),
        own_bias,
        own_grad_up.reshape(up_weight.shape),
        own_up_bias,
        own_grad_down.reshape(down_weight.shape),
        own_bias,
    )


def solution(mesh):
    return jax.shard_map(
        per_device,
        mesh=mesh,
        in_specs=(
            P(("dp", "mp"), None),
            P("dp"),
            P("dp"),
            P(None, "dp", "mp"),
            P(None, ("mp", "dp")),
            P("dp", "mp"),
            P("dp"),
            P("dp", "mp"),
            P(("mp", "dp")),
            P("dp", "mp"),
            P("dp"),
            P(("dp", "mp"), None),
        ),
        out_specs=(
            P(("dp", "mp"), None),
            P(("dp", "mp"), None),
            P("dp"),
            P("dp"),
            P(None, "dp", "mp"),
            P(None, ("mp", "dp")),
            P("dp", "mp"),
            P("dp"),
            P("dp", "mp"),
            P(("mp", "dp")),
            P("dp", "mp"),
            P("dp"),
        ),
        check_vma=False,
    )
```

time: 922 us -> 648 us (0.70)
  blocking collectives: 156 us -> 0 us
  Pallas kernels: 0 us -> 150 us
  waiting for transfers between devices: 235 us -> 113 us
  local copies, waits for them, and re-layouts: 167 us -> 63 us
  matrix products: 192 us -> 122 us
  starting transfers between devices: 63.3 us -> 121 us
  between operations: 16.7 us -> 2.37 us
  other arithmetic: 78.9 us -> 66.4 us
    pallas_call x0 -> x4, Pallas kernels: none -> 150 us  [the longest x1 96.4 us: gather_first(): pl.pallas_call(functools.partial(gather_kernel, lines), out_shape=(togeth...]
    unnamed x2 -> x0, blocking collectives: 148 us -> none
    ppermute x32 -> x38, waiting for transfers between devices: 195 us -> 107 us  [the longest x6 48.1 us: to_owners(): piece = lax.ppermute(piece, ('dp', 'mp'), pairs)]
    ppermute x32 -> x38, starting transfers between devices: 46.4 us -> 113 us  [the longest x9 69.6 us: step(): self.ups.append(lax.ppermute(up, 'dp', up_pairs))]
    dot_general x16 -> x15, matrix products: 166 us -> 103 us  [the longest x1 13.4 us: per_device(): grad_act = jnp.dot(then(grad_rows), full_down, preferred_element_type=F32)]
    unnamed x146 -> x169, local copies, waits for them, and re-layouts: 44.6 us -> 6.46 us
    dynamic_update_slice x30 -> x1, local copies, waits for them, and re-layouts: 34.3 us -> 0.07 us  [place(): return lax.dynamic_update_index_in_dim(buffer, piece, index, axis)]
    ppermute x24 -> x12, waiting for transfers between devices: 38.9 us -> 5.45 us  [swap_quarters(): piece = lax.ppermute(piece, 'dp', [(d, d ^ j) for d in range(n_dp)])]
  transfers between devices with their start and end apart: 62 -> 50, of which waited for: 16 -> 11; matrix products, arithmetic and copies ran while one was open for 36% -> 34% of each run, Pallas kernels for 0% -> 8%
where the time goes in v2:
time: 648 us; the launch traced here: 637 us
  Pallas kernels  150 us (23%)
  matrix products  122 us (19%)
  starting transfers between devices  121 us (19%)
  waiting for transfers between devices  113 us (17%)
  other arithmetic  66.4 us (10%)
  local copies, waits for them, and re-layouts  63 us (10%)
    pallas_call x1, Pallas kernels, gather_first(): pl.pallas_call(functools.partial(gather_kernel, lines), out_shape=(togeth...  96.4 us
    ppermute x9, starting transfers between devices, step(): self.ups.append(lax.ppermute(up, 'dp', up_pairs))  69.6 us
    ppermute x6, waiting for transfers between devices, to_owners(): piece = lax.ppermute(piece, ('dp', 'mp'), pairs)  48.1 us
    ppermute x9, waiting for transfers between devices, step(): self.ups.append(lax.ppermute(up, 'dp', up_pairs))  34.1 us
    pallas_call x1, Pallas kernels, attention(): pl.pallas_call(functools.partial(attention_kernel, heads), grid=(rows //...  24.3 us
    convert_element_type x8, other arithmetic, add(): return (part.astype(F32) + got[-1].astype(F32)).astype(BF16)  20.3 us
    dynamic_slice x14, local copies, waits for them, and re-layouts, pick(): return lax.dynamic_index_in_dim(array, index, axis, keepdims=False)  19.3 us
    dot_general x1, matrix products, per_device(): preact = jnp.dot(normed, full_up, preferred_element_type=F32) + my_up_bias  18.8 us
  transfers between devices with their start and end apart: 50, of which 11 were waited for; matrix products, arithmetic and copies ran while one was open for 34% of the time, Pallas kernels for 8%

profile of v2, /device:TPU:0, one launch (start us, length us, event | category | flops | bytes accessed | tf_op | source)
XLA Modules:
  0.0 637.2 jit_solution(5105167933716605300)
XLA Ops:
  1.5 3.4 concatenate.67
  5.5 96.4 %shard_map.211 = (bf16[2048,2048]{1,0:T(8,128)(2,1)}, bf16[2048,2048]{1,0:T(8,128)(2,1)}, bf16[4,512,256]{2,1,0:T(8,128)(2,1)}, bf16[2048,1024]{1,0:T(8,128)(2,1)}, bf16[256,128]{1,0:T(8,128)(2,1)}) custom-call(bf16[256,2048]{1,0:T(8,128)(2,1)} %tok_ref.1, bf16[256,2048]{1,0:T(8,128)(2,1)} %cot_ref.1, bf16[3,128,1024]{2,1,0:T(8,128)(2,1)} %in_ref.1, ...), custom_call_target="tpu_custom_call" | custom-call | tf_op jit(solution)/shard_map/pallas_call | solution.py:401
  103.4 5.6 collective-permute-start
  113.0 11.1 %shard_map.212 = bf16[2048,2048]{1,0:T(8,128)(2,1)} custom-call(bf16[2048,2048]{1,0:T(8,128)(2,1)} %get-tuple-element.85.rows_ref, f32[1,2048]{1,0:T(1,128)} %bitcast.267, f32[1,2048]{1,0:T(1,128)} %bitcast.266), custom_call_target="tpu_custom_call" | custom-call | flops 33554432 | bytes 16777216 | tf_op jit(solution)/shard_map/pallas_call | solution.py:517
  124.0 18.8 %fusion.8 = (bf16[2048,1024]{1,0:T(8,128)(2,1)}, bf16[2048,1024]{1,0:T(8,128)(2,1)}) fusion(f32[1024]{0:T(1024)S(1)} %bitcast.274, bf16[2048,2048]{1,0:T(8,128)(2,1)} %shard_map.212, bf16[2048,1024]{1,0:T(8,128)(2,1)} %get-tuple-element.90), kind=kOutput, calls=%fused_computation.10 | convolution fusion | flops 8631877632 | bytes 20975616 | tf_op jit(solution)/shard_map/dot_general | solution.py:740
  142.8 12.7 %convolution_convert_fusion.1 = bf16[2048,1024]{1,0:T(8,128)(2,1)S(1)} fusion(bf16[2048,2048]{1,0:T(8,128)(2,1)} %get-tuple-element.113, bf16[2048,1024]{1,0:T(8,128)(2,1)} %get-tuple-element.91), kind=kOutput, calls=%fused_computation.32 | convolution fusion | flops 8592031744 | bytes 16777216 | tf_op jit(solution)/shard_map/sd,sf->df/dot_general | solution.py:744
  155.5 2.2 collective-permute-start.2
  163.6 21.7 %collective-permute-start.9 = (bf16[512,1024]{1,0:T(8,128)(2,1)}, bf16[512,1024]{1,0:T(8,128)(2,1)}, u32[]{:S(2)}, u32[]{:S(2)}) collective-permute-start(bf16[512,1024]{1,0:T(8,128)(2,1)} %get-tuple-element.187), channel_id=1, source_target_pairs={{0,8},{2,10},{4,12},{6,14},{1,9},{3,11},{5,13},{7,15}} | collective-permute-start | bytes 3145736 | tf_op jit(solution)/shard_map/ppermute | solution.py:650
  186.4 3.1 collective-permute-done.3
  192.3 4.7 constant_dynamic-slice_fusion.14
  198.5 8.8 %collective-permute-done.9 = bf16[512,1024]{1,0:T(8,128)(2,1)} collective-permute-done((bf16[512,1024]{1,0:T(8,128)(2,1)}, bf16[512,1024]{1,0:T(8,128)(2,1)}, u32[]{:S(2)}, u32[]{:S(2)}) %collective-permute-start.9) | collective-permute-done | bytes 1048608 | tf_op jit(solution)/shard_map/ppermute | solution.py:650
  207.3 4.0 add_convert_fusion.17
  213.0 5.3 collective-permute-start.11
  219.6 5.5 collective-permute-start.13
  225.1 2.4 select_select_fusion.7
  227.9 8.6 %add_bitcast_fusion.pre_ref = f32[3,2048,256]{2,1,0:T(8,128)} fusion(bf16[2048,2048]{1,0:T(8,128)(2,1)S(1)} %bitcast.236, f32[3,256]{1,0:T(4,128)S(1)} %add.384, bf16[4,2048,256]{2,1,0:T(8,128)(2,1)S(1)} %pad_maximum_fusion), kind=kOutput, calls=%fused_computation.28 | convolution fusion | flops 6444023808 | bytes 17829888 | tf_op jit(solution)/shard_map/sd,kde->kse/dot_general | solution.py:762
  236.6 3.4 convolution_convert_fusion.3.dout_ref
  240.0 4.7 collective-permute-done.14
  244.7 17.0 %collective-permute-done.13 = bf16[512,1024]{1,0:T(8,128)(2,1)} collective-permute-done((bf16[512,1024]{1,0:T(8,128)(2,1)S(1)}, bf16[512,1024]{1,0:T(8,128)(2,1)}, u32[]{:S(2)}, u32[]{:S(2)}) %collective-permute-start.13) | collective-permute-done | bytes 1048608 | tf_op jit(solution)/shard_map/ppermute | solution.py:596
  267.2 3.2 add_convert_fusion.15
  271.6 9.6 %collective-permute-start.21 = (bf16[512,1024]{1,0:T(8,128)(2,1)S(1)}, bf16[512,1024]{1,0:T(8,128)(2,1)S(1)}, u32[]{:S(2)}, u32[]{:S(2)}) collective-permute-start(bf16[512,1024]{1,0:T(8,128)(2,1)S(1)} %get-tuple-element.181), channel_id=1, source_target_pairs={{0,8},{2,10},{4,12},{6,14},{8,16},{10,18},{12,20},{14,22},{16,24},... | collective-permute-start | bytes 3145736 | tf_op jit(solution)/shard_map/ppermute | solution.py:650
  281.3 2.8 copy-done.1
  285.3 24.3 %shard_map.213 = (bf16[2048,256]{1,0:T(8,128)(2,1)S(1)}, bf16[3,2048,256]{2,1,0:T(8,128)(2,1)S(1)}) custom-call(f32[3,2048,256]{2,1,0:T(8,128)S(1)} %copy-done.1, f32[3,512,256]{2,1,0:T(8,128)S(1)} %copy-done, bf16[2048,256]{1,0:T(8,128)(2,1)S(1)} %copy-done.2), custom_call_target="tpu_custom_call" | custom-call | flops 3758096384 | bytes 12582912 | tf_op jit(solution)/shard_map/pallas_call | solution.py:123
  312.3 6.6 %convolution_convert_fusion.2 = bf16[2048,256]{1,0:T(8,128)(2,1)S(1)} fusion(bf16[2048,2048]{1,0:T(8,128)(2,1)} %get-tuple-element.113, bf16[2048,256]{1,0:T(8,128)(2,1)S(1)} %get-tuple-element.109), kind=kOutput, calls=%fused_computation.39 | convolution fusion | flops 2148007936 | bytes 10485760 | tf_op jit(solution)/shard_map/sd,se->de/dot_general | solution.py:778
  320.5 8.3 %fusion.17 = bf16[3,256,2048]{2,1,0:T(8,128)(2,1)} fusion(bf16[3,2048,256]{2,1,0:T(8,128)(2,1)S(1)} %get-tuple-element.110, bf16[2048,2048]{1,0:T(8,128)(2,1)S(1)} %bitcast.238), kind=kOutput, calls=%fused_computation.33 | convolution fusion | flops 6444023808 | bytes 14680064 | tf_op jit(solution)/shard_map/sd,kse->kde/dot_general | solution.py:782
  334.3 4.7 dynamic-slice_bitcast_fusion.7
  340.1 5.3 collective-permute-start.17
  346.5 2.0 collective-permute-start.18
  348.5 3.7 select_select_fusion.3
  352.2 13.4 %convert_reduce_fusion = (f32[1024]{0:T(1024)S(1)}, bf16[2048,1024]{1,0:T(8,128)(2,1)S(1)}) fusion(bf16[2048,1024]{1,0:T(8,128)(2,1)} %get-tuple-element.121, bf16[2048,2048]{1,0:T(8,128)(2,1)} %get-tuple-element.113, bf16[512,1024]{1,0:T(8,128)(2,1)} %get-tuple-element.201, bf16[512,1024]{1,0:T(8,128)(2,1)S(1)} %get-tuple-element.200, ...), kind=kOutput, calls=%fused_computation.19 | convolution fusion | flops 8617196544 | bytes 20975616 | tf_op jit(solution)/shard_map/dot_general | solution.py:794
  366.7 10.9 %convolution_convert_fusion = bf16[2048,1024]{1,0:T(8,128)(2,1)} fusion(bf16[2048,2048]{1,0:T(8,128)(2,1)S(1)} %bitcast.240, bf16[2048,1024]{1,0:T(8,128)(2,1)S(1)} %get-tuple-element.268), kind=kOutput, calls=%fused_computation.31 | convolution fusion | flops 8592031744 | bytes 16777216 | tf_op jit(solution)/shard_map/sd,sf->df/dot_general | solution.py:798
  377.6 6.3 fusion.58
  384.0 3.3 add_convert_fusion.3
  392.0 2.0 add_convert_fusion.4
  398.1 2.6 add_convert_fusion.13
  402.4 2.6 add_convert_fusion.14
  405.0 4.6 collective-permute-start.24
  409.6 4.5 fusion.57
  417.4 14.4 %collective-permute-done.24 = bf16[4,512,256]{1,2,0:T(8,128)(2,1)} collective-permute-done((bf16[4,512,256]{1,2,0:T(8,128)(2,1)}, bf16[4,512,256]{1,2,0:T(8,128)(2,1)}, u32[]{:S(2)}, u32[]{:S(2)}) %collective-permute-start.24) | collective-permute-done | bytes 1048608 | tf_op jit(solution)/shard_map/ppermute | solution.py:650
  431.8 6.2 add_convert_fusion.1
  437.9 4.6 fusion.61
  442.6 5.2 fusion.10
  453.1 6.0 collective-permute-start.29
  459.1 2.1 fusion.38
  465.6 4.6 collective-permute-start.34
  472.5 9.9 %collective-permute-done.29 = bf16[512,1024]{1,0:T(8,128)(2,1)S(1)} collective-permute-done((bf16[512,1024]{1,0:T(8,128)(2,1)S(1)}, bf16[512,1024]{1,0:T(8,128)(2,1)S(1)}, u32[]{:S(2)}, u32[]{:S(2)}) %collective-permute-start.29) | collective-permute-done | bytes 1048608 | tf_op jit(solution)/shard_map/ppermute | solution.py:650
  482.5 2.3 add_convert_fusion.11
  486.6 6.9 %fusion.62 = f32[1024,2048]{1,0:T(8,128)} fusion(bf16[1024,1024]{1,0:T(8,128)(2,1)S(1)} %bitcast.255, bf16[2048,1024]{1,0:T(8,128)(2,1)S(1)} %copy-done.75), kind=kOutput, calls=%fused_computation.209 | convolution fusion | flops 4294967296 | bytes 14680064 | tf_op jit(solution)/shard_map/dot_general | solution.py:816
  493.5 7.3 %fusion.9 = bf16[1024,2048]{1,0:T(8,128)(2,1)} fusion(f32[1024,2048]{1,0:T(8,128)} %fusion.62, bf16[3,1024,256]{2,1,0:T(8,128)(2,1)S(1)} %copy-done.35, bf16[4,2048,256]{2,1,0:T(8,128)(2,1)S(1)} %copy-done.18), kind=kOutput, calls=%fused_computation.12 | convolution fusion | flops 3225419776 | bytes 17301504 | tf_op jit(solution)/shard_map/kse,kde->sd/dot_general | solution.py:817
  500.9 5.2 collective-permute-start.31
  507.3 3.3 constant_dynamic-slice_fusion.1
  515.6 5.4 add_convert_fusion
  521.0 2.0 collective-permute-start.40
  524.8 5.4 collective-permute-done.40
  532.3 2.1 collective-permute-start.38
  540.3 12.5 %collective-permute-done.27 = bf16[256,2048]{1,0:T(8,128)(2,1)} collective-permute-done((bf16[256,2048]{1,0:T(8,128)(2,1)}, bf16[256,2048]{1,0:T(8,128)(2,1)}, u32[]{:S(2)}, u32[]{:S(2)}) %collective-permute-start.27) | collective-permute-done | bytes 1048608 | tf_op jit(solution)/shard_map/ppermute | solution.py:701
  552.8 26.1 %collective-permute-done.26 = bf16[256,2048]{1,0:T(8,128)(2,1)} collective-permute-done((bf16[256,2048]{1,0:T(8,128)(2,1)S(1)}, bf16[256,2048]{1,0:T(8,128)(2,1)}, u32[]{:S(2)}, u32[]{:S(2)}) %collective-permute-start.26) | collective-permute-done | bytes 1048608 | tf_op jit(solution)/shard_map/ppermute | solution.py:701
  578.9 2.5 add_convert_fusion.6
  582.9 7.3 %collective-permute-start.42 = (bf16[512,1024]{1,0:T(8,128)(2,1)S(1)}, bf16[512,1024]{1,0:T(8,128)(2,1)S(1)}, u32[]{:S(2)}, u32[]{:S(2)}) collective-permute-start(bf16[512,1024]{1,0:T(8,128)(2,1)S(1)} %get-tuple-element.166), channel_id=1, source_target_pairs={{0,8},{2,10},{4,12},{6,14},{8,16},{10,18},{12,20},{14,22},{16,24},... | collective-permute-start | bytes 3145736 | tf_op jit(solution)/shard_map/ppermute | solution.py:650
  590.2 9.5 %collective-permute-done.36 = bf16[256,2048]{1,0:T(8,128)(2,1)} collective-permute-done((bf16[256,2048]{1,0:T(8,128)(2,1)}, bf16[256,2048]{1,0:T(8,128)(2,1)}, u32[]{:S(2)}, u32[]{:S(2)}) %collective-permute-start.36) | collective-permute-done | bytes 1048608 | tf_op jit(solution)/shard_map/ppermute | solution.py:701
  599.7 3.7 fusion.31
  603.4 4.9 convert_reduce_fusion.3
  610.2 2.0 collective-permute-start.44
  612.9 17.9 %shard_map.214 = f32[8,128]{1,0:T(8,128)} custom-call(f32[4,4,8,128]{3,2,1,0:T(8,128)} %reshape.202.vec_ref), custom_call_target="tpu_custom_call" | custom-call | tf_op jit(solution)/shard_map/pallas_call | solution.py:482
  (340 shorter events, 95.4 us)
Async XLA Ops:
  0.6 108.3 %copy-start.55 = (bf16[128,4096]{1,0:T(8,128)(2,1)S(1)}, bf16[128,4096]{1,0:T(8,128)(2,1)}, u32[]{:S(2)}) copy-start(bf16[128,4096]{1,0:T(8,128)(2,1)} %param.21) | copy-start | bytes 3145732
  102.0 53.6 %collective-permute-start.1 = (bf16[4,512,256]{2,1,0:T(8,128)(2,1)}, bf16[4,512,256]{2,1,0:T(8,128)(2,1)S(1)}, u32[]{:S(2)}, u32[]{:S(2)}) collective-permute-start(bf16[4,512,256]{2,1,0:T(8,128)(2,1)} %get-tuple-element.84), channel_id=1, source_target_pairs={{30,22},{28,20},{26,18},{24,16},{22,14},{20,12},{18,10},{16,8},{14... | collective-permute-start | bytes 3145736 | tf_op jit(solution)/shard_map/ppermute | solution.py:597
  103.4 52.1 %collective-permute-start = (bf16[4,512,256]{2,1,0:T(8,128)(2,1)}, bf16[4,512,256]{2,1,0:T(8,128)(2,1)}, u32[]{:S(2)}, u32[]{:S(2)}) collective-permute-start(bf16[4,512,256]{2,1,0:T(8,128)(2,1)} %get-tuple-element.84), channel_id=1, source_target_pairs={{0,8},{2,10},{4,12},{6,14},{8,16},{10,18},{12,20},{14,22},{16,24},... | collective-permute-start | bytes 3145736 | tf_op jit(solution)/shard_map/ppermute | solution.py:596
  111.0 78.5 %collective-permute-start.7 = (bf16[128,1024]{1,0:T(8,128)(2,1)}, bf16[128,1024]{1,0:T(8,128)(2,1)}, u32[]{:S(2)}, u32[]{:S(2)}) collective-permute-start(bf16[128,1024]{1,0:T(8,128)(2,1)} %get-tuple-element.251), channel_id=1, source_target_pairs={{0,4},{2,6},{4,0},{6,2},{8,12},{10,14},{12,8},{14,10},{16,20},{18,... | collective-permute-start | bytes 786440 | tf_op jit(solution)/shard_map/ppermute | solution.py:579
  112.1 78.2 %collective-permute-start.8 = (bf16[128,1024]{1,0:T(8,128)(2,1)}, bf16[128,1024]{1,0:T(8,128)(2,1)}, u32[]{:S(2)}, u32[]{:S(2)}) collective-permute-start(bf16[128,1024]{1,0:T(8,128)(2,1)} %get-tuple-element.252), channel_id=1, source_target_pairs={{0,6},{2,4},{4,2},{6,0},{8,14},{10,12},{12,10},{14,8},{16,22},{18,... | collective-permute-start | bytes 786440 | tf_op jit(solution)/shard_map/ppermute | solution.py:579
  155.5 8.1 %collective-permute-start.2 = (bf16[4,512,256]{2,1,0:T(8,128)(2,1)}, bf16[4,512,256]{2,1,0:T(8,128)(2,1)}, u32[]{:S(2)}, u32[]{:S(2)}) collective-permute-start(bf16[4,512,256]{2,1,0:T(8,128)(2,1)} %collective-permute-done), channel_id=1, source_target_pairs={{8,16},{10,18},{12,20},{14,22},{16,24},{18,26},{20,28},{22,30},{9,... | collective-permute-start | bytes 3145736 | tf_op jit(solution)/shard_map/ppermute | solution.py:596
  159.3 39.2 %collective-permute-start.10 = (bf16[512,1024]{1,0:T(8,128)(2,1)}, bf16[512,1024]{1,0:T(8,128)(2,1)}, u32[]{:S(2)}, u32[]{:S(2)}) collective-permute-start(bf16[512,1024]{1,0:T(8,128)(2,1)} %get-tuple-element.186), channel_id=1, source_target_pairs={{30,22},{28,20},{26,18},{24,16},{31,23},{29,21},{27,19},{25,17}} | collective-permute-start | bytes 3145736 | tf_op jit(solution)/shard_map/ppermute | solution.py:651
  161.1 28.3 %collective-permute-start.3 = (bf16[4,512,256]{2,1,0:T(8,128)(2,1)S(1)}, bf16[4,512,256]{2,1,0:T(8,128)(2,1)}, u32[]{:S(2)}, u32[]{:S(2)}) collective-permute-start(bf16[4,512,256]{2,1,0:T(8,128)(2,1)S(1)} %collective-permute-done.1), channel_id=1, source_target_pairs={{22,14},{20,12},{18,10},{16,8},{14,6},{12,4},{10,2},{8,0},{23,15},... | collective-permute-start | bytes 3145736 | tf_op jit(solution)/shard_map/ppermute | solution.py:597
  163.3 26.9 %copy-start.69 = (f32[256]{0:T(256)}, f32[256]{0:T(256)S(1)}, u32[]{:S(2)}) copy-start(f32[256]{0:T(256)S(1)} %broadcast_multiply_fusion.2) | copy-start | bytes 3076
  163.6 43.7 %collective-permute-start.9 = (bf16[512,1024]{1,0:T(8,128)(2,1)}, bf16[512,1024]{1,0:T(8,128)(2,1)}, u32[]{:S(2)}, u32[]{:S(2)}) collective-permute-start(bf16[512,1024]{1,0:T(8,128)(2,1)} %get-tuple-element.187), channel_id=1, source_target_pairs={{0,8},{2,10},{4,12},{6,14},{1,9},{3,11},{5,13},{7,15}} | collective-permute-start | bytes 3145736 | tf_op jit(solution)/shard_map/ppermute | solution.py:650
  189.4 7.6 %collective-permute-start.6 = (bf16[128,1024]{1,0:T(8,128)(2,1)}, bf16[128,1024]{1,0:T(8,128)(2,1)}, u32[]{:S(2)}, u32[]{:S(2)}) collective-permute-start(bf16[128,1024]{1,0:T(8,128)(2,1)} %get-tuple-element.253), channel_id=1, source_target_pairs={{0,2},{2,0},{4,6},{6,4},{8,10},{10,8},{12,14},{14,12},{16,18},{18,... | collective-permute-start | bytes 786440 | tf_op jit(solution)/shard_map/ppermute | solution.py:579
  189.5 28.8 %collective-permute-start.4 = (bf16[4,512,256]{2,1,0:T(8,128)(2,1)}, bf16[4,512,256]{2,1,0:T(8,128)(2,1)S(1)}, u32[]{:S(2)}, u32[]{:S(2)}) collective-permute-start(bf16[4,512,256]{2,1,0:T(8,128)(2,1)} %collective-permute-done.2), channel_id=1, source_target_pairs={{16,24},{18,26},{20,28},{22,30},{17,25},{19,27},{21,29},{23,31}} | collective-permute-start | bytes 3145736 | tf_op jit(solution)/shard_map/ppermute | solution.py:596
  190.2 28.0 %collective-permute-start.5 = (bf16[4,512,256]{2,1,0:T(8,128)(2,1)}, bf16[4,512,256]{2,1,0:T(8,128)(2,1)}, u32[]{:S(2)}, u32[]{:S(2)}) collective-permute-start(bf16[4,512,256]{2,1,0:T(8,128)(2,1)} %collective-permute-done.3), channel_id=1, source_target_pairs={{14,6},{12,4},{10,2},{8,0},{15,7},{13,5},{11,3},{9,1}} | collective-permute-start | bytes 3145736 | tf_op jit(solution)/shard_map/ppermute | solution.py:597
  198.4 26.7 %copy-start.37 = (bf16[4,512,256]{2,1,0:T(8,128)(2,1)S(1)}, bf16[4,512,256]{2,1,0:T(8,128)(2,1)}, u32[]{:S(2)}) copy-start(bf16[4,512,256]{2,1,0:T(8,128)(2,1)} %get-tuple-element.84) | copy-start | bytes 3145732
  198.5 29.0 %copy-start.14 = (bf16[512,1024]{1,0:T(8,128)(2,1)}, bf16[512,1024]{1,0:T(8,128)(2,1)S(1)}, u32[]{:S(2)}) copy-start(bf16[512,1024]{1,0:T(8,128)(2,1)S(1)} %pad_maximum_fusion.4) | copy-start | bytes 3145732
  211.3 55.8 %collective-permute-start.12 = (bf16[512,1024]{1,0:T(8,128)(2,1)}, bf16[512,1024]{1,0:T(8,128)(2,1)}, u32[]{:S(2)}, u32[]{:S(2)}) collective-permute-start(bf16[512,1024]{1,0:T(8,128)(2,1)} %get-tuple-element.184), channel_id=1, source_target_pairs={{30,22},{28,20},{26,18},{24,16},{22,14},{20,12},{18,10},{16,8},{31... | collective-permute-start | bytes 3145736 | tf_op jit(solution)/shard_map/ppermute | solution.py:651
  213.0 54.2 %collective-permute-start.11 = (bf16[512,1024]{1,0:T(8,128)(2,1)}, bf16[512,1024]{1,0:T(8,128)(2,1)}, u32[]{:S(2)}, u32[]{:S(2)}) collective-permute-start(bf16[512,1024]{1,0:T(8,128)(2,1)} %get-tuple-element.185), channel_id=1, source_target_pairs={{0,8},{2,10},{4,12},{6,14},{8,16},{10,18},{12,20},{14,22},{1,9},{3... | collective-permute-start | bytes 3145736 | tf_op jit(solution)/shard_map/ppermute | solution.py:650
  218.3 26.4 %collective-permute-start.14 = (bf16[512,1024]{1,0:T(8,128)(2,1)S(1)}, bf16[512,1024]{1,0:T(8,128)(2,1)}, u32[]{:S(2)}, u32[]{:S(2)}) collective-permute-start(bf16[512,1024]{1,0:T(8,128)(2,1)S(1)} %pad_maximum_fusion.4), channel_id=1, source_target_pairs={{30,22},{28,20},{26,18},{24,16},{22,14},{20,12},{18,10},{16,8},{14... | collective-permute-start | bytes 3145736 | tf_op jit(solution)/shard_map/ppermute | solution.py:597
  219.6 42.2 %collective-permute-start.13 = (bf16[512,1024]{1,0:T(8,128)(2,1)S(1)}, bf16[512,1024]{1,0:T(8,128)(2,1)}, u32[]{:S(2)}, u32[]{:S(2)}) collective-permute-start(bf16[512,1024]{1,0:T(8,128)(2,1)S(1)} %pad_maximum_fusion.4), channel_id=1, source_target_pairs={{0,8},{2,10},{4,12},{6,14},{8,16},{10,18},{12,20},{14,22},{16,24},... | collective-permute-start | bytes 3145736 | tf_op jit(solution)/shard_map/ppermute | solution.py:596
  240.0 26.5 %copy-start.72 = (f32[256]{0:T(256)S(1)}, f32[256]{0:T(256)}, u32[]{:S(2)}) copy-start(f32[256]{0:T(256)} %fusion.32) | copy-start | bytes 3076
  261.7 49.0 %collective-permute-start.15 = (bf16[512,1024]{1,0:T(8,128)(2,1)}, bf16[512,1024]{1,0:T(8,128)(2,1)}, u32[]{:S(2)}, u32[]{:S(2)}) collective-permute-start(bf16[512,1024]{1,0:T(8,128)(2,1)} %collective-permute-done.13), channel_id=1, source_target_pairs={{8,16},{10,18},{12,20},{14,22},{16,24},{18,26},{20,28},{22,30},{9,... | collective-permute-start | bytes 3145736 | tf_op jit(solution)/shard_map/ppermute | solution.py:596
  263.4 47.3 %collective-permute-start.16 = (bf16[512,1024]{1,0:T(8,128)(2,1)}, bf16[512,1024]{1,0:T(8,128)(2,1)}, u32[]{:S(2)}, u32[]{:S(2)}) collective-permute-start(bf16[512,1024]{1,0:T(8,128)(2,1)} %collective-permute-done.14), channel_id=1, source_target_pairs={{22,14},{20,12},{18,10},{16,8},{14,6},{12,4},{10,2},{8,0},{23,15},... | collective-permute-start | bytes 3145736 | tf_op jit(solution)/shard_map/ppermute | solution.py:597
  270.3 58.5 %collective-permute-start.22 = (bf16[512,1024]{1,0:T(8,128)(2,1)S(1)}, bf16[512,1024]{1,0:T(8,128)(2,1)S(1)}, u32[]{:S(2)}, u32[]{:S(2)}) collective-permute-start(bf16[512,1024]{1,0:T(8,128)(2,1)S(1)} %get-tuple-element.180), channel_id=1, source_target_pairs={{30,22},{28,20},{26,18},{24,16},{22,14},{20,12},{18,10},{16,8},{14... | collective-permute-start | bytes 3145736 | tf_op jit(solution)/shard_map/ppermute | solution.py:651
  271.6 57.2 %collective-permute-start.21 = (bf16[512,1024]{1,0:T(8,128)(2,1)S(1)}, bf16[512,1024]{1,0:T(8,128)(2,1)S(1)}, u32[]{:S(2)}, u32[]{:S(2)}) collective-permute-start(bf16[512,1024]{1,0:T(8,128)(2,1)S(1)} %get-tuple-element.181), channel_id=1, source_target_pairs={{0,8},{2,10},{4,12},{6,14},{8,16},{10,18},{12,20},{14,22},{16,24},... | collective-permute-start | bytes 3145736 | tf_op jit(solution)/shard_map/ppermute | solution.py:650
  310.7 37.8 %collective-permute-start.20 = (bf16[512,1024]{1,0:T(8,128)(2,1)}, bf16[512,1024]{1,0:T(8,128)(2,1)}, u32[]{:S(2)}, u32[]{:S(2)}) collective-permute-start(bf16[512,1024]{1,0:T(8,128)(2,1)} %collective-permute-done.16), channel_id=1, source_target_pairs={{14,6},{12,4},{10,2},{8,0},{15,7},{13,5},{11,3},{9,1}} | collective-permute-start | bytes 3145736 | tf_op jit(solution)/shard_map/ppermute | solution.py:597
  318.9 29.6 %collective-permute-start.19 = (bf16[512,1024]{1,0:T(8,128)(2,1)}, bf16[512,1024]{1,0:T(8,128)(2,1)}, u32[]{:S(2)}, u32[]{:S(2)}) collective-permute-start(bf16[512,1024]{1,0:T(8,128)(2,1)} %collective-permute-done.15), channel_id=1, source_target_pairs={{16,24},{18,26},{20,28},{22,30},{17,25},{19,27},{21,29},{23,31}} | collective-permute-start | bytes 3145736 | tf_op jit(solution)/shard_map/ppermute | solution.py:596
  340.1 25.5 %collective-permute-start.17 = (bf16[4,512,256]{1,2,0:T(8,128)(2,1)}, bf16[4,512,256]{1,2,0:T(8,128)(2,1)S(1)}, u32[]{:S(2)}, u32[]{:S(2)}) collective-permute-start(bf16[4,512,256]{1,2,0:T(8,128)(2,1)} %pad_maximum_fusion.5), channel_id=1, source_target_pairs={{0,8},{2,10},{4,12},{6,14},{1,9},{3,11},{5,13},{7,15}} | collective-permute-start | bytes 3145736 | tf_op jit(solution)/shard_map/ppermute | solution.py:650
  346.5 19.2 %collective-permute-start.18 = (bf16[4,512,256]{1,2,0:T(8,128)(2,1)}, bf16[4,512,256]{1,2,0:T(8,128)(2,1)}, u32[]{:S(2)}, u32[]{:S(2)}) collective-permute-start(bf16[4,512,256]{1,2,0:T(8,128)(2,1)} %pad_maximum_fusion.6), channel_id=1, source_target_pairs={{30,22},{28,20},{26,18},{24,16},{31,23},{29,21},{27,19},{25,17}} | collective-permute-start | bytes 3145736 | tf_op jit(solution)/shard_map/ppermute | solution.py:651
  352.2 25.4 %copy-start.44 = (bf16[512,1024]{1,0:T(8,128)(2,1)}, bf16[512,1024]{1,0:T(8,128)(2,1)S(1)}, u32[]{:S(2)}) copy-start(bf16[512,1024]{1,0:T(8,128)(2,1)S(1)} %get-tuple-element.198) | copy-start | bytes 3145732
  352.2 25.4 %copy-start.46 = (bf16[512,1024]{1,0:T(8,128)(2,1)}, bf16[512,1024]{1,0:T(8,128)(2,1)S(1)}, u32[]{:S(2)}) copy-start(bf16[512,1024]{1,0:T(8,128)(2,1)S(1)} %get-tuple-element.199) | copy-start | bytes 3145732
  387.3 44.4 %collective-permute-start.23 = (bf16[1024,2048]{1,0:T(8,128)(2,1)}, bf16[1024,2048]{1,0:T(8,128)(2,1)}, u32[]{:S(2)}, u32[]{:S(2)}) collective-permute-start(bf16[1024,2048]{1,0:T(8,128)(2,1)} %add_convert_fusion.3), channel_id=1, source_target_pairs={{0,2},{2,0},{4,6},{6,4},{8,10},{10,8},{12,14},{14,12},{16,18},{18,... | collective-permute-start | bytes 12582920 | tf_op jit(solution)/shard_map/ppermute | solution.py:687
  394.9 58.1 %collective-permute-start.48 = (bf16[128,1024]{1,0:T(8,128)(2,1)}, bf16[128,1024]{1,0:T(8,128)(2,1)}, u32[]{:S(2)}, u32[]{:S(2)}) collective-permute-start(bf16[128,1024]{1,0:T(8,128)(2,1)} %get-tuple-element.218), channel_id=1, source_target_pairs={{0,4},{2,6},{4,0},{6,2},{8,12},{10,14},{12,8},{14,10},{16,20},{18,... | collective-permute-start | bytes 786440 | tf_op jit(solution)/shard_map/ppermute | solution.py:579
  394.9 64.1 %collective-permute-start.49 = (bf16[128,1024]{1,0:T(8,128)(2,1)}, bf16[128,1024]{1,0:T(8,128)(2,1)}, u32[]{:S(2)}, u32[]{:S(2)}) collective-permute-start(bf16[128,1024]{1,0:T(8,128)(2,1)} %get-tuple-element.219), channel_id=1, source_target_pairs={{0,6},{2,4},{4,2},{6,0},{8,14},{10,12},{12,10},{14,8},{16,22},{18,... | collective-permute-start | bytes 786440 | tf_op jit(solution)/shard_map/ppermute | solution.py:579
  400.7 16.5 %collective-permute-start.25 = (bf16[4,512,256]{1,2,0:T(8,128)(2,1)}, bf16[4,512,256]{1,2,0:T(8,128)(2,1)}, u32[]{:S(2)}, u32[]{:S(2)}) collective-permute-start(bf16[4,512,256]{1,2,0:T(8,128)(2,1)} %add_convert_fusion.13), channel_id=1, source_target_pairs={{30,22},{28,20},{26,18},{24,16},{22,14},{20,12},{18,10},{16,8},{31... | collective-permute-start | bytes 3145736 | tf_op jit(solution)/shard_map/ppermute | solution.py:651
  405.0 26.8 %collective-permute-start.24 = (bf16[4,512,256]{1,2,0:T(8,128)(2,1)}, bf16[4,512,256]{1,2,0:T(8,128)(2,1)}, u32[]{:S(2)}, u32[]{:S(2)}) collective-permute-start(bf16[4,512,256]{1,2,0:T(8,128)(2,1)} %add_convert_fusion.14), channel_id=1, source_target_pairs={{0,8},{2,10},{4,12},{6,14},{8,16},{10,18},{12,20},{14,22},{1,9},{3... | collective-permute-start | bytes 3145736 | tf_op jit(solution)/shard_map/ppermute | solution.py:650
  417.3 41.8 %collective-permute-start.47 = (bf16[128,1024]{1,0:T(8,128)(2,1)}, bf16[128,1024]{1,0:T(8,128)(2,1)}, u32[]{:S(2)}, u32[]{:S(2)}) collective-permute-start(bf16[128,1024]{1,0:T(8,128)(2,1)} %get-tuple-element.220), channel_id=1, source_target_pairs={{0,2},{2,0},{4,6},{6,4},{8,10},{10,8},{12,14},{14,12},{16,18},{18,... | collective-permute-start | bytes 786440 | tf_op jit(solution)/shard_map/ppermute | solution.py:579
  447.8 67.5 %collective-permute-start.33 = (bf16[1024,2048]{1,0:T(8,128)(2,1)}, bf16[1024,2048]{1,0:T(8,128)(2,1)}, u32[]{:S(2)}, u32[]{:S(2)}) collective-permute-start(bf16[1024,2048]{1,0:T(8,128)(2,1)} %fusion.10), channel_id=1, source_target_pairs={{0,2},{2,0},{4,6},{6,4},{8,10},{10,8},{12,14},{14,12},{16,18},{18,... | collective-permute-start | bytes 12582920 | tf_op jit(solution)/shard_map/ppermute | solution.py:687
  452.3 19.8 %collective-permute-start.30 = (bf16[512,1024]{1,0:T(8,128)(2,1)S(1)}, bf16[512,1024]{1,0:T(8,128)(2,1)S(1)}, u32[]{:S(2)}, u32[]{:S(2)}) collective-permute-start(bf16[512,1024]{1,0:T(8,128)(2,1)S(1)} %get-tuple-element.174), channel_id=1, source_target_pairs={{30,22},{28,20},{26,18},{24,16},{31,23},{29,21},{27,19},{25,17}} | collective-permute-start | bytes 3145736 | tf_op jit(solution)/shard_map/ppermute | solution.py:651
  453.1 29.4 %collective-permute-start.29 = (bf16[512,1024]{1,0:T(8,128)(2,1)S(1)}, bf16[512,1024]{1,0:T(8,128)(2,1)S(1)}, u32[]{:S(2)}, u32[]{:S(2)}) collective-permute-start(bf16[512,1024]{1,0:T(8,128)(2,1)S(1)} %get-tuple-element.175), channel_id=1, source_target_pairs={{0,8},{2,10},{4,12},{6,14},{1,9},{3,11},{5,13},{7,15}} | collective-permute-start | bytes 3145736 | tf_op jit(solution)/shard_map/ppermute | solution.py:650
  462.7 38.1 %collective-permute-start.35 = (bf16[4,512,256]{1,2,0:T(8,128)(2,1)S(1)}, bf16[4,512,256]{1,2,0:T(8,128)(2,1)S(1)}, u32[]{:S(2)}, u32[]{:S(2)}) collective-permute-start(bf16[4,512,256]{1,2,0:T(8,128)(2,1)S(1)} %add_convert_fusion.9), channel_id=1, source_target_pairs={{30,22},{28,20},{26,18},{24,16},{22,14},{20,12},{18,10},{16,8},{14... | collective-permute-start | bytes 3145736 | tf_op jit(solution)/shard_map/ppermute | solution.py:651
  465.6 40.5 %collective-permute-start.34 = (bf16[4,512,256]{1,2,0:T(8,128)(2,1)S(1)}, bf16[4,512,256]{1,2,0:T(8,128)(2,1)S(1)}, u32[]{:S(2)}, u32[]{:S(2)}) collective-permute-start(bf16[4,512,256]{1,2,0:T(8,128)(2,1)S(1)} %add_convert_fusion.10), channel_id=1, source_target_pairs={{0,8},{2,10},{4,12},{6,14},{8,16},{10,18},{12,20},{14,22},{16,24},... | collective-permute-start | bytes 3145736 | tf_op jit(solution)/shard_map/ppermute | solution.py:650
  472.1 59.0 %collective-permute-start.28 = (bf16[256,2048]{1,0:T(8,128)(2,1)}, bf16[256,2048]{1,0:T(8,128)(2,1)}, u32[]{:S(2)}, u32[]{:S(2)}) collective-permute-start(bf16[256,2048]{1,0:T(8,128)(2,1)} %get-tuple-element.176), channel_id=1, source_target_pairs={{0,5},{1,4},{2,7},{3,6},{4,1},{5,0},{6,3},{7,2},{8,13},{9,12},{10,... | collective-permute-start | bytes 3145736 | tf_op jit(solution)/shard_map/ppermute | solution.py:701
  484.8 47.5 %collective-permute-start.32 = (bf16[512,1024]{1,0:T(8,128)(2,1)}, bf16[512,1024]{1,0:T(8,128)(2,1)}, u32[]{:S(2)}, u32[]{:S(2)}) collective-permute-start(bf16[512,1024]{1,0:T(8,128)(2,1)} %get-tuple-element.172), channel_id=1, source_target_pairs={{30,22},{28,20},{26,18},{24,16},{22,14},{20,12},{18,10},{16,8},{31... | collective-permute-start | bytes 3145736 | tf_op jit(solution)/shard_map/ppermute | solution.py:651
  500.9 33.5 %collective-permute-start.31 = (bf16[512,1024]{1,0:T(8,128)(2,1)}, bf16[512,1024]{1,0:T(8,128)(2,1)}, u32[]{:S(2)}, u32[]{:S(2)}) collective-permute-start(bf16[512,1024]{1,0:T(8,128)(2,1)} %get-tuple-element.173), channel_id=1, source_target_pairs={{0,8},{2,10},{4,12},{6,14},{8,16},{10,18},{12,20},{14,22},{1,9},{3... | collective-permute-start | bytes 3145736 | tf_op jit(solution)/shard_map/ppermute | solution.py:650
  515.3 5.7 collective-permute-start.39
  515.3 9.4 %collective-permute-start.41 = (bf16[4,128,256]{2,1,0:T(8,128)(2,1)}, bf16[4,128,256]{2,1,0:T(8,128)(2,1)S(1)}, u32[]{:S(2)}, u32[]{:S(2)}) collective-permute-start(bf16[4,128,256]{2,1,0:T(8,128)(2,1)} %bitcast.77), channel_id=1, source_target_pairs={{0,6},{2,4},{4,2},{6,0},{8,14},{10,12},{12,10},{14,8},{16,22},{18,... | collective-permute-start | bytes 786440 | tf_op jit(solution)/shard_map/ppermute | solution.py:579
  521.0 9.2 %collective-permute-start.40 = (bf16[4,128,256]{2,1,0:T(8,128)(2,1)S(1)}, bf16[4,128,256]{2,1,0:T(8,128)(2,1)S(1)}, u32[]{:S(2)}, u32[]{:S(2)}) collective-permute-start(bf16[4,128,256]{2,1,0:T(8,128)(2,1)S(1)} %bitcast.263), channel_id=1, source_target_pairs={{0,4},{2,6},{4,0},{6,2},{8,12},{10,14},{12,8},{14,10},{16,20},{18,... | collective-permute-start | bytes 786440 | tf_op jit(solution)/shard_map/ppermute | solution.py:579
  524.7 28.1 %collective-permute-start.27 = (bf16[256,2048]{1,0:T(8,128)(2,1)}, bf16[256,2048]{1,0:T(8,128)(2,1)}, u32[]{:S(2)}, u32[]{:S(2)}) collective-permute-start(bf16[256,2048]{1,0:T(8,128)(2,1)} %get-tuple-element.177), channel_id=1, source_target_pairs={{0,4},{1,5},{2,6},{3,7},{4,0},{5,1},{6,2},{7,3},{8,12},{9,13},{10,... | collective-permute-start | bytes 3145736 | tf_op jit(solution)/shard_map/ppermute | solution.py:701
  530.2 48.7 %collective-permute-start.26 = (bf16[256,2048]{1,0:T(8,128)(2,1)S(1)}, bf16[256,2048]{1,0:T(8,128)(2,1)}, u32[]{:S(2)}, u32[]{:S(2)}) collective-permute-start(bf16[256,2048]{1,0:T(8,128)(2,1)S(1)} %copy-done.38), channel_id=1, source_target_pairs={{0,1},{1,0},{2,3},{3,2},{4,5},{5,4},{6,7},{7,6},{8,9},{9,8},{10,11... | collective-permute-start | bytes 3145736 | tf_op jit(solution)/shard_map/ppermute | solution.py:701
  531.1 68.6 %collective-permute-start.36 = (bf16[256,2048]{1,0:T(8,128)(2,1)}, bf16[256,2048]{1,0:T(8,128)(2,1)}, u32[]{:S(2)}, u32[]{:S(2)}) collective-permute-start(bf16[256,2048]{1,0:T(8,128)(2,1)} %get-tuple-element.167), channel_id=1, source_target_pairs={{0,1},{1,0},{2,3},{3,2},{4,5},{5,4},{6,7},{7,6},{8,9},{9,8},{10,11... | collective-permute-start | bytes 3145736 | tf_op jit(solution)/shard_map/ppermute | solution.py:701
  532.3 67.4 %collective-permute-start.38 = (bf16[256,2048]{1,0:T(8,128)(2,1)}, bf16[256,2048]{1,0:T(8,128)(2,1)}, u32[]{:S(2)}, u32[]{:S(2)}) collective-permute-start(bf16[256,2048]{1,0:T(8,128)(2,1)} %get-tuple-element.168), channel_id=1, source_target_pairs={{0,5},{1,4},{2,7},{3,6},{4,1},{5,0},{6,3},{7,2},{8,13},{9,12},{10,... | collective-permute-start | bytes 3145736 | tf_op jit(solution)/shard_map/ppermute | solution.py:701
  534.4 65.3 %collective-permute-start.37 = (bf16[256,2048]{1,0:T(8,128)(2,1)}, bf16[256,2048]{1,0:T(8,128)(2,1)}, u32[]{:S(2)}, u32[]{:S(2)}) collective-permute-start(bf16[256,2048]{1,0:T(8,128)(2,1)} %get-tuple-element.169), channel_id=1, source_target_pairs={{0,4},{1,5},{2,6},{3,7},{4,0},{5,1},{6,2},{7,3},{8,12},{9,13},{10,... | collective-permute-start | bytes 3145736 | tf_op jit(solution)/shard_map/ppermute | solution.py:701
  537.9 41.0 %copy-start.8 = (bf16[2048,1024]{1,0:T(8,128)(2,1)S(1)}, bf16[2048,1024]{1,0:T(8,128)(2,1)}, u32[]{:S(2)}) copy-start(bf16[2048,1024]{1,0:T(8,128)(2,1)} %convolution_convert_fusion) | copy-start | bytes 12582916
  539.4 60.3 %copy-start.4 = (bf16[256,2048]{1,0:T(8,128)(2,1)S(1)}, bf16[256,2048]{1,0:T(8,128)(2,1)}, u32[]{:S(2)}) copy-start(bf16[256,2048]{1,0:T(8,128)(2,1)} %tok_ref.1) | copy-start | bytes 3145732
  539.4 60.3 %copy-start.65 = (f32[2048]{0:T(1024)S(1)}, f32[2048]{0:T(1024)}, u32[]{:S(2)}) copy-start(f32[2048]{0:T(1024)} %get-tuple-element.254) | copy-start | bytes 24580
  539.4 60.3 %copy-start.70 = (f32[256]{0:T(256)S(1)}, f32[256]{0:T(256)}, u32[]{:S(2)}) copy-start(f32[256]{0:T(256)} %copy-done.69) | copy-start | bytes 3076
  539.4 60.3 %copy-start.71 = (f32[256]{0:T(256)S(1)}, f32[256]{0:T(256)}, u32[]{:S(2)}) copy-start(f32[256]{0:T(256)} %add_rsqrt_fusion) | copy-start | bytes 3076
  581.5 21.9 %copy-start.21 = (bf16[256,2048]{1,0:T(8,128)(2,1)S(1)}, bf16[256,2048]{1,0:T(8,128)(2,1)}, u32[]{:S(2)}) copy-start(bf16[256,2048]{1,0:T(8,128)(2,1)} %cot_ref.1) | copy-start | bytes 3145732
  581.5 21.9 %copy-start.67 = (f32[2048]{0:T(1024)S(1)}, f32[2048]{0:T(1024)}, u32[]{:S(2)}) copy-start(f32[2048]{0:T(1024)} %get-tuple-element.255) | copy-start | bytes 24580
  581.5 26.8 %collective-permute-start.43 = (bf16[512,1024]{1,0:T(8,128)(2,1)S(1)}, bf16[512,1024]{1,0:T(8,128)(2,1)S(1)}, u32[]{:S(2)}, u32[]{:S(2)}) collective-permute-start(bf16[512,1024]{1,0:T(8,128)(2,1)S(1)} %get-tuple-element.165), channel_id=1, source_target_pairs={{30,22},{28,20},{26,18},{24,16},{22,14},{20,12},{18,10},{16,8},{14... | collective-permute-start | bytes 3145736 | tf_op jit(solution)/shard_map/ppermute | solution.py:651
  582.9 26.4 %collective-permute-start.42 = (bf16[512,1024]{1,0:T(8,128)(2,1)S(1)}, bf16[512,1024]{1,0:T(8,128)(2,1)S(1)}, u32[]{:S(2)}, u32[]{:S(2)}) collective-permute-start(bf16[512,1024]{1,0:T(8,128)(2,1)S(1)} %get-tuple-element.166), channel_id=1, source_target_pairs={{0,8},{2,10},{4,12},{6,14},{8,16},{10,18},{12,20},{14,22},{16,24},... | collective-permute-start | bytes 3145736 | tf_op jit(solution)/shard_map/ppermute | solution.py:650
  610.0 24.7 %collective-permute-start.45 = (bf16[128,1024]{1,0:T(8,128)(2,1)S(1)}, bf16[128,1024]{1,0:T(8,128)(2,1)S(1)}, u32[]{:S(2)}, u32[]{:S(2)}) collective-permute-start(bf16[128,1024]{1,0:T(8,128)(2,1)S(1)} %get-tuple-element.221), channel_id=1, source_target_pairs={{0,4},{2,6},{4,0},{6,2},{8,12},{10,14},{12,8},{14,10},{16,20},{18,... | collective-permute-start | bytes 786440 | tf_op jit(solution)/shard_map/ppermute | solution.py:579
  610.1 24.7 %collective-permute-start.46 = (bf16[128,1024]{1,0:T(8,128)(2,1)S(1)}, bf16[128,1024]{1,0:T(8,128)(2,1)S(1)}, u32[]{:S(2)}, u32[]{:S(2)}) collective-permute-start(bf16[128,1024]{1,0:T(8,128)(2,1)S(1)} %get-tuple-element.222), channel_id=1, source_target_pairs={{0,6},{2,4},{4,2},{6,0},{8,14},{10,12},{12,10},{14,8},{16,22},{18,... | collective-permute-start | bytes 786440 | tf_op jit(solution)/shard_map/ppermute | solution.py:579
  610.2 24.6 %collective-permute-start.44 = (bf16[128,1024]{1,0:T(8,128)(2,1)S(1)}, bf16[128,1024]{1,0:T(8,128)(2,1)S(1)}, u32[]{:S(2)}, u32[]{:S(2)}) collective-permute-start(bf16[128,1024]{1,0:T(8,128)(2,1)S(1)} %get-tuple-element.223), channel_id=1, source_target_pairs={{0,2},{2,0},{4,6},{6,4},{8,10},{10,8},{12,14},{14,12},{16,18},{18,... | collective-permute-start | bytes 786440 | tf_op jit(solution)/shard_map/ppermute | solution.py:579
  (70 other events, 650.2 us)

commit v3 on v1

v3 whole, which is shorter than its diff:
```python
import functools
import math

import jax
import jax.numpy as jnp
import numpy as np
from jax import lax
from jax.experimental import pallas as pl
from jax.experimental.pallas import tpu as pltpu
from jax.sharding import PartitionSpec as P

HEAD = 64
ROT = 32
QUARTERS = 4
SMALL = 16
norm_eps = 1e-05
F32 = jnp.float32
BF16 = jnp.bfloat16


def normalize(rows):
    middle = jnp.mean(rows, axis=-1, keepdims=True)
    centered = rows - middle
    spread = jnp.mean(centered * centered, axis=-1, keepdims=True)
    inv_spread = lax.rsqrt(spread + norm_eps)
    return (centered * inv_spread, inv_spread)


def roll_lanes(v, by):
    wide = v.shape[1]
    return jnp.concatenate([v[:, wide - by :], v[:, : wide - by]], axis=1)


def attention_block(pre, table, douts):
    length, wide = douts.shape
    heads = wide // HEAD
    block = length // 2
    half_rot = ROT // 2
    scale = 1.0 / math.sqrt(HEAD)
    cosine, first, second = table

    def turn(v):
        return (
            v * cosine
            + roll_lanes(v, wide - half_rot) * first
            + roll_lanes(v, half_rot) * second
        )

    def turn_back(g):
        return (
            g * cosine
            + roll_lanes(g * first, half_rot)
            + roll_lanes(g * second, wide - half_rot)
        )

    queries = turn(pre[0]).astype(BF16)
    keys = turn(pre[1]).astype(BF16)
    values = pre[2].astype(BF16)
    head_of = lax.broadcasted_iota(jnp.int32, (block, wide), 1) // HEAD
    nothing = jnp.zeros((block, wide), BF16)
    mixed = [None, None]
    dq, dk, dv = [None, None], [None, None], [None, None]

    def dot(a, b, contract):
        return lax.dot_general(a, b, (contract, ((), ())), preferred_element_type=F32)

    def add(total, part):
        return part if total is None else total + part

    for head in range(heads):
        here = head_of == head

        def only(v):
            return jnp.where(here, v, nothing)

        q_here = [only(queries[i * block : (i + 1) * block]) for i in range(2)]
        k_here = [only(keys[i * block : (i + 1) * block]) for i in range(2)]
        v_here = [only(values[i * block : (i + 1) * block]) for i in range(2)]
        d_here = [only(douts[i * block : (i + 1) * block]) for i in range(2)]
        for i in range(2):
            seen = (i + 1) * block
            scores = dot(q_here[i], keys[:seen], ((1,), (1,))) * scale
            row = lax.broadcasted_iota(jnp.int32, (block, seen), 0) + i * block
            col = lax.broadcasted_iota(jnp.int32, (block, seen), 1)
            scores = jnp.where(col <= row, scores, -1e30)
            powers = jnp.exp(scores - jnp.max(scores, axis=1, keepdims=True))
            probs = powers * (1.0 / jnp.sum(powers, axis=1, keepdims=True))
            low = probs.astype(BF16)
            dprobs = dot(d_here[i], values[:seen], ((1,), (1,)))
            total = jnp.sum(probs * dprobs, axis=1, keepdims=True)
            dscores = (probs * (dprobs - total)).astype(BF16)
            for j in range(i + 1):
                part = slice(j * block, (j + 1) * block)
                mixed[i] = add(mixed[i], dot(low[:, part], v_here[j], ((1,), (0,))))
                dq[i] = add(dq[i], dot(dscores[:, part], k_here[j], ((1,), (0,))))
                dv[j] = add(dv[j], dot(low[:, part], d_here[i], ((0,), (0,))))
                dk[j] = add(dk[j], dot(dscores[:, part], q_here[i], ((0,), (0,))))
    value = jnp.concatenate(mixed, axis=0).astype(BF16)
    dq_low = (jnp.concatenate(dq, axis=0) * scale).astype(BF16)
    dk_low = (jnp.concatenate(dk, axis=0) * scale).astype(BF16)
    backs = (
        turn_back(dq_low.astype(F32)).astype(BF16),
        turn_back(dk_low.astype(F32)).astype(BF16),
        jnp.concatenate(dv, axis=0).astype(BF16),
    )
    return value, backs


def rotary_tables(length, heads):
    half_rot = ROT // 2
    freqs = np.exp(np.arange(half_rot) * (-math.log(10000.0) / half_rot))
    angles = np.arange(length)[:, None] * freqs[None, :]
    cosine, sine = np.cos(angles), np.sin(angles)
    rest = np.zeros((length, HEAD - ROT))
    none = np.zeros_like(sine)
    tables = np.stack(
        [
            np.concatenate([cosine, cosine, rest + 1.0], axis=1),
            np.concatenate([-sine, none, rest], axis=1),
            np.concatenate([none, sine, rest], axis=1),
        ]
    )
    return jnp.asarray(np.tile(tables, (1, 1, heads)), F32)


MESH = pl.DeviceIdType.MESH
VMEM_BYTES = 60 * 2**20


def layer_kernel(
    lines,
    tok_ref,
    cot_ref,
    in_ref,
    out_ref,
    up_ref,
    down_ref,
    small_ref,
    table_ref,
    seq_ref,
    dy_ref,
    heads_ref,
    up_full_ref,
    down_full_ref,
    smalls_ref,
    normed_ref,
    act_ref,
    slope_ref,
    mixed_ref,
    proj_ref,
    pre_ref,
    grads_ref,
    land_ref,
    stage_ref,
    total_ref,
    final_ref,
    half_ref,
    twin_ref,
    pair_ref,
    owner_ref,
    proj_sum_ref,
    pre_sum_ref,
    small_v,
    small_f,
    gain_v,
    shift_v,
    in_bias_v,
    up_bias_v,
    local_sem,
    swap_send,
    swap_recv,
    team_send,
    team_recv,
    line_send,
    line_recv,
    sum_send,
    sum_recv,
    final_send,
    final_recv,
    twin_send,
    twin_recv,
    owner_send,
    owner_recv,
):
    dp = lax.axis_index("dp")
    mp = lax.axis_index("mp")
    quarter = dp % QUARTERS
    line = dp // QUARTERS
    other = 1 - mp
    core = dp % 2
    rows, width = tok_ref.shape
    depth = out_ref.shape[0]
    chunk = QUARTERS * depth
    wide = out_ref.shape[1] // QUARTERS
    unit = up_ref.shape[1] // QUARTERS
    tall = small_ref.shape[0]
    length = table_ref.shape[1]
    count = seq_ref.shape[0]
    has_above = line < lines - 1
    has_below = line > 0
    across, aside, twin = (dp ^ 2, mp), (dp, other), (dp ^ 1, mp)

    barrier = pltpu.get_barrier_semaphore()
    for peer in (twin, across, (dp ^ 3, mp), aside, (dp ^ 2, other)):
        pl.semaphore_signal(barrier, inc=1, device_id=peer, device_id_type=MESH)

    @pl.when(has_above)
    def _():
        pl.semaphore_signal(barrier, inc=1, device_id=(dp + QUARTERS, mp), device_id_type=MESH)

    @pl.when(has_below)
    def _():
        pl.semaphore_signal(barrier, inc=1, device_id=(dp - QUARTERS, mp), device_id_type=MESH)

    pl.semaphore_wait(barrier, 5 + has_above.astype(jnp.int32) + has_below.astype(jnp.int32))

    pending = []

    def begin(*copies):
        for copy in copies:
            copy.start()
            pending.append(copy)

    def remote(src, dst, send, recv, peer):
        return pltpu.make_async_remote_copy(
            src_ref=src,
            dst_ref=dst,
            send_sem=send,
            recv_sem=recv,
            device_id=peer,
            device_id_type=MESH,
        )

    def columns(index, size):
        return pl.ds(pl.multiple_of(index * size, size), size)

    def weight_views(device, to):
        mine, part = columns(device, depth), columns(device, depth)
        views = [
            (small_ref, smalls_ref.at[columns(device, tall), :]),
            (up_ref.at[:, columns(to, unit)], up_full_ref.at[mine, :]),
        ]
        for k in range(3):
            views.append(
                (in_ref.at[k, :, columns(to, wide)], heads_ref.at[part, pl.ds(k * wide, wide)])
            )
        views.append((out_ref.at[:, columns(to, wide)], heads_ref.at[part, pl.ds(3 * wide, wide)]))
        views.append((down_ref.at[:, columns(to, unit)], down_full_ref.at[part, :]))
        return views

    def swap(kind, j, device):
        src, dst = weight_views(device, quarter ^ j)[kind]
        return remote(
            src, dst, swap_send.at[kind, j - 1], swap_recv.at[kind, j - 1], (dp ^ j, mp)
        )

    own = [
        pltpu.make_async_copy(src, dst, local_sem.at[kind])
        for kind, (src, dst) in enumerate(weight_views(dp, quarter))
    ]

    def begin_swap(*kinds):
        for kind in kinds:
            begin(*[swap(kind, j, dp) for j in (2, 3, 1)])
            own[kind].start()

    def end_swap(*kinds):
        for kind in kinds:
            own[kind].wait()
            for j in (1, 2, 3):
                swap(kind, j, dp ^ j).wait_recv()

    def line_view(kind, index):
        if kind == 0:
            return smalls_ref.at[columns(index, QUARTERS * tall), :]
        return (up_full_ref, heads_ref, down_full_ref)[kind - 1].at[columns(index, chunk), :]

    def line_copy(kind, way, step, index):
        view = line_view(kind, index)
        return remote(
            view,
            view,
            line_send.at[kind, way, step - 1],
            line_recv.at[kind, way, step - 1],
            (dp + (QUARTERS if way == 0 else -QUARTERS), mp),
        )

    def sends(way, step):
        if way == 0:
            return (line >= step - 1) & has_above, line - (step - 1)
        return (line <= lines - step) & has_below, line + (step - 1)

    def takes(way, step):
        if way == 0:
            return line >= step, line - step
        return line <= lines - 1 - step, line + step

    def start_line(step, *kinds):
        if step < lines:
            for kind in kinds:
                for way in (0, 1):
                    go, index = sends(way, step)

                    @pl.when(go)
                    def _():
                        line_copy(kind, way, step, index).start()

    def wait_line(step, *kinds):
        if step < lines:
            for kind in kinds:
                for way in (0, 1):
                    go, index = takes(way, step)

                    @pl.when(go)
                    def _():
                        line_copy(kind, way, step, index).wait_recv()

    def line_step(step, *kinds):
        wait_line(step, *kinds)
        start_line(step + 1, *kinds)

    def line_rest(step, *kinds):
        for later in range(step, lines):
            line_step(later, *kinds)

    rows_of = ((tok_ref, seq_ref), (cot_ref, dy_ref))

    def seat(device, half_of):
        return columns((device % QUARTERS) * 2 + half_of, rows)

    def part_seat(device, half_of, part):
        low = rows // 4 * 3
        start = ((device % QUARTERS) * 2 + half_of) * rows + part * low
        size = rows - low if part else low
        return pl.ds(pl.multiple_of(start, rows // 4), size)

    def relay(which, number, place, peer):
        view = rows_of[which][1].at[place, :]
        return remote(view, view, team_send.at[which, number], team_recv.at[which, number], peer)

    def offer(which, number, peer):
        src, dst = rows_of[which]
        return remote(
            src,
            dst.at[seat(dp, mp), :],
            team_send.at[which, number],
            team_recv.at[which, number],
            peer,
        )

    own_rows = [
        pltpu.make_async_copy(src, dst.at[seat(dp, mp), :], local_sem.at[7 + which])
        for which, (src, dst) in enumerate(rows_of)
    ]
    near, beside = seat(dp ^ 2, mp), seat(dp, other)

    def pass_on(which):
        relay(which, 0, near, across).wait_recv()
        begin(
            relay(which, 3, part_seat(dp ^ 2, mp, 0), aside),
            relay(which, 4, near, twin),
        )
        relay(which, 1, beside, aside).wait_recv()
        begin(
            relay(which, 5, part_seat(dp, other, 1), across),
            relay(which, 6, beside, twin),
        )

    def hand_over(which):
        for part, peer in ((0, aside), (1, across)):
            far = part_seat(dp ^ 2, other, part)
            relay(which, 3 + 2 * part, far, peer).wait_recv()
            begin(relay(which, 7 + part, far, twin))

    def all_rows(which):
        own_rows[which].wait()
        relay(which, 2, seat(dp ^ 1, mp), twin).wait_recv()
        relay(which, 4, seat(dp ^ 3, mp), twin).wait_recv()
        relay(which, 6, seat(dp ^ 1, other), twin).wait_recv()
        for part in (0, 1):
            relay(which, 7 + part, part_seat(dp ^ 3, other, part), twin).wait_recv()

    def dot(a, b, contract):
        return lax.dot_general(a, b, (contract, ((), ())), preferred_element_type=F32)

    nn, nt, tn = ((1,), (0,)), ((1,), (1,)), ((0,), (0,))
    tile = min(256, count)

    def pipeline(body, grid, in_specs, out_specs, *refs):
        pltpu.emit_pipeline(
            body, grid=grid, in_specs=in_specs, out_specs=out_specs, _explicit_indices=True
        )(*refs)

    def row_blocks(size, columns_, place=0):
        return pl.BlockSpec((size, columns_), lambda i: (i, place))

    def fixed(shape, *place):
        return pl.BlockSpec(shape, lambda i: place or (0,) * len(shape))

    def normalize_rows():
        def body(step, rows_in, rows_out):
            unit_rows = normalize(rows_in[...].astype(F32))[0]
            rows_out[...] = (unit_rows * gain_v[...] + shift_v[...]).astype(BF16)

        pipeline(
            body,
            (count // tile,),
            [row_blocks(tile, width)],
            [row_blocks(tile, width)],
            seq_ref,
            normed_ref,
        )

    def activate():
        def body(step, rows_in, weight, act, slope):
            u = dot(rows_in[...], weight[...], nn) + up_bias_v[...]
            value, derivative = smooth_gate(u)
            act[...] = value.astype(BF16)
            slope[...] = derivative.astype(BF16)

        pipeline(
            body,
            (count // tile,),
            [row_blocks(tile, width), fixed((width, unit))],
            [row_blocks(tile, unit), row_blocks(tile, unit)],
            normed_ref,
            up_full_ref,
            act_ref,
            slope_ref,
        )

    tall_tile = min(512, width)

    def weight_grad(left, right, right_wide, kind, start=0):
        def body(step, a, b, out):
            out[...] = dot(a[...], b[...], tn).astype(BF16)

        pipeline(
            body,
            (width // tall_tile,),
            [
                pl.BlockSpec((count, tall_tile), lambda i: (0, i)),
                fixed((count, right_wide)),
            ],
            [row_blocks(tall_tile, right_wide)],
            left,
            right,
            grads_ref.at[kind, :, pl.ds(start, right_wide)],
        )

    def attend(first, last):
        def shifted(columns_):
            return pl.BlockSpec((length, columns_), lambda i: (i + first, 0))

        def body(step, rows_in, dys, weight, mixed, proj):
            pre = dot(rows_in[...], weight[:, : 3 * wide], nn) + in_bias_v[...]
            douts = dot(dys[...], weight[:, 3 * wide :], nn).astype(BF16)
            value, backs = attention_block(
                [pre[:, k * wide : (k + 1) * wide] for k in range(3)],
                [table_ref[k] for k in range(3)],
                douts,
            )
            mixed[...] = value
            for k in range(3):
                proj[:, k * wide : (k + 1) * wide] = backs[k]
                part = jnp.sum(backs[k].astype(F32), axis=0, keepdims=True)
                place = slice(k * wide, (k + 1) * wide)

                proj_sum_ref[:, place] = proj_sum_ref[:, place] + part

        pipeline(
            body,
            (last - first,),
            [shifted(width), shifted(width), fixed((width, 4 * wide))],
            [shifted(wide), shifted(3 * wide)],
            normed_ref,
            dy_ref,
            heads_ref,
            mixed_ref,
            proj_ref,
        )

    def gate_back():
        def body(step, dys, weight, slope, pre):
            value = (dot(dys[...], weight[...], nn) * slope[...].astype(F32)).astype(BF16)
            pre[...] = value
            part = jnp.sum(value.astype(F32), axis=0, keepdims=True)

            @pl.when(step.index[0] == 0)
            def _():
                pre_sum_ref[...] = part

            @pl.when(step.index[0] > 0)
            def _():
                pre_sum_ref[...] = pre_sum_ref[...] + part

        pipeline(
            body,
            (count // tile,),
            [row_blocks(tile, width), fixed((width, unit)), row_blocks(tile, unit)],
            [row_blocks(tile, unit)],
            dy_ref,
            down_full_ref,
            slope_ref,
            pre_ref,
        )

    def back_to_rows(which, wide_rows, wide_weight, thin_rows, thin_wide, start, half_of, got):
        per = length // tile
        grid = (QUARTERS // 2 * per,)

        def rows_at(i):
            return ((i // per) * 2 + half_of) * per + i % per

        def body(step, a, weight, b, thin, *rest):
            sums = dot(a[...], weight[...], nt) + dot(b[...], thin[...], nt)
            if got:
                sums = sums + rest[0][...].astype(F32)
            rest[-1][...] = sums.astype(BF16)

        in_specs = [
            pl.BlockSpec((tile, unit), lambda i: (rows_at(i), 0)),
            fixed((width, unit)),
            pl.BlockSpec((tile, thin_wide), lambda i: (rows_at(i), 0)),
            fixed((width, thin_wide)),
        ]
        refs = [wide_rows, wide_weight, thin_rows, heads_ref.at[:, pl.ds(start, thin_wide)]]
        if got:
            in_specs.append(row_blocks(tile, width))
            refs.append(twin_ref.at[which])
        refs.append(pair_ref.at[which] if got else half_ref.at[which])
        pipeline(body, grid, in_specs, [row_blocks(tile, width)], *refs)

    def forward_rows(half_of, got):
        back_to_rows(0, act_ref, down_full_ref, mixed_ref, wide, 3 * wide, half_of, got)

    def backward_rows(half_of, got):
        back_to_rows(1, pre_ref, up_full_ref, proj_ref, 3 * wide, 0, half_of, got)

    def twin_copy(which):
        return remote(
            half_ref.at[which], twin_ref.at[which], twin_send.at[which], twin_recv.at[which], twin
        )

    def owner_copy(which, number, peer, place):
        return remote(
            pair_ref.at[which, columns(place, rows), :],
            owner_ref.at[which, number],
            owner_send.at[which, number],
            owner_recv.at[which, number],
            peer,
        )

    chip = (dp // 2) % (QUARTERS // 2)

    def to_owners(which):
        begin(
            owner_copy(which, 2, (dp ^ 2, other), (1 - chip) * 2 + other),
            owner_copy(which, 0, across, (1 - chip) * 2 + mp),
            owner_copy(which, 1, aside, chip * 2 + other),
        )

    add_tile = min(256, chunk)

    def add_chunks(dst, *parts):
        def body(step, *refs):
            *ins, out = refs
            out[...] = sum(ref[...].astype(F32) for ref in ins).astype(BF16)

        pipeline(
            body,
            (chunk // add_tile,),
            [row_blocks(add_tile, unit)] * len(parts),
            [row_blocks(add_tile, unit)],
            *parts,
            dst,
        )

    def sum_sends(way, step):
        far = lines - step
        if way == 0:
            return (line <= step - 1) & has_above, line + far, line == 0
        return (line >= lines - step) & has_below, line - far, line == lines - 1

    def sum_takes(way, step):
        if way == 0:
            return has_below & (line <= step)
        return has_above & (line >= lines - 1 - step)

    def sum_copy(kind, way, step, src):
        return remote(
            src,
            land_ref.at[kind, way, step - 1],
            sum_send.at[kind, way, step - 1],
            sum_recv.at[kind, way, step - 1],
            (dp + (QUARTERS if way == 0 else -QUARTERS), mp),
        )

    def sum_start(kind, step):
        if step < lines:
            for way in (0, 1):
                go, index, first = sum_sends(way, step)
                view = grads_ref.at[kind, columns(index, chunk), :]

                @pl.when(go & first)
                def _():
                    sum_copy(kind, way, step, view).start()

                if step > 1:

                    @pl.when(go & ~first)
                    def _():
                        staged = stage_ref.at[kind, way, step - 1]
                        add_chunks(staged, view, land_ref.at[kind, way, step - 2])
                        sum_copy(kind, way, step, staged).start()

    def sum_wait(kind, step):
        if step < lines:
            for way in (0, 1):

                @pl.when(sum_takes(way, step))
                def _():
                    sum_copy(kind, way, step, stage_ref.at[kind, way, step - 1]).wait_recv()

    def sum_step(kind, step):
        sum_wait(kind, step)
        sum_start(kind, step + 1)

    def final_copy(kind, j):
        return remote(
            total_ref.at[kind, columns(quarter ^ j, depth), :],
            final_ref.at[kind, quarter],
            final_send.at[kind, j - 1],
            final_recv.at[kind, j - 1],
            (dp ^ j, mp),
        )

    def final_in(kind, j):
        return remote(
            total_ref.at[kind, columns(quarter, depth), :],
            final_ref.at[kind, quarter ^ j],
            final_send.at[kind, j - 1],
            final_recv.at[kind, j - 1],
            (dp ^ j, mp),
        )

    def final_own(kind):
        return pltpu.make_async_copy(
            total_ref.at[kind, columns(quarter, depth), :],
            final_ref.at[kind, quarter],
            local_sem.at[10 + kind],
        )

    def sum_total(kind, step):
        for later in range(step, lines):
            sum_step(kind, later)
        view = grads_ref.at[kind, columns(line, chunk), :]
        below = land_ref.at[kind, 0, lines - 2]
        above = land_ref.at[kind, 1, lines - 2]

        @pl.when(has_below & has_above)
        def _():
            add_chunks(total_ref.at[kind], view, below, above)

        @pl.when(has_below & ~has_above)
        def _():
            add_chunks(total_ref.at[kind], view, below)

        @pl.when(has_above & ~has_below)
        def _():
            add_chunks(total_ref.at[kind], view, above)

        begin(*[final_copy(kind, j) for j in (2, 3, 1)])
        final_own(kind).start()

    begin_swap(0, 1)
    begin(offer(0, 1, aside), offer(0, 2, twin))
    own_rows[0].start()
    own_rows[1].start()
    end_swap(0, 1)
    start_line(1, 0, 1)
    begin(offer(0, 0, across), offer(1, 1, aside), offer(1, 2, twin))
    line_step(1, 0, 1)
    pass_on(0)
    begin_swap(2, 3, 4, 5)
    begin(offer(1, 0, across))
    hand_over(0)
    line_step(2, 0, 1)
    end_swap(2, 3, 4, 5)
    start_line(1, 2)
    all_rows(0)
    line_rest(3, 0)
    fetch = pltpu.make_async_copy(smalls_ref, small_v, local_sem.at[9])
    fetch.start()
    fetch.wait()
    small_f[...] = small_v[...].astype(F32)
    each = width // (lines * QUARTERS)
    for d in range(lines * QUARTERS):
        place = slice(d * each, (d + 1) * each)
        gain_v[:, place] = small_f[d * tall : d * tall + 1, :each]
        shift_v[:, place] = small_f[d * tall + 1 : d * tall + 2, :each]
    in_each = wide // lines
    up_each = unit // lines
    up_low = min(up_each, 128)
    for i in range(lines):
        top = pl.multiple_of((quarter * lines + i) * tall, tall)
        block = small_f[pl.ds(top, tall), :]
        for k in range(3):
            start = k * wide + i * in_each
            in_bias_v[:, start : start + in_each] = block[4 + k : 5 + k, :in_each]
        for r in range(up_each // up_low):
            start = i * up_each + r * up_low
            up_bias_v[:, start : start + up_low] = block[7 + r : 8 + r, :up_low]
    normalize_rows()
    pass_on(1)
    line_rest(3, 1)
    activate()
    hand_over(1)
    begin_swap(6)
    line_step(1, 2)
    all_rows(1)
    weight_grad(dy_ref, act_ref, unit, 0)
    sum_start(0, 1)
    line_step(2, 2)
    end_swap(6)
    sum_step(0, 1)
    line_rest(3, 2)
    start_line(1, 3)

    groups = count // length
    proj_sum_ref[...] = jnp.zeros_like(proj_sum_ref)
    attend(0, groups // 2)
    sum_step(0, 2)
    attend(groups // 2, groups)
    line_step(1, 3)
    weight_grad(dy_ref, mixed_ref, wide, 1, 3 * wide)
    line_step(2, 3)
    weight_grad(normed_ref, proj_ref, 3 * wide, 1, 0)
    sum_start(1, 1)
    sum_total(0, 3)
    sum_step(1, 1)
    line_rest(3, 3)
    gate_back()
    sum_step(1, 2)
    weight_grad(normed_ref, pre_ref, unit, 2)
    sum_start(2, 1)
    forward_rows(1 - core, False)
    begin(twin_copy(0))
    sum_step(2, 1)
    backward_rows(1 - core, False)
    begin(twin_copy(1))
    sum_total(1, 3)
    twin_copy(0).wait_recv()
    forward_rows(core, True)
    to_owners(0)
    sum_step(2, 2)
    twin_copy(1).wait_recv()
    backward_rows(core, True)
    to_owners(1)
    sum_total(2, 3)

    for which in (0, 1):
        for number, peer in ((0, across), (1, aside), (2, (dp ^ 2, other))):
            owner_copy(which, number, peer, 0).wait_recv()
    for kind in range(3):
        final_own(kind).wait()
        for j in (1, 2, 3):
            final_in(kind, j).wait_recv()
    for copy in pending:
        copy.wait_send()
    for step in range(1, lines):
        for way in (0, 1):
            go, index = sends(way, step)
            sent, which, first = sum_sends(way, step)

            @pl.when(go)
            def _():
                for kind in range(4):
                    line_copy(kind, way, step, index).wait_send()

            @pl.when(sent)
            def _():
                for kind in range(3):
                    sum_copy(kind, way, step, stage_ref.at[kind, way, step - 1]).wait_send()


def run_layer(lines, team, tokens, cotangent, in_weight, out_weight, up_weight, down_weight, small, table):
    rows, width = tokens.shape
    depth = out_weight.shape[0]
    wide = out_weight.shape[1] // QUARTERS
    unit = up_weight.shape[1] // QUARTERS
    chunk = QUARTERS * depth
    whole = lines * chunk
    count = team * rows
    smalls = lines * QUARTERS * small.shape[0]
    steps = max(lines - 1, 1)
    anywhere = pl.BlockSpec(memory_space=pl.ANY)
    inside = pl.BlockSpec(memory_space=pltpu.VMEM)

    def low(*shape):
        return jax.ShapeDtypeStruct(shape, BF16)

    outs = [
        low(count, width),
        low(count, width),
        low(whole, 4 * wide),
        low(whole, unit),
        low(whole, unit),
        low(smalls, 128),
        low(count, width),
        low(count, unit),
        low(count, unit),
        low(count, wide),
        low(count, 3 * wide),
        low(count, unit),
        low(3, width, unit),
        low(3, 2, steps, chunk, unit),
        low(3, 2, steps, chunk, unit),
        low(3, chunk, unit),
        low(3, QUARTERS, depth, unit),
        low(2, count // 2, width),
        low(2, count // 2, width),
        low(2, count // 2, width),
        low(2, 3, rows, width),
    ]
    sums = [
        jax.ShapeDtypeStruct((1, 3 * wide), F32),
        jax.ShapeDtypeStruct((1, unit), F32),
    ]
    dma = pltpu.SemaphoreType.DMA
    results = pl.pallas_call(
        functools.partial(layer_kernel, lines),
        out_shape=outs + sums,
        in_specs=[anywhere] * 7 + [inside],
        out_specs=[anywhere] * len(outs) + [inside] * 2,
        scratch_shapes=[
            pltpu.VMEM((smalls, 128), BF16),
            pltpu.VMEM((smalls, 128), F32),
            pltpu.VMEM((1, width), F32),
            pltpu.VMEM((1, width), F32),
            pltpu.VMEM((1, 3 * wide), F32),
            pltpu.VMEM((1, unit), F32),
            dma((13,)),
            dma((7, 3)),
            dma((7, 3)),
            dma((2, 9)),
            dma((2, 9)),
            dma((4, 2, steps)),
            dma((4, 2, steps)),
            dma((3, 2, steps)),
            dma((3, 2, steps)),
            dma((3, 3)),
            dma((3, 3)),
            dma((2,)),
            dma((2,)),
            dma((2, 3)),
            dma((2, 3)),
        ],
        compiler_params=pltpu.CompilerParams(
            collective_id=1, has_side_effects=True, vmem_limit_bytes=VMEM_BYTES
        ),
    )(tokens, cotangent, in_weight, out_weight, up_weight, down_weight, small, table)
    return results[5], results[16], results[19], results[20], results[21], results[22]


def small_kernel(lines, both, vec_ref, total_ref, land_a, part, land_b, land_c, send, recv):
    dp = lax.axis_index("dp")
    mp = lax.axis_index("mp")
    quarter = dp % QUARTERS
    line = dp // QUARTERS
    aside = (dp, 1 - mp)

    def in_line(k):
        return (lax.rem(line + k, lines) * QUARTERS + quarter, mp)

    barrier = pltpu.get_barrier_semaphore()
    peers = [(dp ^ j, mp) for j in (1, 2, 3)] + [in_line(k) for k in range(1, lines)] + [aside]
    for peer in peers:
        pl.semaphore_signal(barrier, inc=1, device_id=peer, device_id_type=MESH)
    pl.semaphore_wait(barrier, len(peers))

    def move(number, src, dst, peer):
        return pltpu.make_async_remote_copy(
            src_ref=src,
            dst_ref=dst,
            send_sem=send.at[number],
            recv_sem=recv.at[number],
            device_id=peer,
            device_id_type=MESH,
        )

    first = [
        move(j - 1, vec_ref.at[quarter ^ j], land_a.at[j - 1], (dp ^ j, mp)) for j in (1, 2, 3)
    ]
    for copy in first:
        copy.start()
    for copy in first:
        copy.wait()
    part[...] = (vec_ref[quarter] + land_a[0]) + (land_a[1] + land_a[2])
    second = [
        move(2 + k, part.at[lax.rem(line + k, lines)], land_b.at[k - 1], in_line(k))
        for k in range(1, lines)
    ]
    for copy in second:
        copy.start()
    total = part[line]
    for k, copy in enumerate(second):
        copy.wait()
        total = total + land_b[k]
    total_ref[...] = total
    third = move(2 + lines, total_ref, land_c, aside)
    third.start()
    third.wait()
    shape = total_ref.shape
    index = lax.broadcasted_iota(jnp.int32, shape, 0) * shape[1]
    index = index + lax.broadcasted_iota(jnp.int32, shape, 1)
    total_ref[...] = jnp.where(index < both, total + land_c[...], total)


def sum_small(lines, both, vector):
    tile = vector.shape[2:]
    count = lines + 3
    return pl.pallas_call(
        functools.partial(small_kernel, lines, both),
        out_shape=jax.ShapeDtypeStruct(tile, F32),
        in_specs=[pl.BlockSpec(memory_space=pltpu.VMEM)],
        out_specs=pl.BlockSpec(memory_space=pltpu.VMEM),
        scratch_shapes=[
            pltpu.VMEM((3, lines) + tile, F32),
            pltpu.VMEM((lines,) + tile, F32),
            pltpu.VMEM((max(lines - 1, 1),) + tile, F32),
            pltpu.VMEM(tile, F32),
            pltpu.SemaphoreType.DMA((count,)),
            pltpu.SemaphoreType.DMA((count,)),
        ],
        compiler_params=pltpu.CompilerParams(collective_id=2, has_side_effects=True),
    )(vector)


def smooth_gate(u):
    slope = math.sqrt(2.0 / math.pi)
    square = u * u
    curve = jnp.tanh(slope * (u + 0.044715 * (u * square)))
    rise = 0.5 * (1.0 + curve)
    bend = 0.5 * u * (1.0 - curve * curve) * (slope * (1.0 + 3.0 * 0.044715 * square))
    return u * rise, rise + bend


def per_device(
    tokens,
    norm_gain,
    norm_shift,
    in_weight,
    in_bias,
    out_weight,
    out_bias,
    up_weight,
    up_bias,
    down_weight,
    down_bias,
    cotangent,
):
    n_dp = lax.axis_size("dp")
    n_mp = lax.axis_size("mp")
    lines = n_dp // QUARTERS
    dp = lax.axis_index("dp")
    mp = lax.axis_index("mp")
    quarter = dp % QUARTERS
    chip = (dp // 2) % (QUARTERS // 2)
    own_rows, width = tokens.shape
    rows_here = in_weight.shape[1]
    each = norm_gain.shape[0]
    in_each = in_bias.shape[1]
    up_each = up_bias.shape[0]
    wide = out_weight.shape[1] // QUARTERS

    def row(vector):
        return jnp.pad(vector, (0, -vector.shape[0] % 128)).reshape(-1, 128)

    small = jnp.concatenate(
        [row(norm_gain), row(norm_shift), row(out_bias), row(down_bias)]
        + [row(in_bias[k]) for k in range(3)]
        + [row(up_bias)]
    )
    small = jnp.pad(small, ((0, SMALL - small.shape[0]), (0, 0)))
    table = rotary_tables(n_mp * own_rows, wide // HEAD)
    smalls, final, pair, owner, grad_in_bias, grad_up_bias = run_layer(
        lines, QUARTERS * n_mp, tokens, cotangent, in_weight, out_weight, up_weight, down_weight, small, table
    )
    smalls = smalls.reshape(n_dp, SMALL, 128)[:, :, :each].astype(F32)
    full_gain = smalls[:, 0].reshape(-1)
    full_out_bias = smalls[:, 2].reshape(-1)
    full_down_bias = smalls[:, 3].reshape(-1)

    def place(buffer, piece, index, axis):
        return lax.dynamic_update_index_in_dim(buffer, piece, index, axis)

    mine = lax.dynamic_slice_in_dim(pair, (chip * 2 + mp) * own_rows, own_rows, 1).astype(F32)
    sums = mine + owner[:, 0].astype(F32) + owner[:, 1].astype(F32) + owner[:, 2].astype(F32)
    summed, grad_own = sums[0], sums[1]
    outcome = (tokens.astype(F32) + summed + full_out_bias + full_down_bias).astype(BF16)
    final = final.astype(F32).transpose(0, 2, 1, 3)
    own_grad_down = final[0]
    own_grad_up = final[2]
    own_heads = final[1].reshape(rows_here, QUARTERS, 4, wide).transpose(2, 0, 1, 3)
    own_grad_in, own_grad_out = own_heads[:3], own_heads[3]
    own_unit, own_inv = normalize(tokens.astype(F32))
    gain_part = jnp.sum(grad_own * own_unit, axis=0)
    shift_part = jnp.sum(grad_own, axis=0)
    bias_part = jnp.sum(cotangent.astype(F32), axis=0)
    scaled = grad_own * full_gain
    centered_grad = (
        scaled
        - jnp.mean(scaled, axis=-1, keepdims=True)
        - own_unit * jnp.mean(scaled * own_unit, axis=-1, keepdims=True)
    )
    grad_input = cotangent.astype(F32) + own_inv * centered_grad

    wide = jnp.stack([gain_part, shift_part, bias_part])
    wide = wide.reshape(3, lines, QUARTERS, each).transpose(2, 1, 0, 3)
    wide = wide.reshape(QUARTERS, lines, 3 * each)
    in_blocks = grad_in_bias.reshape(3, lines, in_each).transpose(1, 0, 2).reshape(lines, -1)
    mine = jnp.concatenate([in_blocks, grad_up_bias.reshape(lines, up_each)], axis=1)
    spread = place(jnp.zeros((QUARTERS,) + mine.shape, F32), mine, quarter, 0)
    spread = spread.reshape(lines, QUARTERS, -1).transpose(1, 0, 2)
    vector = jnp.concatenate([wide, spread], axis=2)
    vector = jnp.pad(vector, ((0, 0), (0, 0), (0, 1024 - vector.shape[2])))
    owned = sum_small(lines, 3 * each, vector.reshape(QUARTERS, lines, 8, 128)).reshape(-1)
    own_gain = owned[:each]
    own_shift = owned[each : 2 * each]
    own_bias = owned[2 * each : 3 * each]
    own_in_bias = owned[3 * each : 3 * each + 3 * in_each].reshape(3, in_each)
    own_up_bias = owned[3 * each + 3 * in_each : 3 * each + 3 * in_each + up_each]

    return (
        outcome,
        grad_input,
        own_gain,
        own_shift,
        own_grad_in.reshape(in_weight.shape),
        own_in_bias,
        own_grad_out.reshape(out_weight.shape),
        own_bias,
        own_grad_up.reshape(up_weight.shape),
        own_up_bias,
        own_grad_down.reshape(down_weight.shape),
        own_bias,
    )


def solution(mesh):
    return jax.shard_map(
        per_device,
        mesh=mesh,
        in_specs=(
            P(("dp", "mp"), None),
            P("dp"),
            P("dp"),
            P(None, "dp", "mp"),
            P(None, ("mp", "dp")),
            P("dp", "mp"),
            P("dp"),
            P("dp", "mp"),
            P(("mp", "dp")),
            P("dp", "mp"),
            P("dp"),
            P(("dp", "mp"), None),
        ),
        out_specs=(
            P(("dp", "mp"), None),
            P(("dp", "mp"), None),
            P("dp"),
            P("dp"),
            P(None, "dp", "mp"),
            P(None, ("mp", "dp")),
            P("dp", "mp"),
            P("dp"),
            P("dp", "mp"),
            P(("mp", "dp")),
            P("dp", "mp"),
            P("dp"),
        ),
        check_vma=False,
    )
```

time: 922 us -> 543 us (0.59)
  Pallas kernels: 0 us -> 490 us
  waiting for transfers between devices: 235 us -> 0 us
  matrix products: 192 us -> 0 us
  blocking collectives: 156 us -> 0 us
  local copies, waits for them, and re-layouts: 167 us -> 28.4 us
  other arithmetic: 78.9 us -> 12.2 us
  starting transfers between devices: 63.3 us -> 0 us
  between operations: 16.7 us -> 1.36 us
    pallas_call x0 -> x2, Pallas kernels: none -> 490 us  [the longest x1 456 us: run_layer(): pl.pallas_call(functools.partial(layer_kernel, lines), out_shape=outs + s...]
    ppermute x56 -> x0, waiting for transfers between devices: 234 us -> none  [the longest x12 125 us: gather_lines(): downs.append(lax.ppermute(downs[-1], 'dp', down_pairs))]
    dot_general x17 -> x0, matrix products: 181 us -> none  [the longest x1 20.1 us: per_device(): grad_act = jnp.dot(grad_rows, full_down, preferred_element_type=F32)]
    unnamed x2 -> x0, blocking collectives: 148 us -> none
    ppermute x56 -> x0, starting transfers between devices: 63.1 us -> none  [the longest x12 24.7 us: gather_lines(): ups.append(lax.ppermute(ups[-1], 'dp', up_pairs))]
    unnamed x146 -> x20, local copies, waits for them, and re-layouts: 44.6 us -> 5.07 us
    dynamic_update_slice x30 -> x1, local copies, waits for them, and re-layouts: 34.3 us -> 0.07 us  [place(): return lax.dynamic_update_index_in_dim(buffer, piece, index, axis)]
    dynamic_slice x27 -> x0, local copies, waits for them, and re-layouts: 23.2 us -> none  [pick(): return lax.dynamic_index_in_dim(array, index, axis, keepdims=False)]
  transfers between devices with their start and end apart: 62 -> 0, of which waited for: 16 -> 0; matrix products, arithmetic and copies ran while one was open for 36% -> 0% of each run, Pallas kernels for 0% -> 0%
where the time goes in v3:
time: 543 us; the launch traced here: 532 us
  Pallas kernels  490 us (90%)
  local copies, waits for them, and re-layouts  28.4 us (5%)
  other arithmetic  12.2 us (2%)
    pallas_call x1, Pallas kernels, run_layer(): pl.pallas_call(functools.partial(layer_kernel, lines), out_shape=outs + s...  456 us
    pallas_call x1, Pallas kernels, sum_small(): pl.pallas_call(functools.partial(small_kernel, lines, both), out_shape=ja...  34.8 us

profile of v3, /device:TPU:0, one launch (start us, length us, event | category | flops | bytes accessed | tf_op | source)
XLA Modules:
  0.0 532.3 jit_solution(10623725726071731748)
XLA Ops:
  0.6 0.8 slice_bitcast_fusion.6
  1.5 1.5 concatenate.10
  3.0 0.6 pad.21.small_ref
  3.6 455.5 %shard_map.220 = (bf16[2048,2048]{1,0:T(8,128)(2,1)}, bf16[2048,2048]{1,0:T(8,128)(2,1)}, bf16[2048,1024]{1,0:T(8,128)(2,1)}, bf16[2048,1024]{1,0:T(8,128)(2,1)}...) custom-call(bf16[256,2048]{1,0:T(8,128)(2,1)} %tok_ref.1, ...), custom_call_target="tpu_custom_call" | custom-call | tf_op jit(solution)/shard_map/pallas_call | solution.py:831
  459.1 0.0 copy-start.1
  459.1 4.2 convert_add_fusion
  463.3 0.0 copy-done.1
  463.3 0.0 copy-start
  463.3 0.2 convert_reduce_fusion
  463.6 0.0 copy-start.2
  463.6 0.4 fusion.9
  464.0 1.6 fusion.15
  465.6 1.0 fusion.8
  466.6 0.0 copy-done
  466.6 0.0 copy-done.2
  466.6 0.0 copy-start.5
  466.6 0.0 copy-start.6
  466.7 0.0 copy-start.3
  466.7 3.2 convert_add_fusion.4
  469.8 0.5 broadcast.60
  470.4 0.0 copy-done.5
  470.4 0.7 reduce.5
  471.0 0.0 copy-done.6
  471.1 0.1 reshape.123
  471.1 0.1 reshape.124
  471.2 0.1 pad_maximum_fusion
  471.3 0.1 dynamic_update_slice.4
  471.4 1.7 slice_reduce_fusion
  473.2 0.7 reshape.126.vec_ref
  473.8 34.8 %shard_map.221 = f32[8,128]{1,0:T(8,128)} custom-call(f32[4,4,8,128]{3,2,1,0:T(8,128)} %reshape.126.vec_ref), custom_call_target="tpu_custom_call" | custom-call | tf_op jit(solution)/shard_map/pallas_call | solution.py:923
  508.6 1.3 slice_bitcast_fusion.3
  510.0 0.0 copy-start.7
  510.0 0.0 copy-done.3
  510.0 0.7 convert_bitcast_fusion
  510.7 2.9 fusion.14
  513.6 2.2 reshape_squeeze.12
  515.8 2.2 copy.34
  517.9 0.0 copy-start.4
  517.9 2.9 reshape.127
  520.9 0.0 copy-done.4
  520.9 0.1 slice.92
  520.9 0.6 slice.109
  521.5 0.5 slice.110
  522.1 0.3 copy.35
  522.4 0.9 copy.40
  523.3 1.9 copy.36
  525.2 1.8 copy.38
  527.0 0.6 slice.98
  527.6 1.9 copy.37
  529.6 1.8 copy.39
  531.4 0.0 copy-done.7
  531.4 0.5 copy.49
  (14 shorter events, 0.1 us)
Async XLA Ops:
  459.1 4.2 copy-start.1
  463.3 3.3 copy-start
  463.6 3.1 copy-start.2
  466.6 3.7 copy-start.5
  466.6 4.4 copy-start.6
  466.7 43.3 %copy-start.3 = (bf16[3,4,128,1024]{3,2,1,0:T(8,128)(2,1)S(1)}, bf16[3,4,128,1024]{3,2,1,0:T(8,128)(2,1)}, u32[]{:S(2)}) copy-start(bf16[3,4,128,1024]{3,2,1,0:T(8,128)(2,1)} %get-tuple-element.23) | copy-start | bytes 9437188
  510.0 21.4 %copy-start.7 = (f32[128]{0:T(128)}, f32[128]{0:T(128)S(1)}, u32[]{:S(2)}) copy-start(f32[128]{0:T(128)S(1)} %get-tuple-element.79) | copy-start | bytes 1540
  517.9 2.9 copy-start.4

commit v4 on v3

--- a/solution.py
+++ b/solution.py
@@ -27,8 +27,7 @@
 
 
 def roll_lanes(v, by):
-    wide = v.shape[1]
-    return jnp.concatenate([v[:, wide - by :], v[:, : wide - by]], axis=1)
+    return pltpu.roll(v, by, 1)
 
 
 def attention_block(pre, table, douts):
@@ -153,17 +152,32 @@
     land_ref,
     stage_ref,
     total_ref,
-    final_ref,
     half_ref,
     twin_ref,
     pair_ref,
     owner_ref,
+    result_ref,
+    grad_ref,
+    final_down_ref,
+    final_up_ref,
+    final_in_ref,
+    final_out_ref,
+    own_small_ref,
     proj_sum_ref,
     pre_sum_ref,
+    gain_sum,
+    shift_sum,
+    dy_sum,
+    vector,
+    vector_land,
+    part,
+    part_land,
+    aside_land,
     small_v,
     small_f,
     gain_v,
     shift_v,
+    out_bias_v,
     in_bias_v,
     up_bias_v,
     local_sem,
@@ -181,6 +195,8 @@
     twin_recv,
     owner_send,
     owner_recv,
+    small_send,
+    small_recv,
 ):
     dp = lax.axis_index("dp")
     mp = lax.axis_index("mp")
@@ -196,30 +212,34 @@
     tall = small_ref.shape[0]
     length = table_ref.shape[1]
     count = seq_ref.shape[0]
+    each = width // (lines * QUARTERS)
+    in_each = wide // lines
+    up_each = unit // lines
+    up_low = min(up_each, 128)
     has_above = line < lines - 1
     has_below = line > 0
     across, aside, twin = (dp ^ 2, mp), (dp, other), (dp ^ 1, mp)
 
     barrier = pltpu.get_barrier_semaphore()
-    for peer in (twin, across, (dp ^ 3, mp), aside, (dp ^ 2, other)):
+    def in_line(k):
+        return (lax.rem(line + k, lines) * QUARTERS + quarter, mp)
+
+    peers = [twin, across, (dp ^ 3, mp), aside, (dp ^ 2, other)]
+    peers += [in_line(k) for k in range(1, lines)]
+    for peer in peers:
         pl.semaphore_signal(barrier, inc=1, device_id=peer, device_id_type=MESH)
-
-    @pl.when(has_above)
-    def _():
-        pl.semaphore_signal(barrier, inc=1, device_id=(dp + QUARTERS, mp), device_id_type=MESH)
-
-    @pl.when(has_below)
-    def _():
-        pl.semaphore_signal(barrier, inc=1, device_id=(dp - QUARTERS, mp), device_id_type=MESH)
-
-    pl.semaphore_wait(barrier, 5 + has_above.astype(jnp.int32) + has_below.astype(jnp.int32))
+    pl.semaphore_wait(barrier, len(peers))
 
     pending = []
+    expected = {}
 
     def begin(*copies):
         for copy in copies:
             copy.start()
-            pending.append(copy)
+            pending.append(copy.wait_send)
+
+    def arrive(*key):
+        expected.pop(key)()
 
     def remote(src, dst, send, recv, peer):
         return pltpu.make_async_remote_copy(
@@ -264,11 +284,16 @@
             begin(*[swap(kind, j, dp) for j in (2, 3, 1)])
             own[kind].start()
 
+            def wait(kind=kind):
+                own[kind].wait()
+                for j in (1, 2, 3):
+                    swap(kind, j, dp ^ j).wait_recv()
+
+            expected["swap", kind] = wait
+
     def end_swap(*kinds):
         for kind in kinds:
-            own[kind].wait()
-            for j in (1, 2, 3):
-                swap(kind, j, dp ^ j).wait_recv()
+            arrive("swap", kind)
 
     def line_view(kind, index):
         if kind == 0:
@@ -295,25 +320,37 @@
             return line >= step, line - step
         return line <= lines - 1 - step, line + step
 
+    def when(go, act):
+        @pl.when(go)
+        def _():
+            act()
+
     def start_line(step, *kinds):
         if step < lines:
             for kind in kinds:
                 for way in (0, 1):
                     go, index = sends(way, step)
-
-                    @pl.when(go)
-                    def _():
-                        line_copy(kind, way, step, index).start()
+                    copy = line_copy(kind, way, step, index)
+                    when(go, copy.start)
+
+                def left(kind=kind):
+                    for way in (0, 1):
+                        go, index = sends(way, step)
+                        when(go, line_copy(kind, way, step, index).wait_send)
+
+                pending.append(left)
+
+                def wait(kind=kind):
+                    for way in (0, 1):
+                        go, index = takes(way, step)
+                        when(go, line_copy(kind, way, step, index).wait_recv)
+
+                expected["line", kind, step] = wait
 
     def wait_line(step, *kinds):
         if step < lines:
             for kind in kinds:
-                for way in (0, 1):
-                    go, index = takes(way, step)
-
-                    @pl.when(go)
-                    def _():
-                        line_copy(kind, way, step, index).wait_recv()
+                arrive("line", kind, step)
 
     def line_step(step, *kinds):
         wait_line(step, *kinds)
@@ -354,31 +391,42 @@
     ]
     near, beside = seat(dp ^ 2, mp), seat(dp, other)
 
+    far_seats = [part_seat(dp ^ 2, other, part) for part in (0, 1)]
+    twin_far = [part_seat(dp ^ 3, other, part) for part in (0, 1)]
+    arrivals = (near, beside, seat(dp ^ 1, mp), far_seats[0], seat(dp ^ 3, mp), far_seats[1])
+    arrivals += (seat(dp ^ 1, other),) + tuple(twin_far)
+
+    def send_rows(which, *numbers):
+        for number in numbers:
+            if number < 3:
+                copy = offer(which, number, (across, aside, twin)[number])
+            elif number in (3, 5):
+                part = number // 5
+                place = part_seat(dp, other, 1) if part else part_seat(dp ^ 2, mp, 0)
+                copy = relay(which, number, place, across if part else aside)
+            else:
+                place = {4: near, 6: beside, 7: far_seats[0], 8: far_seats[1]}[number]
+                copy = relay(which, number, place, twin)
+            begin(copy)
+            wait = relay(which, number, arrivals[number], twin).wait_recv
+            expected["rows", which, number] = wait
+
     def pass_on(which):
-        relay(which, 0, near, across).wait_recv()
-        begin(
-            relay(which, 3, part_seat(dp ^ 2, mp, 0), aside),
-            relay(which, 4, near, twin),
-        )
-        relay(which, 1, beside, aside).wait_recv()
-        begin(
-            relay(which, 5, part_seat(dp, other, 1), across),
-            relay(which, 6, beside, twin),
-        )
+        arrive("rows", which, 0)
+        send_rows(which, 3, 4)
+        arrive("rows", which, 1)
+        send_rows(which, 5, 6)
 
     def hand_over(which):
-        for part, peer in ((0, aside), (1, across)):
-            far = part_seat(dp ^ 2, other, part)
-            relay(which, 3 + 2 * part, far, peer).wait_recv()
-            begin(relay(which, 7 + part, far, twin))
+        arrive("rows", which, 3)
+        send_rows(which, 7)
+        arrive("rows", which, 5)
+        send_rows(which, 8)
 
     def all_rows(which):
         own_rows[which].wait()
-        relay(which, 2, seat(dp ^ 1, mp), twin).wait_recv()
-        relay(which, 4, seat(dp ^ 3, mp), twin).wait_recv()
-        relay(which, 6, seat(dp ^ 1, other), twin).wait_recv()
-        for part in (0, 1):
-            relay(which, 7 + part, part_seat(dp ^ 3, other, part), twin).wait_recv()
+        for number in (2, 4, 6, 7, 8):
+            arrive("rows", which, number)
 
     def dot(a, b, contract):
         return lax.dot_general(a, b, (contract, ((), ())), preferred_element_type=F32)
@@ -448,11 +496,10 @@
             grads_ref.at[kind, :, pl.ds(start, right_wide)],
         )
 
-    def attend(first, last):
-        def shifted(columns_):
-            return pl.BlockSpec((length, columns_), lambda i: (i + first, 0))
-
+    def attend(hooks):
         def body(step, rows_in, dys, weight, mixed, proj):
+            for number, hook in hooks.items():
+                when(step.index[0] == min(number, count // length - 1), hook)
             pre = dot(rows_in[...], weight[:, : 3 * wide], nn) + in_bias_v[...]
             douts = dot(dys[...], weight[:, 3 * wide :], nn).astype(BF16)
             value, backs = attention_block(
@@ -470,9 +517,9 @@
 
         pipeline(
             body,
-            (last - first,),
-            [shifted(width), shifted(width), fixed((width, 4 * wide))],
-            [shifted(wide), shifted(3 * wide)],
+            (count // length,),
+            [row_blocks(length, width), row_blocks(length, width), fixed((width, 4 * wide))],
+            [row_blocks(length, wide), row_blocks(length, 3 * wide)],
             normed_ref,
             dy_ref,
             heads_ref,
@@ -542,6 +589,10 @@
             half_ref.at[which], twin_ref.at[which], twin_send.at[which], twin_recv.at[which], twin
         )
 
+    def to_twin(which):
+        begin(twin_copy(which))
+        expected["twin", which] = twin_copy(which).wait_recv
+
     def owner_copy(which, number, peer, place):
         return remote(
             pair_ref.at[which, columns(place, rows), :],
@@ -560,6 +611,12 @@
             owner_copy(which, 1, aside, chip * 2 + other),
         )
 
+        def wait():
+            for number, peer in ((0, across), (1, aside), (2, (dp ^ 2, other))):
+                owner_copy(which, number, peer, 0).wait_recv()
+
+        expected["owner", which] = wait
+
     add_tile = min(256, chunk)
 
     def add_chunks(dst, *parts):
@@ -597,59 +654,77 @@
         )
 
     def sum_start(kind, step):
-        if step < lines:
+        if step >= lines:
+            return
+        for way in (0, 1):
+            go, index, first = sum_sends(way, step)
+            view = grads_ref.at[kind, columns(index, chunk), :]
+            staged = stage_ref.at[kind, way, step - 1]
+            when(go & first, sum_copy(kind, way, step, view).start)
+            if step > 1:
+
+                def pass_on_sum():
+                    add_chunks(staged, view, land_ref.at[kind, way, step - 2])
+                    sum_copy(kind, way, step, staged).start()
+
+                when(go & ~first, pass_on_sum)
+
+        def left():
             for way in (0, 1):
-                go, index, first = sum_sends(way, step)
-                view = grads_ref.at[kind, columns(index, chunk), :]
-
-                @pl.when(go & first)
-                def _():
-                    sum_copy(kind, way, step, view).start()
-
-                if step > 1:
-
-                    @pl.when(go & ~first)
-                    def _():
-                        staged = stage_ref.at[kind, way, step - 1]
-                        add_chunks(staged, view, land_ref.at[kind, way, step - 2])
-                        sum_copy(kind, way, step, staged).start()
+                staged = stage_ref.at[kind, way, step - 1]
+                when(sum_sends(way, step)[0], sum_copy(kind, way, step, staged).wait_send)
+
+        pending.append(left)
+
+        def wait():
+            for way in (0, 1):
+                staged = stage_ref.at[kind, way, step - 1]
+                when(sum_takes(way, step), sum_copy(kind, way, step, staged).wait_recv)
+
+        expected["sum", kind, step] = wait
 
     def sum_wait(kind, step):
         if step < lines:
-            for way in (0, 1):
-
-                @pl.when(sum_takes(way, step))
-                def _():
-                    sum_copy(kind, way, step, stage_ref.at[kind, way, step - 1]).wait_recv()
+            arrive("sum", kind, step)
 
     def sum_step(kind, step):
         sum_wait(kind, step)
         sum_start(kind, step + 1)
 
-    def final_copy(kind, j):
-        return remote(
-            total_ref.at[kind, columns(quarter ^ j, depth), :],
-            final_ref.at[kind, quarter],
-            final_send.at[kind, j - 1],
-            final_recv.at[kind, j - 1],
-            (dp ^ j, mp),
-        )
-
-    def final_in(kind, j):
-        return remote(
-            total_ref.at[kind, columns(quarter, depth), :],
-            final_ref.at[kind, quarter ^ j],
-            final_send.at[kind, j - 1],
-            final_recv.at[kind, j - 1],
-            (dp ^ j, mp),
-        )
+    def final_views(kind, of, by):
+        mine = columns(of, depth)
+        if kind == 1:
+            views = [
+                (
+                    total_ref.at[1, mine, pl.ds(k * wide, wide)],
+                    final_in_ref.at[k, :, columns(by, wide)],
+                )
+                for k in range(3)
+            ]
+            views.append(
+                (total_ref.at[1, mine, pl.ds(3 * wide, wide)], final_out_ref.at[:, columns(by, wide)])
+            )
+            return views
+        whole = final_down_ref if kind == 0 else final_up_ref
+        return [(total_ref.at[kind, mine, :], whole.at[:, columns(by, unit)])]
+
+    def final_copies(kind, of, by, j):
+        return [
+            remote(
+                src,
+                dst,
+                final_send.at[kind, number, j - 1],
+                final_recv.at[kind, number, j - 1],
+                (dp ^ j, mp),
+            )
+            for number, (src, dst) in enumerate(final_views(kind, of, by))
+        ]
 
     def final_own(kind):
-        return pltpu.make_async_copy(
-            total_ref.at[kind, columns(quarter, depth), :],
-            final_ref.at[kind, quarter],
-            local_sem.at[10 + kind],
-        )
+        return [
+            pltpu.make_async_copy(src, dst, local_sem.at[10 + 4 * kind + number])
+            for number, (src, dst) in enumerate(final_views(kind, quarter, quarter))
+        ]
 
     def sum_total(kind, step):
         for later in range(step, lines):
@@ -670,38 +745,147 @@
         def _():
             add_chunks(total_ref.at[kind], view, above)
 
-        begin(*[final_copy(kind, j) for j in (2, 3, 1)])
-        final_own(kind).start()
+        for j in (2, 3, 1):
+            begin(*final_copies(kind, quarter ^ j, quarter, j))
+        for copy in final_own(kind):
+            copy.start()
+
+        def wait():
+            for copy in final_own(kind):
+                copy.wait()
+            for j in (1, 2, 3):
+                for copy in final_copies(kind, quarter, quarter ^ j, j):
+                    copy.wait_recv()
+
+        expected["final", kind] = wait
+
+    own_tile = min(64, rows)
+
+    def own_pipeline(body, which, extra, out):
+        own_place = pl.ds(pl.multiple_of((chip * 2 + mp) * rows, rows), rows)
+        pipeline(
+            body,
+            (rows // own_tile,),
+            [row_blocks(own_tile, width)] * (4 + len(extra)),
+            [row_blocks(own_tile, width)],
+            pair_ref.at[which, own_place, :],
+            owner_ref.at[which, 0],
+            owner_ref.at[which, 1],
+            owner_ref.at[which, 2],
+            *extra,
+            out,
+        )
+
+    def add_four(parts):
+        return sum(ref[...].astype(F32) for ref in parts)
+
+    def finish_result():
+        def body(step, a, b, c, d, tok, out):
+            value = tok[...].astype(F32) + add_four((a, b, c, d)) + out_bias_v[...]
+            out[...] = value.astype(BF16)
+
+        own_pipeline(body, 0, [tok_ref], result_ref)
+
+    def finish_grad():
+        gain_sum[...] = jnp.zeros_like(gain_sum)
+        shift_sum[...] = jnp.zeros_like(shift_sum)
+        dy_sum[...] = jnp.zeros_like(dy_sum)
+
+        def body(step, a, b, c, d, tok, cot, out):
+            grad = add_four((a, b, c, d))
+            unit_rows, inv_spread = normalize(tok[...].astype(F32))
+            dy = cot[...].astype(F32)
+            along = grad * unit_rows
+            gain_sum[...] = gain_sum[...] + jnp.sum(along, axis=0, keepdims=True)
+            shift_sum[...] = shift_sum[...] + jnp.sum(grad, axis=0, keepdims=True)
+            dy_sum[...] = dy_sum[...] + jnp.sum(dy, axis=0, keepdims=True)
+            scaled = grad * gain_v[...]
+            centered = (
+                scaled
+                - jnp.mean(scaled, axis=-1, keepdims=True)
+                - unit_rows * jnp.mean(along * gain_v[...], axis=-1, keepdims=True)
+            )
+            out[...] = dy + inv_spread * centered
+
+        own_pipeline(body, 1, [tok_ref, cot_ref], grad_ref)
+
+    def small_move(number, src, dst, peer):
+        return remote(src, dst, small_send.at[number], small_recv.at[number], peer)
+
+    def sum_small():
+        vector[...] = jnp.zeros_like(vector)
+        for l in range(lines):
+            for q in range(QUARTERS):
+                d = l * QUARTERS + q
+                place = slice(d * each, (d + 1) * each)
+                for number, ref in enumerate((gain_sum, shift_sum, dy_sum)):
+                    vector[q, l, number : number + 1, :each] = ref[:, place]
+        for i in range(lines):
+            owner = quarter * lines + i
+            q, l = owner % QUARTERS, owner // QUARTERS
+            for k in range(3):
+                start = k * wide + i * in_each
+                vector[q, l, 3 + k : 4 + k, :in_each] = proj_sum_ref[:, start : start + in_each]
+            for r in range(up_each // up_low):
+                start = i * up_each + r * up_low
+                vector[q, l, 6 + r : 7 + r, :up_low] = pre_sum_ref[:, start : start + up_low]
+        first = [
+            small_move(j - 1, vector.at[quarter ^ j], vector_land.at[j - 1], (dp ^ j, mp))
+            for j in (1, 2, 3)
+        ]
+        for copy in first:
+            copy.start()
+        for copy in first:
+            copy.wait()
+        part[...] = (vector[quarter] + vector_land[0]) + (vector_land[1] + vector_land[2])
+        second = [
+            small_move(
+                2 + k, part.at[lax.rem(line + k, lines)], part_land.at[k - 1], in_line(k)
+            )
+            for k in range(1, lines)
+        ]
+        for copy in second:
+            copy.start()
+        total = part[line]
+        for k, copy in enumerate(second):
+            copy.wait()
+            total = total + part_land[k]
+        own_small_ref[...] = total
+        third = small_move(2 + lines, own_small_ref, aside_land, aside)
+        third.start()
+        third.wait()
+        row = lax.broadcasted_iota(jnp.int32, total.shape, 0)
+        own_small_ref[...] = jnp.where(row < 3, total + aside_land[...], total)
 
     begin_swap(0, 1)
-    begin(offer(0, 1, aside), offer(0, 2, twin))
+    send_rows(0, 1, 2)
     own_rows[0].start()
     own_rows[1].start()
     end_swap(0, 1)
     start_line(1, 0, 1)
-    begin(offer(0, 0, across), offer(1, 1, aside), offer(1, 2, twin))
+    begin_swap(2, 3, 4, 5)
+    send_rows(0, 0)
     line_step(1, 0, 1)
     pass_on(0)
-    begin_swap(2, 3, 4, 5)
-    begin(offer(1, 0, across))
-    hand_over(0)
-    line_step(2, 0, 1)
     end_swap(2, 3, 4, 5)
     start_line(1, 2)
+    hand_over(0)
+    send_rows(1, 1, 2)
+    send_rows(1, 0)
+    line_step(2, 0, 1)
+    begin_swap(6)
     all_rows(0)
     line_rest(3, 0)
     fetch = pltpu.make_async_copy(smalls_ref, small_v, local_sem.at[9])
     fetch.start()
     fetch.wait()
     small_f[...] = small_v[...].astype(F32)
-    each = width // (lines * QUARTERS)
     for d in range(lines * QUARTERS):
         place = slice(d * each, (d + 1) * each)
         gain_v[:, place] = small_f[d * tall : d * tall + 1, :each]
         shift_v[:, place] = small_f[d * tall + 1 : d * tall + 2, :each]
-    in_each = wide // lines
-    up_each = unit // lines
-    up_low = min(up_each, 128)
+        bias = small_f[d * tall + 2 : d * tall + 3, :each]
+        out_bias_v[:, place] = bias + small_f[d * tall + 3 : d * tall + 4, :each]
     for i in range(lines):
         top = pl.multiple_of((quarter * lines + i) * tall, tall)
         block = small_f[pl.ds(top, tall), :]
@@ -712,76 +896,56 @@
             start = i * up_each + r * up_low
             up_bias_v[:, start : start + up_low] = block[7 + r : 8 + r, :up_low]
     normalize_rows()
+    line_step(1, 2)
     pass_on(1)
     line_rest(3, 1)
     activate()
     hand_over(1)
-    begin_swap(6)
-    line_step(1, 2)
+    line_step(2, 2)
+    end_swap(6)
+    start_line(1, 3)
     all_rows(1)
     weight_grad(dy_ref, act_ref, unit, 0)
     sum_start(0, 1)
-    line_step(2, 2)
-    end_swap(6)
-    sum_step(0, 1)
     line_rest(3, 2)
-    start_line(1, 3)
-
-    groups = count // length
     proj_sum_ref[...] = jnp.zeros_like(proj_sum_ref)
-    attend(0, groups // 2)
+    attend({2: lambda: line_step(1, 3), 3: lambda: sum_step(0, 1)})
+    line_step(2, 3)
+    weight_grad(dy_ref, mixed_ref, wide, 1, 3 * wide)
+    weight_grad(normed_ref, proj_ref, 3 * wide, 1, 0)
     sum_step(0, 2)
-    attend(groups // 2, groups)
-    line_step(1, 3)
-    weight_grad(dy_ref, mixed_ref, wide, 1, 3 * wide)
-    line_step(2, 3)
-    weight_grad(normed_ref, proj_ref, 3 * wide, 1, 0)
+    line_rest(3, 3)
     sum_start(1, 1)
-    sum_total(0, 3)
-    sum_step(1, 1)
-    line_rest(3, 3)
+    forward_rows(1 - core, False)
+    to_twin(0)
     gate_back()
-    sum_step(1, 2)
     weight_grad(normed_ref, pre_ref, unit, 2)
     sum_start(2, 1)
-    forward_rows(1 - core, False)
-    begin(twin_copy(0))
-    sum_step(2, 1)
-    backward_rows(1 - core, False)
-    begin(twin_copy(1))
-    sum_total(1, 3)
-    twin_copy(0).wait_recv()
+    sum_total(0, 3)
+    arrive("twin", 0)
     forward_rows(core, True)
     to_owners(0)
-    sum_step(2, 2)
-    twin_copy(1).wait_recv()
+    sum_step(1, 1)
+    backward_rows(1 - core, False)
+    to_twin(1)
+    sum_step(2, 1)
+    arrive("twin", 1)
     backward_rows(core, True)
     to_owners(1)
+    sum_step(1, 2)
+    sum_step(2, 2)
+    sum_total(1, 3)
+    arrive("owner", 0)
+    finish_result()
+    arrive("owner", 1)
+    finish_grad()
     sum_total(2, 3)
-
-    for which in (0, 1):
-        for number, peer in ((0, across), (1, aside), (2, (dp ^ 2, other))):
-            owner_copy(which, number, peer, 0).wait_recv()
-    for kind in range(3):
-        final_own(kind).wait()
-        for j in (1, 2, 3):
-            final_in(kind, j).wait_recv()
-    for copy in pending:
-        copy.wait_send()
-    for step in range(1, lines):
-        for way in (0, 1):
-            go, index = sends(way, step)
-            sent, which, first = sum_sends(way, step)
-
-            @pl.when(go)
-            def _():
-                for kind in range(4):
-                    line_copy(kind, way, step, index).wait_send()
-
-            @pl.when(sent)
-            def _():
-                for kind in range(3):
-                    sum_copy(kind, way, step, stage_ref.at[kind, way, step - 1]).wait_send()
+    sum_small()
+
+    for key in list(expected):
+        arrive(*key)
+    for wait in pending:
+        wait()
 
 
 def run_layer(lines, team, tokens, cotangent, in_weight, out_weight, up_weight, down_weight, small, table):
@@ -817,30 +981,43 @@
         low(3, 2, steps, chunk, unit),
         low(3, 2, steps, chunk, unit),
         low(3, chunk, unit),
-        low(3, QUARTERS, depth, unit),
         low(2, count // 2, width),
         low(2, count // 2, width),
         low(2, count // 2, width),
         low(2, 3, rows, width),
+        low(rows, width),
+        jax.ShapeDtypeStruct((rows, width), F32),
+        low(depth, QUARTERS * unit),
+        low(depth, QUARTERS * unit),
+        low(3, depth, QUARTERS * wide),
+        low(depth, QUARTERS * wide),
     ]
-    sums = [
-        jax.ShapeDtypeStruct((1, 3 * wide), F32),
-        jax.ShapeDtypeStruct((1, unit), F32),
-    ]
+    tile = (8, 128)
     dma = pltpu.SemaphoreType.DMA
     results = pl.pallas_call(
         functools.partial(layer_kernel, lines),
-        out_shape=outs + sums,
+        out_shape=outs + [jax.ShapeDtypeStruct(tile, F32)],
         in_specs=[anywhere] * 7 + [inside],
-        out_specs=[anywhere] * len(outs) + [inside] * 2,
+        out_specs=[anywhere] * len(outs) + [inside],
         scratch_shapes=[
+            pltpu.VMEM((1, 3 * wide), F32),
+            pltpu.VMEM((1, unit), F32),
+            pltpu.VMEM((1, width), F32),
+            pltpu.VMEM((1, width), F32),
+            pltpu.VMEM((1, width), F32),
+            pltpu.VMEM((QUARTERS, lines) + tile, F32),
+            pltpu.VMEM((3, lines) + tile, F32),
+            pltpu.VMEM((lines,) + tile, F32),
+            pltpu.VMEM((steps,) + tile, F32),
+            pltpu.VMEM(tile, F32),
             pltpu.VMEM((smalls, 128), BF16),
             pltpu.VMEM((smalls, 128), F32),
             pltpu.VMEM((1, width), F32),
             pltpu.VMEM((1, width), F32),
+            pltpu.VMEM((1, width), F32),
             pltpu.VMEM((1, 3 * wide), F32),
             pltpu.VMEM((1, unit), F32),
-            dma((13,)),
+            dma((22,)),
             dma((7, 3)),
             dma((7, 3)),
             dma((2, 9)),
@@ -849,92 +1026,20 @@
             dma((4, 2, steps)),
             dma((3, 2, steps)),
             dma((3, 2, steps)),
-            dma((3, 3)),
-            dma((3, 3)),
+            dma((3, 4, 3)),
+            dma((3, 4, 3)),
             dma((2,)),
             dma((2,)),
             dma((2, 3)),
             dma((2, 3)),
+            dma((lines + 3,)),
+            dma((lines + 3,)),
         ],
         compiler_params=pltpu.CompilerParams(
             collective_id=1, has_side_effects=True, vmem_limit_bytes=VMEM_BYTES
         ),
     )(tokens, cotangent, in_weight, out_weight, up_weight, down_weight, small, table)
-    return results[5], results[16], results[19], results[20], results[21], results[22]
-
-
-def small_kernel(lines, both, vec_ref, total_ref, land_a, part, land_b, land_c, send, recv):
-    dp = lax.axis_index("dp")
-    mp = lax.axis_index("mp")
-    quarter = dp % QUARTERS
-    line = dp // QUARTERS
-    aside = (dp, 1 - mp)
-
-    def in_line(k):
-        return (lax.rem(line + k, lines) * QUARTERS + quarter, mp)
-
-    barrier = pltpu.get_barrier_semaphore()
-    peers = [(dp ^ j, mp) for j in (1, 2, 3)] + [in_line(k) for k in range(1, lines)] + [aside]
-    for peer in peers:
-        pl.semaphore_signal(barrier, inc=1, device_id=peer, device_id_type=MESH)
-    pl.semaphore_wait(barrier, len(peers))
-
-    def move(number, src, dst, peer):
-        return pltpu.make_async_remote_copy(
-            src_ref=src,
-            dst_ref=dst,
-            send_sem=send.at[number],
-            recv_sem=recv.at[number],
-            device_id=peer,
-            device_id_type=MESH,
-        )
-
-    first = [
-        move(j - 1, vec_ref.at[quarter ^ j], land_a.at[j - 1], (dp ^ j, mp)) for j in (1, 2, 3)
-    ]
-    for copy in first:
-        copy.start()
-    for copy in first:
-        copy.wait()
-    part[...] = (vec_ref[quarter] + land_a[0]) + (land_a[1] + land_a[2])
-    second = [
-        move(2 + k, part.at[lax.rem(line + k, lines)], land_b.at[k - 1], in_line(k))
-        for k in range(1, lines)
-    ]
-    for copy in second:
-        copy.start()
-    total = part[line]
-    for k, copy in enumerate(second):
-        copy.wait()
-        total = total + land_b[k]
-    total_ref[...] = total
-    third = move(2 + lines, total_ref, land_c, aside)
-    third.start()
-    third.wait()
-    shape = total_ref.shape
-    index = lax.broadcasted_iota(jnp.int32, shape, 0) * shape[1]
-    index = index + lax.broadcasted_iota(jnp.int32, shape, 1)
-    total_ref[...] = jnp.where(index < both, total + land_c[...], total)
-
-
-def sum_small(lines, both, vector):
-    tile = vector.shape[2:]
-    count = lines + 3
-    return pl.pallas_call(
-        functools.partial(small_kernel, lines, both),
-        out_shape=jax.ShapeDtypeStruct(tile, F32),
-        in_specs=[pl.BlockSpec(memory_space=pltpu.VMEM)],
-        out_specs=pl.BlockSpec(memory_space=pltpu.VMEM),
-        scratch_shapes=[
-            pltpu.VMEM((3, lines) + tile, F32),
-            pltpu.VMEM((lines,) + tile, F32),
-            pltpu.VMEM((max(lines - 1, 1),) + tile, F32),
-            pltpu.VMEM(tile, F32),
-            pltpu.SemaphoreType.DMA((count,)),
-            pltpu.SemaphoreType.DMA((count,)),
-        ],
-        compiler_params=pltpu.CompilerParams(collective_id=2, has_side_effects=True),
-    )(vector)
+    return results[20:]
 
 
 def smooth_gate(u):
@@ -963,12 +1068,7 @@
     n_dp = lax.axis_size("dp")
     n_mp = lax.axis_size("mp")
     lines = n_dp // QUARTERS
-    dp = lax.axis_index("dp")
-    mp = lax.axis_index("mp")
-    quarter = dp % QUARTERS
-    chip = (dp // 2) % (QUARTERS // 2)
     own_rows, width = tokens.shape
-    rows_here = in_weight.shape[1]
     each = norm_gain.shape[0]
     in_each = in_bias.shape[1]
     up_each = up_bias.shape[0]
@@ -984,66 +1084,22 @@
     )
     small = jnp.pad(small, ((0, SMALL - small.shape[0]), (0, 0)))
     table = rotary_tables(n_mp * own_rows, wide // HEAD)
-    smalls, final, pair, owner, grad_in_bias, grad_up_bias = run_layer(
+    outcome, grad_input, grad_down, grad_up, grad_in, grad_out, owned = run_layer(
         lines, QUARTERS * n_mp, tokens, cotangent, in_weight, out_weight, up_weight, down_weight, small, table
     )
-    smalls = smalls.reshape(n_dp, SMALL, 128)[:, :, :each].astype(F32)
-    full_gain = smalls[:, 0].reshape(-1)
-    full_out_bias = smalls[:, 2].reshape(-1)
-    full_down_bias = smalls[:, 3].reshape(-1)
-
-    def place(buffer, piece, index, axis):
-        return lax.dynamic_update_index_in_dim(buffer, piece, index, axis)
-
-    mine = lax.dynamic_slice_in_dim(pair, (chip * 2 + mp) * own_rows, own_rows, 1).astype(F32)
-    sums = mine + owner[:, 0].astype(F32) + owner[:, 1].astype(F32) + owner[:, 2].astype(F32)
-    summed, grad_own = sums[0], sums[1]
-    outcome = (tokens.astype(F32) + summed + full_out_bias + full_down_bias).astype(BF16)
-    final = final.astype(F32).transpose(0, 2, 1, 3)
-    own_grad_down = final[0]
-    own_grad_up = final[2]
-    own_heads = final[1].reshape(rows_here, QUARTERS, 4, wide).transpose(2, 0, 1, 3)
-    own_grad_in, own_grad_out = own_heads[:3], own_heads[3]
-    own_unit, own_inv = normalize(tokens.astype(F32))
-    gain_part = jnp.sum(grad_own * own_unit, axis=0)
-    shift_part = jnp.sum(grad_own, axis=0)
-    bias_part = jnp.sum(cotangent.astype(F32), axis=0)
-    scaled = grad_own * full_gain
-    centered_grad = (
-        scaled
-        - jnp.mean(scaled, axis=-1, keepdims=True)
-        - own_unit * jnp.mean(scaled * own_unit, axis=-1, keepdims=True)
-    )
-    grad_input = cotangent.astype(F32) + own_inv * centered_grad
-
-    wide = jnp.stack([gain_part, shift_part, bias_part])
-    wide = wide.reshape(3, lines, QUARTERS, each).transpose(2, 1, 0, 3)
-    wide = wide.reshape(QUARTERS, lines, 3 * each)
-    in_blocks = grad_in_bias.reshape(3, lines, in_each).transpose(1, 0, 2).reshape(lines, -1)
-    mine = jnp.concatenate([in_blocks, grad_up_bias.reshape(lines, up_each)], axis=1)
-    spread = place(jnp.zeros((QUARTERS,) + mine.shape, F32), mine, quarter, 0)
-    spread = spread.reshape(lines, QUARTERS, -1).transpose(1, 0, 2)
-    vector = jnp.concatenate([wide, spread], axis=2)
-    vector = jnp.pad(vector, ((0, 0), (0, 0), (0, 1024 - vector.shape[2])))
-    owned = sum_small(lines, 3 * each, vector.reshape(QUARTERS, lines, 8, 128)).reshape(-1)
-    own_gain = owned[:each]
-    own_shift = owned[each : 2 * each]
-    own_bias = owned[2 * each : 3 * each]
-    own_in_bias = owned[3 * each : 3 * each + 3 * in_each].reshape(3, in_each)
-    own_up_bias = owned[3 * each + 3 * in_each : 3 * each + 3 * in_each + up_each]
-
+    own_bias = owned[2, :each]
     return (
         outcome,
         grad_input,
-        own_gain,
-        own_shift,
-        own_grad_in.reshape(in_weight.shape),
-        own_in_bias,
-        own_grad_out.reshape(out_weight.shape),
+        owned[0, :each],
+        owned[1, :each],
+        grad_in.astype(F32),
+        owned[3:6, :in_each],
+        grad_out.astype(F32),
         own_bias,
-        own_grad_up.reshape(up_weight.shape),
-        own_up_bias,
-        own_grad_down.reshape(down_weight.shape),
+        grad_up.astype(F32),
+        owned[6:8, : min(up_each, 128)].reshape(-1)[:up_each],
+        grad_down.astype(F32),
         own_bias,
     )
 

time: 543 us -> 448 us (0.83); the launches traced: 532 us -> 446 us
  Pallas kernels: 490 us -> 427 us
  local copies, waits for them, and re-layouts: 28.4 us -> 9.62 us
    pallas_call x2 -> x1, Pallas kernels: 490 us -> 427 us  [run_layer(): pl.pallas_call(functools.partial(layer_kernel, lines), out_shape=outs + [...]
    slice x11 -> x1, local copies, waits for them, and re-layouts: 13.9 us -> 1.26 us  [per_device(): owned[3:6, :in_each]]
    convert_element_type x0 -> x4, other arithmetic: none -> 8.76 us  [the longest x1 2.91 us: per_device(): grad_up.astype(F32)]
    add x2 -> x0, other arithmetic: 7.37 us -> none  [the longest x1 4.19 us: per_device(): mine + owner[:, 0].astype(F32) + owner[:, 1].astype(F32)]
where the time goes in v4:
time: 448 us; the launch traced here: 446 us
  Pallas kernels  427 us (95%)
  local copies, waits for them, and re-layouts  9.62 us (2%)
  other arithmetic  8.76 us (2%)
    pallas_call x1, Pallas kernels, run_layer(): pl.pallas_call(functools.partial(layer_kernel, lines), out_shape=outs + [...  427 us

profile of v4, /device:TPU:0, one launch (start us, length us, event | category | flops | bytes accessed | tf_op | source)
XLA Modules:
  0.0 445.9 jit_solution(6369427913560386755)
XLA Ops:
  0.6 0.8 slice_bitcast_fusion.4
  1.5 1.5 concatenate.3
  3.0 0.6 pad.17.small_ref
  3.6 426.9 %shard_map.220 = (bf16[2048,2048]{1,0:T(8,128)(2,1)}, bf16[2048,2048]{1,0:T(8,128)(2,1)}, bf16[2048,1024]{1,0:T(8,128)(2,1)}, bf16[2048,1024]{1,0:T(8,128)(2,1)}...) custom-call(bf16[256,2048]{1,0:T(8,128)(2,1)} %tok_ref.1, ...), custom_call_target="tpu_custom_call" | custom-call | tf_op jit(solution)/shard_map/pallas_call | solution.py:997
  430.4 0.0 copy-start.1
  430.4 1.3 slice_bitcast_fusion
  431.8 1.3 slice_bitcast_fusion.1
  433.1 0.0 copy-start.3
  433.1 1.3 slice.29
  434.3 1.8 convert_element_type.19
  436.1 0.0 copy-start.2
  436.1 2.5 convert_element_type.18
  438.7 0.0 copy-start
  438.7 2.9 convert_element_type.20
  441.6 0.0 copy-done.1
  441.6 1.5 convert_element_type.21
  443.1 0.0 copy-done.3
  443.1 0.5 copy.28
  443.6 0.0 copy-done.2
  443.6 1.0 copy.29
  444.6 0.0 copy-done
  444.6 1.3 copy.30
  (2 shorter events, 0.0 us)
Async XLA Ops:
  430.4 11.2 %copy-start.1 = (bf16[128,4096]{1,0:T(8,128)(2,1)S(1)}, bf16[128,4096]{1,0:T(8,128)(2,1)}, u32[]{:S(2)}) copy-start(bf16[128,4096]{1,0:T(8,128)(2,1)} %get-tuple-element.25) | copy-start | bytes 3145732
  433.1 10.0 %copy-start.3 = (f32[128]{0:T(128)}, f32[128]{0:T(128)S(1)}, u32[]{:S(2)}) copy-start(f32[128]{0:T(128)S(1)} %get-tuple-element.77) | copy-start | bytes 1540
  436.1 7.5 %copy-start.2 = (bf16[256,2048]{1,0:T(8,128)(2,1)S(1)}, bf16[256,2048]{1,0:T(8,128)(2,1)}, u32[]{:S(2)}) copy-start(bf16[256,2048]{1,0:T(8,128)(2,1)} %get-tuple-element.70) | copy-start | bytes 3145732
  438.7 5.9 %copy-start = (f32[256,2048]{1,0:T(8,128)S(1)}, f32[256,2048]{1,0:T(8,128)}, u32[]{:S(2)}) copy-start(f32[256,2048]{1,0:T(8,128)} %get-tuple-element.71) | copy-start | bytes 6291460

commit v5 on v4

--- a/solution.py
+++ b/solution.py
@@ -233,10 +233,15 @@
     pending = []
     expected = {}
 
-    def begin(*copies):
-        for copy in copies:
+    def begin(make):
+        for copy in make():
             copy.start()
-            pending.append(copy.wait_send)
+
+        def left():
+            for copy in make():
+                copy.wait_send()
+
+        pending.append(left)
 
     def arrive(*key):
         expected.pop(key)()
@@ -281,7 +286,7 @@
 
     def begin_swap(*kinds):
         for kind in kinds:
-            begin(*[swap(kind, j, dp) for j in (2, 3, 1)])
+            begin(lambda kind=kind: [swap(kind, j, dp) for j in (2, 3, 1)])
             own[kind].start()
 
             def wait(kind=kind):
@@ -397,18 +402,22 @@
     arrivals += (seat(dp ^ 1, other),) + tuple(twin_far)
 
     def send_rows(which, *numbers):
-        for number in numbers:
+        def copy_of(number):
             if number < 3:
-                copy = offer(which, number, (across, aside, twin)[number])
-            elif number in (3, 5):
+                return offer(which, number, (across, aside, twin)[number])
+            if number in (3, 5):
                 part = number // 5
                 place = part_seat(dp, other, 1) if part else part_seat(dp ^ 2, mp, 0)
-                copy = relay(which, number, place, across if part else aside)
-            else:
-                place = {4: near, 6: beside, 7: far_seats[0], 8: far_seats[1]}[number]
-                copy = relay(which, number, place, twin)
-            begin(copy)
-            wait = relay(which, number, arrivals[number], twin).wait_recv
+                return relay(which, number, place, across if part else aside)
+            place = {4: near, 6: beside, 7: far_seats[0], 8: far_seats[1]}[number]
+            return relay(which, number, place, twin)
+
+        for number in numbers:
+            begin(lambda number=number: [copy_of(number)])
+
+            def wait(number=number):
+                relay(which, number, arrivals[number], twin).wait_recv()
+
             expected["rows", which, number] = wait
 
     def pass_on(which):
@@ -459,8 +468,9 @@
             normed_ref,
         )
 
-    def activate():
+    def activate(hooks):
         def body(step, rows_in, weight, act, slope):
+            call_hooks(step, hooks, count // tile)
             u = dot(rows_in[...], weight[...], nn) + up_bias_v[...]
             value, derivative = smooth_gate(u)
             act[...] = value.astype(BF16)
@@ -477,29 +487,35 @@
             slope_ref,
         )
 
-    tall_tile = min(512, width)
-
-    def weight_grad(left, right, right_wide, kind, start=0):
+    far_chunk = jnp.where(2 * line < lines, lines - 1, 0)
+
+    def weight_grad(part, left, right, right_wide, kind, start=0):
+        def place(i):
+            return lax.rem(far_chunk + i + (0 if part == "far" else 1), lines)
+
         def body(step, a, b, out):
             out[...] = dot(a[...], b[...], tn).astype(BF16)
 
         pipeline(
             body,
-            (width // tall_tile,),
+            (1 if part == "far" else lines - 1,),
             [
-                pl.BlockSpec((count, tall_tile), lambda i: (0, i)),
+                pl.BlockSpec((count, chunk), lambda i: (0, place(i))),
                 fixed((count, right_wide)),
             ],
-            [row_blocks(tall_tile, right_wide)],
+            [pl.BlockSpec((chunk, right_wide), lambda i: (place(i), 0))],
             left,
             right,
             grads_ref.at[kind, :, pl.ds(start, right_wide)],
         )
 
+    def call_hooks(step, hooks, last):
+        for number, hook in hooks.items():
+            when(step.index[0] == min(number, last - 1), hook)
+
     def attend(hooks):
         def body(step, rows_in, dys, weight, mixed, proj):
-            for number, hook in hooks.items():
-                when(step.index[0] == min(number, count // length - 1), hook)
+            call_hooks(step, hooks, count // length)
             pre = dot(rows_in[...], weight[:, : 3 * wide], nn) + in_bias_v[...]
             douts = dot(dys[...], weight[:, 3 * wide :], nn).astype(BF16)
             value, backs = attention_block(
@@ -527,8 +543,9 @@
             proj_ref,
         )
 
-    def gate_back():
+    def gate_back(hooks):
         def body(step, dys, weight, slope, pre):
+            call_hooks(step, hooks, count // tile)
             value = (dot(dys[...], weight[...], nn) * slope[...].astype(F32)).astype(BF16)
             pre[...] = value
             part = jnp.sum(value.astype(F32), axis=0, keepdims=True)
@@ -590,8 +607,8 @@
         )
 
     def to_twin(which):
-        begin(twin_copy(which))
-        expected["twin", which] = twin_copy(which).wait_recv
+        begin(lambda: [twin_copy(which)])
+        expected["twin", which] = lambda: twin_copy(which).wait_recv()
 
     def owner_copy(which, number, peer, place):
         return remote(
@@ -606,9 +623,11 @@
 
     def to_owners(which):
         begin(
-            owner_copy(which, 2, (dp ^ 2, other), (1 - chip) * 2 + other),
-            owner_copy(which, 0, across, (1 - chip) * 2 + mp),
-            owner_copy(which, 1, aside, chip * 2 + other),
+            lambda: [
+                owner_copy(which, 2, (dp ^ 2, other), (1 - chip) * 2 + other),
+                owner_copy(which, 0, across, (1 - chip) * 2 + mp),
+                owner_copy(which, 1, aside, chip * 2 + other),
+            ]
         )
 
         def wait():
@@ -745,8 +764,11 @@
         def _():
             add_chunks(total_ref.at[kind], view, above)
 
-        for j in (2, 3, 1):
-            begin(*final_copies(kind, quarter ^ j, quarter, j))
+        begin(
+            lambda: [
+                copy for j in (2, 3, 1) for copy in final_copies(kind, quarter ^ j, quarter, j)
+            ]
+        )
         for copy in final_own(kind):
             copy.start()
 
@@ -861,19 +883,20 @@
     send_rows(0, 1, 2)
     own_rows[0].start()
     own_rows[1].start()
+    proj_sum_ref[...] = jnp.zeros_like(proj_sum_ref)
     end_swap(0, 1)
     start_line(1, 0, 1)
+    send_rows(0, 0)
     begin_swap(2, 3, 4, 5)
-    send_rows(0, 0)
     line_step(1, 0, 1)
+    begin_swap(6)
     pass_on(0)
+    send_rows(1, 0)
     end_swap(2, 3, 4, 5)
     start_line(1, 2)
+    line_step(2, 0, 1)
     hand_over(0)
     send_rows(1, 1, 2)
-    send_rows(1, 0)
-    line_step(2, 0, 1)
-    begin_swap(6)
     all_rows(0)
     line_rest(3, 0)
     fetch = pltpu.make_async_copy(smalls_ref, small_v, local_sem.at[9])
@@ -896,30 +919,40 @@
             start = i * up_each + r * up_low
             up_bias_v[:, start : start + up_low] = block[7 + r : 8 + r, :up_low]
     normalize_rows()
-    line_step(1, 2)
-    pass_on(1)
     line_rest(3, 1)
-    activate()
-    hand_over(1)
+
+    def act_1():
+        pass_on(1)
+        line_step(1, 2)
+
+    activate({4: act_1})
     line_step(2, 2)
     end_swap(6)
     start_line(1, 3)
+    hand_over(1)
     all_rows(1)
-    weight_grad(dy_ref, act_ref, unit, 0)
+    weight_grad("far", dy_ref, act_ref, unit, 0)
     sum_start(0, 1)
+    weight_grad("rest", dy_ref, act_ref, unit, 0)
     line_rest(3, 2)
-    proj_sum_ref[...] = jnp.zeros_like(proj_sum_ref)
-    attend({2: lambda: line_step(1, 3), 3: lambda: sum_step(0, 1)})
+
+    def att_3():
+        line_step(1, 3)
+        sum_step(0, 1)
+
+    attend({3: att_3})
+    weight_grad("far", dy_ref, mixed_ref, wide, 1, 3 * wide)
     line_step(2, 3)
-    weight_grad(dy_ref, mixed_ref, wide, 1, 3 * wide)
-    weight_grad(normed_ref, proj_ref, 3 * wide, 1, 0)
+    weight_grad("far", normed_ref, proj_ref, 3 * wide, 1, 0)
+    sum_start(1, 1)
+    weight_grad("rest", normed_ref, proj_ref, 3 * wide, 1, 0)
+    weight_grad("rest", dy_ref, mixed_ref, wide, 1, 3 * wide)
     sum_step(0, 2)
     line_rest(3, 3)
-    sum_start(1, 1)
     forward_rows(1 - core, False)
     to_twin(0)
-    gate_back()
-    weight_grad(normed_ref, pre_ref, unit, 2)
+    gate_back({})
+    weight_grad("far", normed_ref, pre_ref, unit, 2)
     sum_start(2, 1)
     sum_total(0, 3)
     arrive("twin", 0)
@@ -928,6 +961,7 @@
     sum_step(1, 1)
     backward_rows(1 - core, False)
     to_twin(1)
+    weight_grad("rest", normed_ref, pre_ref, unit, 2)
     sum_step(2, 1)
     arrive("twin", 1)
     backward_rows(core, True)
@@ -935,11 +969,11 @@
     sum_step(1, 2)
     sum_step(2, 2)
     sum_total(1, 3)
-    arrive("owner", 0)
-    finish_result()
     arrive("owner", 1)
     finish_grad()
     sum_total(2, 3)
+    arrive("owner", 0)
+    finish_result()
     sum_small()
 
     for key in list(expected):

time: 448 us -> 445 us (level)
  no operation moved by 1% of the time
where the time goes in v5:
time: 445 us; the launch traced here: 443 us
  Pallas kernels  424 us (95%)
  local copies, waits for them, and re-layouts  9.62 us (2%)
  other arithmetic  8.76 us (2%)
    pallas_call x1, Pallas kernels, run_layer(): pl.pallas_call(functools.partial(layer_kernel, lines), out_shape=outs + [...  424 us

profile of v5, /device:TPU:0, one launch (start us, length us, event | category | flops | bytes accessed | tf_op | source)
XLA Modules:
  0.0 442.6 jit_solution(3970255449335188495)
XLA Ops:
  0.6 0.8 slice_bitcast_fusion.4
  1.5 1.5 concatenate.3
  3.0 0.6 pad.17.small_ref
  3.6 423.5 %shard_map.220 = (bf16[2048,2048]{1,0:T(8,128)(2,1)}, bf16[2048,2048]{1,0:T(8,128)(2,1)}, bf16[2048,1024]{1,0:T(8,128)(2,1)}, bf16[2048,1024]{1,0:T(8,128)(2,1)}...) custom-call(bf16[256,2048]{1,0:T(8,128)(2,1)} %tok_ref.1, ...), custom_call_target="tpu_custom_call" | custom-call | tf_op jit(solution)/shard_map/pallas_call | solution.py:1031
  427.1 0.0 copy-start.1
  427.1 1.3 slice_bitcast_fusion
  428.4 1.3 slice_bitcast_fusion.1
  429.7 0.0 copy-start.3
  429.7 1.3 slice.29
  431.0 1.8 convert_element_type.19
  432.8 0.0 copy-start.2
  432.8 2.5 convert_element_type.18
  435.3 0.0 copy-start
  435.3 2.9 convert_element_type.20
  438.2 0.0 copy-done.1
  438.2 1.5 convert_element_type.21
  439.8 0.0 copy-done.3
  439.8 0.5 copy.28
  440.3 0.0 copy-done.2
  440.3 1.0 copy.29
  441.3 0.0 copy-done
  441.3 1.3 copy.30
  (2 shorter events, 0.0 us)
Async XLA Ops:
  427.1 11.2 %copy-start.1 = (bf16[128,4096]{1,0:T(8,128)(2,1)S(1)}, bf16[128,4096]{1,0:T(8,128)(2,1)}, u32[]{:S(2)}) copy-start(bf16[128,4096]{1,0:T(8,128)(2,1)} %get-tuple-element.25) | copy-start | bytes 3145732
  429.7 10.0 %copy-start.3 = (f32[128]{0:T(128)}, f32[128]{0:T(128)S(1)}, u32[]{:S(2)}) copy-start(f32[128]{0:T(128)S(1)} %get-tuple-element.77) | copy-start | bytes 1540
  432.8 7.5 %copy-start.2 = (bf16[256,2048]{1,0:T(8,128)(2,1)S(1)}, bf16[256,2048]{1,0:T(8,128)(2,1)}, u32[]{:S(2)}) copy-start(bf16[256,2048]{1,0:T(8,128)(2,1)} %get-tuple-element.70) | copy-start | bytes 3145732
  435.3 5.9 %copy-start = (f32[256,2048]{1,0:T(8,128)S(1)}, f32[256,2048]{1,0:T(8,128)}, u32[]{:S(2)}) copy-start(f32[256,2048]{1,0:T(8,128)} %get-tuple-element.71) | copy-start | bytes 6291460
